TPU v7x, 32 devices: a whole 2x2x4 slice. The times are simulated.
32 devices in a mesh: inner: 4 (over y, x), outer: 2 (over core), head: 4 (over z).
Axes of the slice: x: 2, y: 2, z: 4, core: 2. Of those that a mesh axis runs over, the one named last changes fastest.
Arguments:
- queries: bfloat16 [1024, 24, 128], P(('outer', 'inner'), 'head'), may hold values from -6 to 6
- key_rows: bfloat16 [1024, 4, 128], P(('outer', 'inner'), 'head'), may hold values from -6 to 6
- value_rows: bfloat16 [1024, 4, 128], P(('outer', 'inner'), 'head'), may hold values from -6 to 6
- attn_out: bfloat16 [1024, 24, 128], P(('outer', 'inner'), 'head'), may hold values from -3 to 3
- grad_out: bfloat16 [1024, 24, 128], P(('outer', 'inner'), 'head'), may hold values from -96 to 96
- log_norms: float32 [24, 1024], P('head', ('outer', 'inner'))
- pair_order: int32 [4], replicated, may hold values from 0 to 3, each once
Outputs:
- grad_queries: bfloat16 [1024, 24, 128], P(('outer', 'inner'), 'head')
- grad_keys: bfloat16 [1024, 4, 128], P(('outer', 'inner'), 'head')
- grad_values: bfloat16 [1024, 4, 128], P(('outer', 'inner'), 'head')
Inputs may be any that keep to these rules, and one draw needn't show every extreme that they name: Index i of inner holds, in every segment, span pair_order[i] in its first 64 rows and span 8 - 1 - pair_order[i] in its last 64 rows.
All inputs are finite; a program needn't handle non-finite values.
Results may differ from a plain program's by a relative error of at most 0.0053.
Values may be sent and summed in bfloat16 or wider, within the bound.
No kernel may reach another device: no remote copies, remote signals or barrier semaphores. Data moves between devices by JAX's collectives and lax.ppermute only.
A program may use at most 64 MiB of HBM per device.

v0:
```python
import math

import jax
import jax.numpy as jnp
from jax import lax
from jax.sharding import PartitionSpec as P


def from_behind(block, axis, distance):
    devices = range(lax.axis_size(axis))
    route = [((i - distance) % len(devices), i) for i in devices]
    return lax.ppermute(block, axis, route)


def passed_along(value, axis, steps):
    count = lax.axis_size(axis)
    initial, last = (max(0, -steps), min(count, count - steps))
    return lax.ppermute(value, axis, [(source, source + steps) for source in range(initial, last)])


def segment_positions(pair_order, within, span_rows):
    slot_index = within // (2 * span_rows)
    local_rows = within % (2 * span_rows)
    rank_value = jnp.take(pair_order, slot_index)
    span_count = 2 * pair_order.shape[0]
    first_half = rank_value * span_rows + local_rows
    second_half = (span_count - 1 - rank_value) * span_rows + local_rows - span_rows
    return jnp.where(local_rows < span_rows, first_half, second_half)


def block_grads(
    queries_five, grad_five, norms_four, dots_four, key_blocks, value_blocks, visible, inv_root
):
    scores = (
        jnp.einsum(
            "arhgd,bkhd->ahgrbk", queries_five, key_blocks, preferred_element_type=jnp.float32
        )
        * inv_root
    )
    attn_weights = jnp.where(
        visible[:, None, None], jnp.exp(scores - norms_four[..., None, None]), 0.0
    )
    weights_half = attn_weights.astype(jnp.bfloat16)
    grad_weights = jnp.einsum(
        "arhgd,bkhd->ahgrbk", grad_five, value_blocks, preferred_element_type=jnp.float32
    )
    grad_scores = (attn_weights * (grad_weights - dots_four[..., None, None])).astype(jnp.bfloat16)
    value_grad = jnp.einsum(
        "ahgrbk,arhgd->bkhd", weights_half, grad_five, preferred_element_type=jnp.float32
    )
    key_grad = (
        jnp.einsum(
            "ahgrbk,arhgd->bkhd", grad_scores, queries_five, preferred_element_type=jnp.float32
        )
        * inv_root
    )
    query_grad = (
        jnp.einsum(
            "ahgrbk,bkhd->arhgd", grad_scores, key_blocks, preferred_element_type=jnp.float32
        )
        * inv_root
    )
    return (query_grad, key_grad, value_grad)


def inner_lap(blocks, moving, resident, update):
    cycle_size = lax.axis_size("inner")
    my_index = lax.axis_index("inner")

    def one_turn(turn_index, state_tuple):
        blocks, moving, resident = state_tuple
        moving, resident = update(blocks, moving, resident, (my_index - turn_index) % cycle_size)
        blocks = from_behind(blocks, "inner", 1)
        moving = from_behind(moving, "inner", 1)
        return (blocks, moving, resident)

    blocks, moving, resident = lax.fori_loop(
        0, cycle_size - 1, one_turn, (blocks, moving, resident)
    )
    moving, resident = update(blocks, moving, resident, (my_index + 1) % cycle_size)
    moving = from_behind(moving, "inner", 1)
    return (moving, resident)


def on_device(queries, key_rows, value_rows, attn_out, grad_out, log_norms, pair_order):
    row_count, q_local, head_size = queries.shape
    kv_local = key_rows.shape[1]
    group_size = q_local // kv_local
    span_rows = row_count // 2
    inv_root = 1.0 / math.sqrt(head_size)
    my_index = lax.axis_index("inner")
    outer_index = lax.axis_index("outer")
    local_rows = jnp.arange(row_count, dtype=jnp.int32)

    def positions_of(slot_index):
        return segment_positions(pair_order, slot_index * row_count + local_rows, span_rows)

    my_positions = positions_of(my_index)
    row_dot = jnp.sum(grad_out.astype(jnp.float32) * attn_out.astype(jnp.float32), axis=-1).T
    own_pairs = jnp.stack([key_rows, value_rows])
    prev_pairs = passed_along(own_pairs, "outer", 1)
    has_prev = outer_index > 0
    query_five = queries.reshape(row_count, kv_local, group_size, head_size)[None]
    grad_five = grad_out.reshape(row_count, kv_local, group_size, head_size)[None]
    norms_four = log_norms.reshape(kv_local, group_size, row_count)[None]
    dots_four = row_dot.reshape(kv_local, group_size, row_count)[None]
    blocks = jnp.stack([own_pairs, prev_pairs])

    def update(blocks, moving, resident, source):
        key_positions = positions_of(source)
        causal = key_positions[None, :] <= my_positions[:, None]
        visible = jnp.stack([causal, jnp.broadcast_to(has_prev, causal.shape)], axis=1)[None]
        query_grad, key_grad, value_grad = block_grads(
            query_five,
            grad_five,
            norms_four,
            dots_four,
            blocks[:, 0],
            blocks[:, 1],
            visible,
            inv_root,
        )
        return (moving + jnp.stack([key_grad, value_grad], axis=1), resident + query_grad)

    moving = jnp.zeros(blocks.shape, jnp.float32)
    resident = jnp.zeros(query_five.shape, jnp.float32)
    moving, resident = inner_lap(blocks, moving, resident, update)
    returned = passed_along(moving[1], "outer", -1)
    pair_grads = moving[0] + returned
    query_total = resident[0]
    grad_queries = query_total.reshape(row_count, q_local, head_size).astype(jnp.bfloat16)
    return (grad_queries, pair_grads[0].astype(jnp.bfloat16), pair_grads[1].astype(jnp.bfloat16))


def solution(mesh):
    in_specs = (
        P(("outer", "inner"), "head", None),
        P(("outer", "inner"), "head", None),
        P(("outer", "inner"), "head", None),
        P(("outer", "inner"), "head", None),
        P(("outer", "inner"), "head", None),
        P("head", ("outer", "inner")),
        P(),
    )
    out_specs = (
        P(("outer", "inner"), "head", None),
        P(("outer", "inner"), "head", None),
        P(("outer", "inner"), "head", None),
    )
    return jax.shard_map(
        on_device, mesh=mesh, in_specs=in_specs, out_specs=out_specs, check_vma=False
    )
```

profile of v0, /device:TPU:0, one launch (start us, length us, event | category | flops | bytes accessed | tf_op | source)
XLA Modules:
  0.0 70.6 jit_solution(4458715017288728873)
XLA Ops:
  0.6 0.8 %fusion.57 = (bf16[1,2,128,1,128]{4,2,0,3,1:T(8,128)(2,1)S(1)}, bf16[2,128,1,128]{3,1,0,2:T(8,128)(2,1)S(1)}) fusion(bf16[1,128,1,128]{3,1,0,2:T(8,128)(2,1)} %bitcast.300, bf16[1,128,1,128]{3,1,0,2:T(8,128)(2,1)} %bitcast.301), kind=kLoop, calls=%fused_computation.111 | loop fusion | flops 32768 | bytes 196608 | tf_op jit(solution)/shard_map/stack | solution.py:107
  1.5 2.4 %collective-permute-start.2 = (bf16[2,128,1,128]{3,1,0,2:T(8,128)(2,1)S(1)}, bf16[2,128,1,128]{3,1,0,2:T(8,128)(2,1)S(1)}, u32[]{:S(2)}, u32[]{:S(2)}) collective-permute-start(bf16[2,128,1,128]{3,1,0,2:T(8,128)(2,1)S(1)} %get-tuple-element.439), channel_id=1, source_target_pairs={{0,4},{1,5},{2,6},{3,7},{8,12},{9,13},{10,14},{11,15},{16,20},{17,... | collective-permute-start | bytes 196616 | tf_op jit(solution)/shard_map/ppermute | solution.py:18
  3.9 0.6 copy-done.2
  4.5 0.7 fusion.59
  5.2 2.6 %compare_select_fusion.17 = s32[128]{0:T(128)S(1)} fusion(s32[]{:T(128)} %bitcast.8, s32[]{:T(128)} %bitcast.7, s32[]{:T(128)} %bitcast.6, s32[]{:T(128)} %bitcast.5, s32[]{:T(128)S(6)} %mul.155), kind=kLoop, calls=%fused_computation.103 | loop fusion | flops 5248 | bytes 532 | tf_op jit(solution)/shard_map/jit(_where)/select_n | solution.py:28
  7.7 2.6 %compare_select_fusion.16 = s32[128]{0:T(128)S(1)} fusion(s32[]{:T(128)} %bitcast.8, s32[]{:T(128)} %bitcast.7, s32[]{:T(128)} %bitcast.6, s32[]{:T(128)} %bitcast.5, s32[]{:T(128)S(6)} %mul.159), kind=kLoop, calls=%fused_computation.100 | loop fusion | flops 5248 | bytes 532 | tf_op jit(solution)/shard_map/jit(_where)/select_n | solution.py:28
  10.4 1.1 %multiply_reduce_fusion = f32[128,6]{0,1:T(8,128)S(1)} fusion(bf16[128,6,128]{2,0,1:T(8,128)(2,1)} %param.14, bf16[128,6,128]{2,0,1:T(8,128)(2,1)S(1)} %copy-done), kind=kLoop, calls=%fused_computation.68 | loop fusion | flops 392448 | bytes 396288 | tf_op jit(solution)/shard_map/reduce_sum | solution.py:99
  11.6 0.9 %copy-done.1 = bf16[128,6,128]{2,0,1:T(8,128)(2,1)S(1)} copy-done((bf16[128,6,128]{2,0,1:T(8,128)(2,1)S(1)}, bf16[128,6,128]{2,0,1:T(8,128)(2,1)}, u32[]{:S(2)}) %copy-start.1) | copy-done | bytes 196632
  12.5 45.7 %while.21 = (s32[]{:T(128)}, bf16[2,2,128,1,128]{4,2,0,3,1:T(8,128)(2,1)S(1)}, f32[2,2,128,1,128]{4,2,0,3,1:T(8,128)S(1)}, f32[1,128,1,6,128]{4,1,3,0,2:T(8,128)...) while((s32[]{:T(128)}, ...), condition=%wide.region_2.4_spmd.clone, body=%wide.region_1.3_spmd.clone.sunk | while | flops 253514896 | bytes 8300465 | solution.py:77
  12.5 0.7 fusion.89
  13.2 2.5 %compare_select_fusion.25 = s32[128]{0:T(128)S(1)} fusion(s32[]{:T(128)} %bitcast.288, s32[]{:T(128)} %bitcast.289, s32[]{:T(128)} %bitcast.290, s32[]{:T(128)} %bitcast.291, s32[]{:T(128)S(6)} %mul.256), kind=kLoop, calls=%fused_computation.39.clone.1 | loop fusion | flops 5248 | bytes 532 | tf_op jit(solution)/shard_map/while/body/eval_jaxpr/jit(_where)/select_n | solution.py:28
  16.9 2.4 %collective-permute-start.1 = (f32[2,2,128,1,128]{4,2,0,3,1:T(8,128)S(1)}, f32[2,2,128,1,128]{4,2,0,3,1:T(8,128)S(1)}, u32[]{:S(2)}, u32[]{:S(2)}) collective-permute-start(f32[2,2,128,1,128]{4,2,0,3,1:T(8,128)S(1)} %maximum_add_fusion.3), channel_id=1, source_target_pairs={{24,0},{0,8},{8,16},{16,24},{25,1},{1,9},{9,17},{17,25},{26,2},{2,... | collective-permute-start | bytes 786440 | tf_op jit(solution)/shard_map/while/body/eval_jaxpr/ppermute | solution.py:12
  19.3 1.5 %collective-permute-start = (bf16[2,2,128,1,128]{4,2,0,3,1:T(8,128)(2,1)S(1)}, bf16[2,2,128,1,128]{4,2,0,3,1:T(8,128)(2,1)S(1)}, u32[]{:S(2)}, u32[]{:S(2)}) collective-permute-start(bf16[2,2,128,1,128]{4,2,0,3,1:T(8,128)(2,1)S(1)} %copy.37), channel_id=1, source_target_pairs={{24,0},{0,8},{8,16},{16,24},{25,1},{1,9},{9,17},{17,25},{26,2},{2,... | collective-permute-start | bytes 393224 | tf_op jit(solution)/shard_map/while/body/eval_jaxpr/ppermute | solution.py:12
  20.8 0.4 fusion.93
  21.2 7.7 %collective-permute-done = bf16[2,2,128,1,128]{4,2,0,3,1:T(8,128)(2,1)S(1)} collective-permute-done((bf16[2,2,128,1,128]{4,2,0,3,1:T(8,128)(2,1)S(1)}, bf16[2,2,128,1,128]{4,2,0,3,1:T(8,128)(2,1)S(1)}, u32[]{:S(2)}, u32[]{:S(2)}) %collective-permute-start) | collective-permute-done | bytes 131104 | tf_op jit(solution)/shard_map/while/body/eval_jaxpr/ppermute | solution.py:12
  28.9 0.7 fusion.89
  29.6 2.5 %compare_select_fusion.25 = s32[128]{0:T(128)S(1)} fusion(s32[]{:T(128)} %bitcast.288, s32[]{:T(128)} %bitcast.289, s32[]{:T(128)} %bitcast.290, s32[]{:T(128)} %bitcast.291, s32[]{:T(128)S(6)} %mul.256), kind=kLoop, calls=%fused_computation.39.clone.1 | loop fusion | flops 5248 | bytes 532 | tf_op jit(solution)/shard_map/while/body/eval_jaxpr/jit(_where)/select_n | solution.py:28
  33.3 0.8 %collective-permute-start.1 = (f32[2,2,128,1,128]{4,2,0,3,1:T(8,128)S(1)}, f32[2,2,128,1,128]{4,2,0,3,1:T(8,128)S(1)}, u32[]{:S(2)}, u32[]{:S(2)}) collective-permute-start(f32[2,2,128,1,128]{4,2,0,3,1:T(8,128)S(1)} %maximum_add_fusion.3), channel_id=1, source_target_pairs={{24,0},{0,8},{8,16},{16,24},{25,1},{1,9},{9,17},{17,25},{26,2},{2,... | collective-permute-start | bytes 786440 | tf_op jit(solution)/shard_map/while/body/eval_jaxpr/ppermute | solution.py:12
  34.1 2.4 %collective-permute-start = (bf16[2,2,128,1,128]{4,2,0,3,1:T(8,128)(2,1)S(1)}, bf16[2,2,128,1,128]{4,2,0,3,1:T(8,128)(2,1)S(1)}, u32[]{:S(2)}, u32[]{:S(2)}) collective-permute-start(bf16[2,2,128,1,128]{4,2,0,3,1:T(8,128)(2,1)S(1)} %copy.37), channel_id=1, source_target_pairs={{24,0},{0,8},{8,16},{16,24},{25,1},{1,9},{9,17},{17,25},{26,2},{2,... | collective-permute-start | bytes 393224 | tf_op jit(solution)/shard_map/while/body/eval_jaxpr/ppermute | solution.py:12
  36.5 0.4 fusion.93
  36.9 7.1 %collective-permute-done = bf16[2,2,128,1,128]{4,2,0,3,1:T(8,128)(2,1)S(1)} collective-permute-done((bf16[2,2,128,1,128]{4,2,0,3,1:T(8,128)(2,1)S(1)}, bf16[2,2,128,1,128]{4,2,0,3,1:T(8,128)(2,1)S(1)}, u32[]{:S(2)}, u32[]{:S(2)}) %collective-permute-start) | collective-permute-done | bytes 131104 | tf_op jit(solution)/shard_map/while/body/eval_jaxpr/ppermute | solution.py:12
  44.0 0.7 fusion.89
  44.7 2.5 %compare_select_fusion.25 = s32[128]{0:T(128)S(1)} fusion(s32[]{:T(128)} %bitcast.288, s32[]{:T(128)} %bitcast.289, s32[]{:T(128)} %bitcast.290, s32[]{:T(128)} %bitcast.291, s32[]{:T(128)S(6)} %mul.256), kind=kLoop, calls=%fused_computation.39.clone.1 | loop fusion | flops 5248 | bytes 532 | tf_op jit(solution)/shard_map/while/body/eval_jaxpr/jit(_where)/select_n | solution.py:28
  48.5 2.8 %collective-permute-start = (bf16[2,2,128,1,128]{4,2,0,3,1:T(8,128)(2,1)S(1)}, bf16[2,2,128,1,128]{4,2,0,3,1:T(8,128)(2,1)S(1)}, u32[]{:S(2)}, u32[]{:S(2)}) collective-permute-start(bf16[2,2,128,1,128]{4,2,0,3,1:T(8,128)(2,1)S(1)} %copy.37), channel_id=1, source_target_pairs={{24,0},{0,8},{8,16},{16,24},{25,1},{1,9},{9,17},{17,25},{26,2},{2,... | collective-permute-start | bytes 393224 | tf_op jit(solution)/shard_map/while/body/eval_jaxpr/ppermute | solution.py:12
  51.3 0.4 fusion.93
  51.7 6.5 %collective-permute-done = bf16[2,2,128,1,128]{4,2,0,3,1:T(8,128)(2,1)S(1)} collective-permute-done((bf16[2,2,128,1,128]{4,2,0,3,1:T(8,128)(2,1)S(1)}, bf16[2,2,128,1,128]{4,2,0,3,1:T(8,128)(2,1)S(1)}, u32[]{:S(2)}, u32[]{:S(2)}) %collective-permute-start) | collective-permute-done | bytes 131104 | tf_op jit(solution)/shard_map/while/body/eval_jaxpr/ppermute | solution.py:12
  58.2 0.3 fusion.33
  59.6 7.1 %collective-permute-done.3 = f32[2,2,128,1,128]{4,2,0,3,1:T(8,128)S(1)} collective-permute-done((f32[2,2,128,1,128]{4,2,0,3,1:T(8,128)S(1)}, f32[2,2,128,1,128]{4,2,0,3,1:T(8,128)S(1)}, u32[]{:S(2)}, u32[]{:S(2)}) %collective-permute-start.3) | collective-permute-done | bytes 262176 | tf_op jit(solution)/shard_map/ppermute | solution.py:12
  66.7 1.3 %collective-permute-start.4 = (f32[2,128,1,128]{3,1,0,2:T(8,128)S(1)}, f32[2,128,1,128]{3,1,0,2:T(8,128)S(1)}, u32[]{:S(2)}, u32[]{:S(2)}) collective-permute-start(f32[2,128,1,128]{3,1,0,2:T(8,128)S(1)} %slice_bitcast_fusion), channel_id=1, source_target_pairs={{4,0},{5,1},{6,2},{7,3},{12,8},{13,9},{14,10},{15,11},{20,16},{21,... | collective-permute-start | bytes 393224 | tf_op jit(solution)/shard_map/ppermute | solution.py:18
  68.2 0.8 %copy.16 = bf16[128,6,128]{2,0,1:T(8,128)(2,1)} copy(bf16[128,6,128]{0,2,1:T(8,128)(2,1)S(1)} %fusion.40) | data formatting | bytes 393216
  69.1 0.9 %collective-permute-done.4 = f32[2,128,1,128]{3,1,0,2:T(8,128)S(1)} collective-permute-done((f32[2,128,1,128]{3,1,0,2:T(8,128)S(1)}, f32[2,128,1,128]{3,1,0,2:T(8,128)S(1)}, u32[]{:S(2)}, u32[]{:S(2)}) %collective-permute-start.4) | collective-permute-done | bytes 131104 | tf_op jit(solution)/shard_map/ppermute | solution.py:18
  70.0 0.6 slice_bitcast_fusion.2
  (49 shorter events, 5.1 us)
Async XLA Ops:
  0.6 9.8 %copy-start = (bf16[128,6,128]{2,0,1:T(8,128)(2,1)S(1)}, bf16[128,6,128]{2,0,1:T(8,128)(2,1)}, u32[]{:S(2)}) copy-start(bf16[128,6,128]{2,0,1:T(8,128)(2,1)} %param.15) | copy-start | bytes 589828
  1.5 10.1 %collective-permute-start.2 = (bf16[2,128,1,128]{3,1,0,2:T(8,128)(2,1)S(1)}, bf16[2,128,1,128]{3,1,0,2:T(8,128)(2,1)S(1)}, u32[]{:S(2)}, u32[]{:S(2)}) collective-permute-start(bf16[2,128,1,128]{3,1,0,2:T(8,128)(2,1)S(1)} %get-tuple-element.439), channel_id=1, source_target_pairs={{0,4},{1,5},{2,6},{3,7},{8,12},{9,13},{10,14},{11,15},{16,20},{17,... | collective-permute-start | bytes 196616 | tf_op jit(solution)/shard_map/ppermute | solution.py:18
  3.8 0.7 copy-start.2
  11.6 0.9 %copy-start.1 = (bf16[128,6,128]{2,0,1:T(8,128)(2,1)S(1)}, bf16[128,6,128]{2,0,1:T(8,128)(2,1)}, u32[]{:S(2)}) copy-start(bf16[128,6,128]{2,0,1:T(8,128)(2,1)} %param.11) | copy-start | bytes 589828
  11.6 0.9 %copy-start.3 = (f32[6,128]{1,0:T(8,128)S(1)}, f32[6,128]{1,0:T(8,128)}, u32[]{:S(2)}) copy-start(f32[6,128]{1,0:T(8,128)} %param.16) | copy-start | bytes 9220
  16.9 12.0 %collective-permute-start.1 = (f32[2,2,128,1,128]{4,2,0,3,1:T(8,128)S(1)}, f32[2,2,128,1,128]{4,2,0,3,1:T(8,128)S(1)}, u32[]{:S(2)}, u32[]{:S(2)}) collective-permute-start(f32[2,2,128,1,128]{4,2,0,3,1:T(8,128)S(1)} %maximum_add_fusion.3), channel_id=1, source_target_pairs={{24,0},{0,8},{8,16},{16,24},{25,1},{1,9},{9,17},{17,25},{26,2},{2,... | collective-permute-start | bytes 786440 | tf_op jit(solution)/shard_map/while/body/eval_jaxpr/ppermute | solution.py:12
  19.3 9.6 %collective-permute-start = (bf16[2,2,128,1,128]{4,2,0,3,1:T(8,128)(2,1)S(1)}, bf16[2,2,128,1,128]{4,2,0,3,1:T(8,128)(2,1)S(1)}, u32[]{:S(2)}, u32[]{:S(2)}) collective-permute-start(bf16[2,2,128,1,128]{4,2,0,3,1:T(8,128)(2,1)S(1)} %copy.37), channel_id=1, source_target_pairs={{24,0},{0,8},{8,16},{16,24},{25,1},{1,9},{9,17},{17,25},{26,2},{2,... | collective-permute-start | bytes 393224 | tf_op jit(solution)/shard_map/while/body/eval_jaxpr/ppermute | solution.py:12
  33.3 10.7 %collective-permute-start.1 = (f32[2,2,128,1,128]{4,2,0,3,1:T(8,128)S(1)}, f32[2,2,128,1,128]{4,2,0,3,1:T(8,128)S(1)}, u32[]{:S(2)}, u32[]{:S(2)}) collective-permute-start(f32[2,2,128,1,128]{4,2,0,3,1:T(8,128)S(1)} %maximum_add_fusion.3), channel_id=1, source_target_pairs={{24,0},{0,8},{8,16},{16,24},{25,1},{1,9},{9,17},{17,25},{26,2},{2,... | collective-permute-start | bytes 786440 | tf_op jit(solution)/shard_map/while/body/eval_jaxpr/ppermute | solution.py:12
  34.1 9.9 %collective-permute-start = (bf16[2,2,128,1,128]{4,2,0,3,1:T(8,128)(2,1)S(1)}, bf16[2,2,128,1,128]{4,2,0,3,1:T(8,128)(2,1)S(1)}, u32[]{:S(2)}, u32[]{:S(2)}) collective-permute-start(bf16[2,2,128,1,128]{4,2,0,3,1:T(8,128)(2,1)S(1)} %copy.37), channel_id=1, source_target_pairs={{24,0},{0,8},{8,16},{16,24},{25,1},{1,9},{9,17},{17,25},{26,2},{2,... | collective-permute-start | bytes 393224 | tf_op jit(solution)/shard_map/while/body/eval_jaxpr/ppermute | solution.py:12
  48.4 9.8 %collective-permute-start.1 = (f32[2,2,128,1,128]{4,2,0,3,1:T(8,128)S(1)}, f32[2,2,128,1,128]{4,2,0,3,1:T(8,128)S(1)}, u32[]{:S(2)}, u32[]{:S(2)}) collective-permute-start(f32[2,2,128,1,128]{4,2,0,3,1:T(8,128)S(1)} %maximum_add_fusion.3), channel_id=1, source_target_pairs={{24,0},{0,8},{8,16},{16,24},{25,1},{1,9},{9,17},{17,25},{26,2},{2,... | collective-permute-start | bytes 786440 | tf_op jit(solution)/shard_map/while/body/eval_jaxpr/ppermute | solution.py:12
  48.5 9.7 %collective-permute-start = (bf16[2,2,128,1,128]{4,2,0,3,1:T(8,128)(2,1)S(1)}, bf16[2,2,128,1,128]{4,2,0,3,1:T(8,128)(2,1)S(1)}, u32[]{:S(2)}, u32[]{:S(2)}) collective-permute-start(bf16[2,2,128,1,128]{4,2,0,3,1:T(8,128)(2,1)S(1)} %copy.37), channel_id=1, source_target_pairs={{24,0},{0,8},{8,16},{16,24},{25,1},{1,9},{9,17},{17,25},{26,2},{2,... | collective-permute-start | bytes 393224 | tf_op jit(solution)/shard_map/while/body/eval_jaxpr/ppermute | solution.py:12
  59.4 7.3 %collective-permute-start.3 = (f32[2,2,128,1,128]{4,2,0,3,1:T(8,128)S(1)}, f32[2,2,128,1,128]{4,2,0,3,1:T(8,128)S(1)}, u32[]{:S(2)}, u32[]{:S(2)}) collective-permute-start(f32[2,2,128,1,128]{4,2,0,3,1:T(8,128)S(1)} %maximum_add_fusion.1), channel_id=1, source_target_pairs={{24,0},{0,8},{8,16},{16,24},{25,1},{1,9},{9,17},{17,25},{26,2},{2,... | collective-permute-start | bytes 786440 | tf_op jit(solution)/shard_map/ppermute | solution.py:12
  66.7 3.2 %collective-permute-start.4 = (f32[2,128,1,128]{3,1,0,2:T(8,128)S(1)}, f32[2,128,1,128]{3,1,0,2:T(8,128)S(1)}, u32[]{:S(2)}, u32[]{:S(2)}) collective-permute-start(f32[2,128,1,128]{3,1,0,2:T(8,128)S(1)} %slice_bitcast_fusion), channel_id=1, source_target_pairs={{4,0},{5,1},{6,2},{7,3},{12,8},{13,9},{14,10},{15,11},{20,16},{21,... | collective-permute-start | bytes 393224 | tf_op jit(solution)/shard_map/ppermute | solution.py:18
where the time goes:
time: 71 us; the launch traced here: 70.6 us
  waiting for transfers between devices  29.3 us (41%)
  other arithmetic  15 us (21%)
  starting transfers between devices  13.7 us (19%)
  local copies, waits for them, and re-layouts  5.88 us (8%)
  matrix products  5.68 us (8%)
  between operations  0.84 us (1%)
    ppermute x7, waiting for transfers between devices, from_behind(): return lax.ppermute(block, axis, route)  28.5 us
    select_n x5, other arithmetic, segment_positions(): return jnp.where(local_rows < span_rows, first_half, second_half)  12.5 us
    ppermute x7, starting transfers between devices, from_behind(): return lax.ppermute(block, axis, route)  10.1 us
    ppermute x2, starting transfers between devices, passed_along(): lax.ppermute(value, axis, [(source, source + steps) for source in range(i...  3.65 us
    gather x4, local copies, waits for them, and re-layouts, segment_positions(): rank_value = jnp.take(pair_order, slot_index)  2.62 us
    unnamed x9, local copies, waits for them, and re-layouts  2.37 us
  transfers between devices with their start and end apart: 9, of which 5 were waited for; matrix products, arithmetic and copies ran while one was open for 13% of the time, Pallas kernels for 0%

commit v1 on v0

v1 whole, which is shorter than its diff:
```python
import functools
import math

import jax
import jax.numpy as jnp
from jax import lax
from jax.experimental import pallas as pl
from jax.experimental.pallas import tpu as pltpu
from jax.sharding import PartitionSpec as P

LOG2E = math.log2(math.e)
STAT_ROWS = 16
SPLIT = 3


def contract(lhs, rhs, lhs_dim, rhs_dim):
    return lax.dot_general(
        lhs, rhs, (((lhs_dim,), (rhs_dim,)), ((), ())), preferred_element_type=jnp.float32
    )


def span_positions(rank_value, rows, span_rows, span_count):
    return jnp.where(
        rows < span_rows,
        rank_value * span_rows + rows,
        (span_count - 2 - rank_value) * span_rows + rows,
    )


def packet_rows(sizes):
    group_size, row_count, _ = sizes
    return 2 * group_size * row_count + SPLIT * STAT_ROWS


def pack_kernel(
    sizes, inner_count, query_hbm, grad_hbm, out_hbm, norm_hbm, key_hbm, value_hbm,
    packet_ref, pairs_ref, out_ref, norm_ref, stat_ref, sems,
):
    group_size, row_count, head_size = sizes
    half = group_size * row_count
    copies = [
        pltpu.make_async_copy(source, target, sems.at[at])
        for at, (source, target) in enumerate(
            [
                (key_hbm, pairs_ref.at[0, 0]),
                (value_hbm, pairs_ref.at[0, 1]),
                (norm_hbm, norm_ref),
                (grad_hbm, packet_ref.at[pl.ds(half, half)]),
                (out_hbm, out_ref),
                (query_hbm, packet_ref.at[pl.ds(0, half)]),
            ]
        )
    ]
    for copy in copies:
        copy.start()
    copies[0].wait()
    copies[1].wait()
    for peer in range(1, inner_count):
        pairs_ref[peer] = pairs_ref[0]
    stat_ref[...] = jnp.zeros_like(stat_ref)
    copies[2].wait()
    stat_ref[:group_size] = norm_ref[...]
    copies[3].wait()
    copies[4].wait()
    for head in range(group_size):
        rows = slice(head * row_count, (head + 1) * row_count)
        grads = packet_ref[half + head * row_count : half + (head + 1) * row_count, :]
        product = grads.astype(jnp.float32) * out_ref[rows, :].astype(jnp.float32)
        stat_ref[8 + head : 9 + head, :] = jnp.sum(product.T, axis=0, keepdims=True)
    rest = jnp.clip(stat_ref[...], -3.38e38, 3.38e38)
    for term in range(SPLIT):
        piece = rest.astype(jnp.bfloat16)
        start = 2 * half + term * STAT_ROWS
        packet_ref[start : start + STAT_ROWS, :] = piece
        rest = rest - piece.astype(jnp.float32)
    copies[5].wait()


def packet_stats(packet_ref, sizes):
    group_size, row_count, _ = sizes
    start = 2 * group_size * row_count
    pieces = [
        packet_ref[start + term * STAT_ROWS : start + (term + 1) * STAT_ROWS, :].astype(jnp.float32)
        for term in range(SPLIT)
    ]
    stats = pieces[0] + (pieces[1] + pieces[2])
    return stats[:8] * LOG2E, stats[8:]


def block_terms(keys, values, visible, packet_ref, sizes):
    group_size, row_count, head_size = sizes
    half = group_size * row_count
    scale = LOG2E / math.sqrt(head_size)
    per_step = 2 if group_size % 2 == 0 else 1
    all_norms, all_dots = packet_stats(packet_ref, sizes)
    key_total = jnp.zeros((keys.shape[0], head_size), jnp.float32)
    value_total = jnp.zeros((keys.shape[0], head_size), jnp.float32)
    query_terms = []
    for first in range(0, group_size, per_step):
        start, stop = first * row_count, (first + per_step) * row_count
        queries = packet_ref[start:stop, :]
        grads = packet_ref[half + start : half + stop, :]
        scores = contract(keys, queries, 1, 1)
        grad_weights = contract(values, grads, 1, 1)
        weights_parts = []
        score_parts = []
        for at in range(per_step):
            head = first + at
            lanes = slice(at * row_count, (at + 1) * row_count)
            weights = jnp.exp2(scores[:, lanes] * scale - all_norms[head : head + 1, :])
            if visible is not None:
                weights = jnp.where(visible, weights, 0.0)
            weights_parts.append(weights.astype(jnp.bfloat16))
            score_parts.append(
                (weights * (grad_weights[:, lanes] - all_dots[head : head + 1, :])).astype(jnp.bfloat16)
            )
        weights_half = jnp.concatenate(weights_parts, axis=1)
        grad_scores = jnp.concatenate(score_parts, axis=1)
        value_total += contract(weights_half, grads, 1, 0)
        key_total += contract(grad_scores, queries, 1, 0)
        query_terms.append(contract(keys, grad_scores, 0, 0))
    return key_total, value_total, query_terms


def store_queries(result_ref, query_terms, sizes):
    group_size, row_count, head_size = sizes
    inv_root = 1.0 / math.sqrt(head_size)
    whole = jnp.concatenate(query_terms, axis=1)
    for head in range(group_size):
        rows = slice(head * row_count, (head + 1) * row_count)
        result_ref[rows, :] = (whole[:, rows] * inv_root).T.astype(result_ref.dtype)


def main_kernel(
    sizes, inner_count, outer_count, pair_ref, packet_ref, next_ref, gathered_ref,
    query_ref, next_query_ref, sums_ref, total_ref,
):
    group_size, row_count, head_size = sizes
    span_rows = row_count // 2
    inv_root = 1.0 / math.sqrt(head_size)
    my_index = lax.axis_index("inner")
    has_next = lax.axis_index("outer") < outer_count - 1

    key_rows = lax.broadcasted_iota(jnp.int32, (row_count, row_count), 0)
    my_rows = lax.broadcasted_iota(jnp.int32, (row_count, row_count), 1)
    my_positions = span_positions(pair_ref[my_index], my_rows, span_rows, 2 * inner_count)
    visible = jnp.concatenate(
        [
            span_positions(pair_ref[peer], key_rows, span_rows, 2 * inner_count) <= my_positions
            for peer in range(inner_count)
        ],
        axis=0,
    )
    keys = jnp.concatenate([gathered_ref[peer, 0] for peer in range(inner_count)], axis=0)
    values = jnp.concatenate([gathered_ref[peer, 1] for peer in range(inner_count)], axis=0)
    key_terms, value_terms, query_terms = block_terms(keys, values, visible, packet_ref, sizes)
    store_queries(query_ref, query_terms, sizes)
    total_ref[0] = key_terms
    total_ref[1] = value_terms

    @pl.when(has_next)
    def _():
        key_terms, value_terms, query_terms = block_terms(keys, values, None, next_ref, sizes)
        store_queries(next_query_ref, query_terms, sizes)
        total_ref[0] += key_terms
        total_ref[1] += value_terms

    for peer in range(inner_count):
        rows = slice(peer * row_count, (peer + 1) * row_count)
        sums_ref[peer, 0] = (total_ref[0, rows, :] * inv_root).astype(jnp.bfloat16)
        sums_ref[peer, 1] = total_ref[1, rows, :].astype(jnp.bfloat16)


def final_kernel(
    inner_count, query_ref, back_ref, sums_ref, query_hbm, key_hbm, value_hbm,
    query_out, key_out, value_out, sems,
):
    key_out[...] = sum(sums_ref[peer, 0].astype(jnp.float32) for peer in range(inner_count)).astype(jnp.bfloat16)
    value_out[...] = sum(sums_ref[peer, 1].astype(jnp.float32) for peer in range(inner_count)).astype(jnp.bfloat16)
    key_copy = pltpu.make_async_copy(key_out, key_hbm, sems.at[0])
    key_copy.start()
    value_copy = pltpu.make_async_copy(value_out, value_hbm, sems.at[1])
    value_copy.start()
    query_out[...] = (query_ref[...] + back_ref[...].astype(jnp.float32)).astype(jnp.bfloat16)
    query_copy = pltpu.make_async_copy(query_out, query_hbm, sems.at[2])
    query_copy.start()
    key_copy.wait()
    value_copy.wait()
    query_copy.wait()


def on_device(queries, key_rows, value_rows, attn_out, grad_out, log_norms, pair_order):
    row_count, group_size, head_size = queries.shape
    inner_count = lax.axis_size("inner")
    outer_count = lax.axis_size("outer")
    sizes = (group_size, row_count, head_size)
    half = group_size * row_count

    def flat(array):
        return jnp.swapaxes(array, 0, 1).reshape(-1, head_size)

    def to_segment(block, ahead):
        route = [(at, at + ahead) for at in range(outer_count) if 0 <= at + ahead < outer_count]
        return lax.ppermute(block, "outer", route)

    smem = pl.BlockSpec(memory_space=pltpu.SMEM)
    vmem = pl.BlockSpec(memory_space=pltpu.VMEM)
    anywhere = pl.BlockSpec(memory_space=pl.ANY)
    params = pltpu.CompilerParams(vmem_limit_bytes=32 * 2**20)
    block_flops = 10 * group_size * row_count * row_count * head_size

    packet, pairs = pl.pallas_call(
        functools.partial(pack_kernel, sizes, inner_count),
        out_shape=(
            jax.ShapeDtypeStruct((packet_rows(sizes), head_size), jnp.bfloat16),
            jax.ShapeDtypeStruct((inner_count, 2, row_count, head_size), jnp.bfloat16),
        ),
        in_specs=[anywhere] * 6,
        out_specs=(vmem, vmem),
        scratch_shapes=[
            pltpu.VMEM((half, head_size), jnp.bfloat16),
            pltpu.VMEM((group_size, row_count), jnp.float32),
            pltpu.VMEM((STAT_ROWS, row_count), jnp.float32),
            pltpu.SemaphoreType.DMA((6,)),
        ],
        cost_estimate=pl.CostEstimate(flops=half * head_size, bytes_accessed=2**20, transcendentals=0),
        compiler_params=params,
    )(flat(queries), flat(grad_out), flat(attn_out), log_norms, flat(key_rows), flat(value_rows))

    next_packet = to_segment(packet, -1)
    gathered = lax.all_to_all(pairs, "inner", 0, 0)

    query_own, query_next, sums = pl.pallas_call(
        functools.partial(main_kernel, sizes, inner_count, outer_count),
        out_shape=(
            jax.ShapeDtypeStruct((half, head_size), jnp.float32),
            jax.ShapeDtypeStruct((half, head_size), jnp.bfloat16),
            jax.ShapeDtypeStruct((inner_count, 2, row_count, head_size), jnp.bfloat16),
        ),
        in_specs=[smem] + [vmem] * 3,
        out_specs=(vmem,) * 3,
        scratch_shapes=[pltpu.VMEM((2, inner_count * row_count, head_size), jnp.float32)],
        cost_estimate=pl.CostEstimate(
            flops=2 * inner_count * block_flops,
            bytes_accessed=2**21,
            transcendentals=2 * inner_count * group_size * row_count**2,
        ),
        compiler_params=params,
    )(pair_order, packet, next_packet, gathered)

    query_back = to_segment(query_next, 1)
    returned = lax.all_to_all(sums, "inner", 0, 0)

    query_out, key_out, value_out = pl.pallas_call(
        functools.partial(final_kernel, inner_count),
        out_shape=(
            jax.ShapeDtypeStruct((half, head_size), jnp.bfloat16),
            jax.ShapeDtypeStruct((row_count, head_size), jnp.bfloat16),
            jax.ShapeDtypeStruct((row_count, head_size), jnp.bfloat16),
        ),
        in_specs=[vmem] * 3,
        out_specs=(anywhere,) * 3,
        scratch_shapes=[
            pltpu.VMEM((half, head_size), jnp.bfloat16),
            pltpu.VMEM((row_count, head_size), jnp.bfloat16),
            pltpu.VMEM((row_count, head_size), jnp.bfloat16),
            pltpu.SemaphoreType.DMA((3,)),
        ],
        compiler_params=params,
    )(query_own, query_back, returned)
    grad_queries = jnp.swapaxes(query_out.reshape(group_size, row_count, head_size), 0, 1)
    return (grad_queries, key_out[:, None, :], value_out[:, None, :])


def solution(mesh):
    in_specs = (
        P(("outer", "inner"), "head", None),
        P(("outer", "inner"), "head", None),
        P(("outer", "inner"), "head", None),
        P(("outer", "inner"), "head", None),
        P(("outer", "inner"), "head", None),
        P("head", ("outer", "inner")),
        P(),
    )
    out_specs = (
        P(("outer", "inner"), "head", None),
        P(("outer", "inner"), "head", None),
        P(("outer", "inner"), "head", None),
    )
    return jax.shard_map(
        on_device, mesh=mesh, in_specs=in_specs, out_specs=out_specs, check_vma=False
    )
```

time: 71 us -> 33.7 us (0.47)
  waiting for transfers between devices: 29.3 us -> 4.03 us
  other arithmetic: 15 us -> 0 us
  blocking collectives: 0 us -> 11.7 us
  starting transfers between devices: 13.7 us -> 6 us
  Pallas kernels: 0 us -> 5.78 us
  matrix products: 5.68 us -> 0 us
  local copies, waits for them, and re-layouts: 5.88 us -> 4.98 us
    ppermute x9 -> x2, waiting for transfers between devices: 29.3 us -> 0.01 us  [to_segment(): return lax.ppermute(block, 'outer', route)]
    select_n x5 -> x0, other arithmetic: 12.5 us -> none  [segment_positions(): return jnp.where(local_rows < span_rows, first_half, second_half)]
    all_to_all x0 -> x1, blocking collectives: none -> 11.7 us  [on_device(): gathered = lax.all_to_all(pairs, 'inner', 0, 0)]
    ppermute x9 -> x2, starting transfers between devices: 13.7 us -> 2.59 us  [to_segment(): return lax.ppermute(block, 'outer', route)]
    pallas_call x0 -> x3, Pallas kernels: none -> 5.78 us  [the longest x1 3.91 us: on_device(): pl.pallas_call(functools.partial(main_kernel, sizes, inner_count, outer_c...]
    dot_general x20 -> x0, matrix products: 5.68 us -> none  [the longest x4 1.38 us: block_grads(): jnp.einsum('ahgrbk,bkhd->arhgd', grad_scores, key_blocks, preferred_eleme...]
    all_to_all x0 -> x1, waiting for transfers between devices: none -> 4.03 us  [on_device(): returned = lax.all_to_all(sums, 'inner', 0, 0)]
    all_to_all x0 -> x1, starting transfers between devices: none -> 3.4 us  [on_device(): returned = lax.all_to_all(sums, 'inner', 0, 0)]
  transfers between devices with their start and end apart: 9 -> 3, of which waited for: 5 -> 1; matrix products, arithmetic and copies ran while one was open for 13% -> 0% of each run, Pallas kernels for 0% -> 0%
where the time goes in v1:
time: 33.7 us; the launch traced here: 33.2 us
  blocking collectives  11.7 us (35%)
  starting transfers between devices  6 us (18%)
  Pallas kernels  5.78 us (17%)
  local copies, waits for them, and re-layouts  4.98 us (15%)
  waiting for transfers between devices  4.03 us (12%)
  between operations  0.69 us (2%)
    all_to_all x1, blocking collectives, on_device(): gathered = lax.all_to_all(pairs, 'inner', 0, 0)  11.7 us
    unnamed x14, local copies, waits for them, and re-layouts  4.98 us
    all_to_all x1, waiting for transfers between devices, on_device(): returned = lax.all_to_all(sums, 'inner', 0, 0)  4.03 us
    pallas_call x1, Pallas kernels, on_device(): pl.pallas_call(functools.partial(main_kernel, sizes, inner_count, outer_c...  3.91 us
    all_to_all x1, starting transfers between devices, on_device(): returned = lax.all_to_all(sums, 'inner', 0, 0)  3.4 us
    ppermute x2, starting transfers between devices, to_segment(): return lax.ppermute(block, 'outer', route)  2.59 us
    pallas_call x1, Pallas kernels, on_device(): pl.pallas_call(functools.partial(pack_kernel, sizes, inner_count), out_sh...  1.1 us
    pallas_call x1, Pallas kernels, on_device(): pl.pallas_call(functools.partial(final_kernel, inner_count), out_shape=(j...  0.77 us
  transfers between devices with their start and end apart: 3, of which 1 were waited for; matrix products, arithmetic and copies ran while one was open for 0% of the time, Pallas kernels for 0%

profile of v1, /device:TPU:0, one launch (start us, length us, event | category | flops | bytes accessed | tf_op | source)
XLA Modules:
  0.0 33.2 jit_solution(11364530373525146318)
XLA Ops:
  0.6 0.0 copy-start.5
  0.6 0.7 %copy-done.5 = f32[6,128]{1,0:T(8,128)S(1)} copy-done((f32[6,128]{1,0:T(8,128)S(1)}, f32[6,128]{1,0:T(8,128)}, u32[]{:S(2)}) %copy-start.5) | copy-done | bytes 3096
  1.3 0.0 copy-start
  1.3 0.9 %copy-done = bf16[128,6,128]{2,0,1:T(8,128)(2,1)S(1)} copy-done((bf16[128,6,128]{2,0,1:T(8,128)(2,1)S(1)}, bf16[128,6,128]{2,0,1:T(8,128)(2,1)}, u32[]{:S(2)}) %copy-start) | copy-done | bytes 196632
  2.2 0.0 copy-start.1
  2.2 0.9 %copy-done.1 = bf16[128,6,128]{2,0,1:T(8,128)(2,1)S(1)} copy-done((bf16[128,6,128]{2,0,1:T(8,128)(2,1)S(1)}, bf16[128,6,128]{2,0,1:T(8,128)(2,1)}, u32[]{:S(2)}) %copy-start.1) | copy-done | bytes 196632
  3.2 0.0 copy-start.2
  3.2 0.9 %copy-done.2 = bf16[128,6,128]{2,0,1:T(8,128)(2,1)S(1)} copy-done((bf16[128,6,128]{2,0,1:T(8,128)(2,1)S(1)}, bf16[128,6,128]{2,0,1:T(8,128)(2,1)}, u32[]{:S(2)}) %copy-start.2) | copy-done | bytes 196632
  4.1 0.0 copy-start.3
  4.1 0.8 %copy-done.3 = bf16[128,1,128]{2,0,1:T(8,128)(2,1)S(1)} copy-done((bf16[128,1,128]{2,0,1:T(8,128)(2,1)S(1)}, bf16[128,1,128]{2,0,1:T(8,128)(2,1)}, u32[]{:S(2)}) %copy-start.3) | copy-done | bytes 32792
  4.9 0.0 copy-start.4
  4.9 0.8 %copy-done.4 = bf16[128,1,128]{2,0,1:T(8,128)(2,1)S(1)} copy-done((bf16[128,1,128]{2,0,1:T(8,128)(2,1)S(1)}, bf16[128,1,128]{2,0,1:T(8,128)(2,1)}, u32[]{:S(2)}) %copy-start.4) | copy-done | bytes 32792
  5.6 1.1 %shard_map.94 = (bf16[1584,128]{1,0:T(8,128)(2,1)S(1)}, bf16[4,2,128,128]{3,2,1,0:T(8,128)(2,1)S(1)}) custom-call(bf16[768,128]{1,0:T(8,128)(2,1)S(1)} %bitcast.16, bf16[768,128]{1,0:T(8,128)(2,1)S(1)} %bitcast.17, bf16[768,128]{1,0:T(8,128)(2,1)S(1)} %bitcast.18, f32[6,128]{1,0:T(8,128)S(1)} %copy-done.5, bf16[128,128]{1,0:T(8,128)(2,1)S(1)} %bitcast.19, ...), custom_call_target="tpu_custom_call" | custom-call | flops 98304 | bytes 1048576 | tf_op jit(solution)/shard_map/pallas_call | solution.py:212
  6.7 1.3 %collective-permute-start = (bf16[1584,128]{1,0:T(8,128)(2,1)S(1)}, bf16[1584,128]{1,0:T(8,128)(2,1)S(1)}, u32[]{:S(2)}, u32[]{:S(2)}) collective-permute-start(bf16[1584,128]{1,0:T(8,128)(2,1)S(1)} %get-tuple-element.11.packet_ref), channel_id=1, source_target_pairs={{4,0},{5,1},{6,2},{7,3},{12,8},{13,9},{14,10},{15,11},{20,16},{21,... | collective-permute-start | bytes 1216520 | tf_op jit(solution)/shard_map/ppermute | solution.py:204
  8.0 0.0 copy-start.6
  8.0 11.7 %all_to_all.10.gathered_ref = bf16[4,2,128,128]{3,2,1,0:T(8,128)(2,1)S(1)} all-to-all(bf16[4,2,128,128]{3,2,1,0:T(8,128)(2,1)S(1)} %get-tuple-element.12), channel_id=1, replica_groups=mesh['inner'=4,'outer'=2,'head'=4] {'inner'}, dimensions={0} | all-to-all | bytes 524288 | tf_op jit(solution)/shard_map/all_to_all | solution.py:231
  19.8 0.0 collective-permute-done.next_ref
  19.8 0.0 copy-done.6
  19.8 3.9 %shard_map.95 = (f32[768,128]{1,0:T(8,128)S(1)}, bf16[768,128]{1,0:T(8,128)(2,1)S(1)}, bf16[4,2,128,128]{3,2,1,0:T(8,128)(2,1)}) custom-call(s32[4]{0:T(128)S(1)} %copy-done.6, bf16[1584,128]{1,0:T(8,128)(2,1)S(1)} %get-tuple-element.11.packet_ref, bf16[1584,128]{1,0:T(8,128)(2,1)S(1)} %collective-permute-done.next_ref, ...), custom_call_target="tpu_custom_call" | custom-call | flops 1006632960 | bytes 2097152 | tf_op jit(solution)/shard_map/pallas_call | solution.py:233
  23.7 3.4 %all-to-all-start.1 = ((bf16[4,2,128,128]{3,2,1,0:T(8,128)(2,1)}), bf16[4,2,128,128]{3,2,1,0:T(8,128)(2,1)S(1)}, u32[]{:S(2)}, u32[]{:S(2)}) async-start(bf16[4,2,128,128]{3,2,1,0:T(8,128)(2,1)} %get-tuple-element.15), calls=%async_computation.1 | async-start | bytes 524288 | tf_op jit(solution)/shard_map/all_to_all | solution.py:252
  27.1 1.3 %collective-permute-start.1 = (bf16[768,128]{1,0:T(8,128)(2,1)S(1)}, bf16[768,128]{1,0:T(8,128)(2,1)S(1)}, u32[]{:S(2)}, u32[]{:S(2)}) collective-permute-start(bf16[768,128]{1,0:T(8,128)(2,1)S(1)} %get-tuple-element.14), channel_id=1, source_target_pairs={{0,4},{1,5},{2,6},{3,7},{8,12},{9,13},{10,14},{11,15},{16,20},{17,... | collective-permute-start | bytes 589832 | tf_op jit(solution)/shard_map/ppermute | solution.py:204
  28.4 4.0 %all-to-all-done.1.sums_ref = bf16[4,2,128,128]{3,2,1,0:T(8,128)(2,1)S(1)} async-done(((bf16[4,2,128,128]{3,2,1,0:T(8,128)(2,1)}), bf16[4,2,128,128]{3,2,1,0:T(8,128)(2,1)S(1)}, u32[]{:S(2)}, u32[]{:S(2)}) %all-to-all-start.1) | async-done | bytes 262176 | tf_op jit(solution)/shard_map/all_to_all | solution.py:252
  32.4 0.0 collective-permute-done.1.back_ref
  32.4 0.8 %shard_map.96 = (bf16[768,128]{1,0:T(8,128)(2,1)}, bf16[128,128]{1,0:T(8,128)(2,1)}, bf16[128,128]{1,0:T(8,128)(2,1)}) custom-call(f32[768,128]{1,0:T(8,128)S(1)} %get-tuple-element.13.query_ref, bf16[768,128]{1,0:T(8,128)(2,1)S(1)} %collective-permute-done.1.back_ref, bf16[4,2,128,128]{3,2,1,0:T(8,128)(2,1)S(1)} %all-to-all-done.1.sums_ref), custom_call_target="tpu_custom_call" | custom-call | tf_op jit(solution)/shard_map/pallas_call | solution.py:254
Async XLA Ops:
  0.6 0.7 %copy-start.5 = (f32[6,128]{1,0:T(8,128)S(1)}, f32[6,128]{1,0:T(8,128)}, u32[]{:S(2)}) copy-start(f32[6,128]{1,0:T(8,128)} %norm_hbm.1) | copy-start | bytes 9220
  1.3 0.9 %copy-start = (bf16[128,6,128]{2,0,1:T(8,128)(2,1)S(1)}, bf16[128,6,128]{2,0,1:T(8,128)(2,1)}, u32[]{:S(2)}) copy-start(bf16[128,6,128]{2,0,1:T(8,128)(2,1)} %param.7) | copy-start | bytes 589828
  2.2 0.9 %copy-start.1 = (bf16[128,6,128]{2,0,1:T(8,128)(2,1)S(1)}, bf16[128,6,128]{2,0,1:T(8,128)(2,1)}, u32[]{:S(2)}) copy-start(bf16[128,6,128]{2,0,1:T(8,128)(2,1)} %param.11) | copy-start | bytes 589828
  3.2 0.9 %copy-start.2 = (bf16[128,6,128]{2,0,1:T(8,128)(2,1)S(1)}, bf16[128,6,128]{2,0,1:T(8,128)(2,1)}, u32[]{:S(2)}) copy-start(bf16[128,6,128]{2,0,1:T(8,128)(2,1)} %param.10) | copy-start | bytes 589828
  4.1 0.8 %copy-start.3 = (bf16[128,1,128]{2,0,1:T(8,128)(2,1)S(1)}, bf16[128,1,128]{2,0,1:T(8,128)(2,1)}, u32[]{:S(2)}) copy-start(bf16[128,1,128]{2,0,1:T(8,128)(2,1)} %param.8) | copy-start | bytes 98308
  4.9 0.8 %copy-start.4 = (bf16[128,1,128]{2,0,1:T(8,128)(2,1)S(1)}, bf16[128,1,128]{2,0,1:T(8,128)(2,1)}, u32[]{:S(2)}) copy-start(bf16[128,1,128]{2,0,1:T(8,128)(2,1)} %param.9) | copy-start | bytes 98308
  6.7 13.1 %collective-permute-start = (bf16[1584,128]{1,0:T(8,128)(2,1)S(1)}, bf16[1584,128]{1,0:T(8,128)(2,1)S(1)}, u32[]{:S(2)}, u32[]{:S(2)}) collective-permute-start(bf16[1584,128]{1,0:T(8,128)(2,1)S(1)} %get-tuple-element.11.packet_ref), channel_id=1, source_target_pairs={{4,0},{5,1},{6,2},{7,3},{12,8},{13,9},{14,10},{15,11},{20,16},{21,... | collective-permute-start | bytes 1216520 | tf_op jit(solution)/shard_map/ppermute | solution.py:204
  8.0 11.8 %copy-start.6 = (s32[4]{0:T(128)S(1)}, s32[4]{0:T(128)}, u32[]{:S(2)}) copy-start(s32[4]{0:T(128)} %pair_ref.1) | copy-start | bytes 52
  23.7 8.8 %all-to-all-start.1 = ((bf16[4,2,128,128]{3,2,1,0:T(8,128)(2,1)}), bf16[4,2,128,128]{3,2,1,0:T(8,128)(2,1)S(1)}, u32[]{:S(2)}, u32[]{:S(2)}) async-start(bf16[4,2,128,128]{3,2,1,0:T(8,128)(2,1)} %get-tuple-element.15), calls=%async_computation.1 | async-start | bytes 524288 | tf_op jit(solution)/shard_map/all_to_all | solution.py:252
  27.1 5.3 %collective-permute-start.1 = (bf16[768,128]{1,0:T(8,128)(2,1)S(1)}, bf16[768,128]{1,0:T(8,128)(2,1)S(1)}, u32[]{:S(2)}, u32[]{:S(2)}) collective-permute-start(bf16[768,128]{1,0:T(8,128)(2,1)S(1)} %get-tuple-element.14), channel_id=1, source_target_pairs={{0,4},{1,5},{2,6},{3,7},{8,12},{9,13},{10,14},{11,15},{16,20},{17,... | collective-permute-start | bytes 589832 | tf_op jit(solution)/shard_map/ppermute | solution.py:204

commit v2 on v1

v2 whole, which is shorter than its diff:
```python
import functools
import math

import jax
import jax.numpy as jnp
from jax import lax
from jax.experimental import pallas as pl
from jax.experimental.pallas import tpu as pltpu
from jax.sharding import PartitionSpec as P

LOG2E = math.log2(math.e)
STAT_ROWS = 16
SPLIT = 3


def contract(lhs, rhs, lhs_dim, rhs_dim):
    return lax.dot_general(
        lhs, rhs, (((lhs_dim,), (rhs_dim,)), ((), ())), preferred_element_type=jnp.float32
    )


def packet_rows(sizes):
    group_size, row_count, _ = sizes
    return 2 * group_size * row_count + SPLIT * STAT_ROWS


def slot_offset(slot, outer_index, bits):
    offset = 0
    for step in range(bits):
        if (slot >> step) & 1:
            offset = offset | lax.shift_left(jnp.int32(1), lax.rem(outer_index + step, bits))
    return offset


def pair_kernel(key_hbm, value_hbm, pair_ref, sems):
    copies = [
        pltpu.make_async_copy(key_hbm, pair_ref.at[0, 0], sems.at[0]),
        pltpu.make_async_copy(value_hbm, pair_ref.at[0, 1], sems.at[1]),
    ]
    for copy in copies:
        copy.start()
    for copy in copies:
        copy.wait()


def pack_kernel(
    sizes, inner_count, bits, query_hbm, grad_hbm, out_hbm, norm_hbm, order_hbm,
    packet_ref, rank_ref, out_ref, norm_ref, stat_ref, order_ref, sems,
):
    group_size, row_count, _ = sizes
    half = group_size * row_count
    copies = [
        pltpu.make_async_copy(source, target, sems.at[at])
        for at, (source, target) in enumerate(
            [
                (grad_hbm, packet_ref.at[pl.ds(half, half)]),
                (out_hbm, out_ref),
                (norm_hbm, norm_ref),
                (order_hbm, order_ref),
                (query_hbm, packet_ref.at[pl.ds(0, half)]),
            ]
        )
    ]
    for copy in copies:
        copy.start()
    stat_ref[...] = jnp.zeros_like(stat_ref)
    for copy in copies[:3]:
        copy.wait()
    stat_ref[:group_size] = norm_ref[...]
    for head in range(group_size):
        rows = slice(head * row_count, (head + 1) * row_count)
        grads = packet_ref[half + head * row_count : half + (head + 1) * row_count, :]
        product = grads.astype(jnp.float32) * out_ref[rows, :].astype(jnp.float32)
        stat_ref[8 + head : 9 + head, :] = jnp.sum(product.T, axis=0, keepdims=True)
    rest = jnp.clip(stat_ref[...], -3.38e38, 3.38e38)
    for term in range(SPLIT):
        piece = rest.astype(jnp.bfloat16)
        start = 2 * half + term * STAT_ROWS
        packet_ref[start : start + STAT_ROWS, :] = piece
        rest = rest - piece.astype(jnp.float32)
    copies[3].wait()
    my_index = lax.axis_index("inner")
    outer_index = lax.axis_index("outer")
    for slot in range(inner_count):
        peer = my_index ^ slot_offset(slot, outer_index, bits)
        rank_ref[slot : slot + 1, :] = jnp.full((1, row_count), order_ref[peer], jnp.int32)
    copies[4].wait()


def packet_stats(packet_ref, sizes):
    group_size, row_count, _ = sizes
    start = 2 * group_size * row_count
    pieces = [
        packet_ref[start + term * STAT_ROWS : start + (term + 1) * STAT_ROWS, :].astype(jnp.float32)
        for term in range(SPLIT)
    ]
    stats = pieces[0] + (pieces[1] + pieces[2])
    return stats[:8] * LOG2E, stats[8:]


def block_terms(keys, values, visible, packet_ref, sizes):
    group_size, row_count, head_size = sizes
    half = group_size * row_count
    scale = LOG2E / math.sqrt(head_size)
    per_step = 2 if group_size % 2 == 0 else 1
    all_norms, all_dots = packet_stats(packet_ref, sizes)
    key_total = jnp.zeros((keys.shape[0], head_size), jnp.float32)
    value_total = jnp.zeros((keys.shape[0], head_size), jnp.float32)
    query_terms = []
    for first in range(0, group_size, per_step):
        start, stop = first * row_count, (first + per_step) * row_count
        queries = packet_ref[start:stop, :]
        grads = packet_ref[half + start : half + stop, :]
        scores = contract(keys, queries, 1, 1)
        grad_weights = contract(values, grads, 1, 1)
        weights_parts = []
        score_parts = []
        for at in range(per_step):
            head = first + at
            lanes = slice(at * row_count, (at + 1) * row_count)
            weights = jnp.exp2(scores[:, lanes] * scale - all_norms[head : head + 1, :])
            if visible is not None:
                weights = jnp.where(visible, weights, 0.0)
            weights_parts.append(weights.astype(jnp.bfloat16))
            score_parts.append(
                (weights * (grad_weights[:, lanes] - all_dots[head : head + 1, :])).astype(jnp.bfloat16)
            )
        weights_half = jnp.concatenate(weights_parts, axis=1)
        grad_scores = jnp.concatenate(score_parts, axis=1)
        value_total += contract(weights_half, grads, 1, 0)
        key_total += contract(grad_scores, queries, 1, 0)
        query_terms.append(contract(keys, grad_scores, 0, 0))
    return key_total, value_total, jnp.concatenate(query_terms, axis=1)


def visible_rows(rank_ref, slots, inner_count, row_count):
    span_rows = row_count // 2
    key_rows = lax.broadcasted_iota(jnp.int32, (row_count, row_count), 0)
    my_rows = lax.broadcasted_iota(jnp.int32, (row_count, row_count), 1)

    def positions(rank, rows):
        return jnp.where(
            rows < span_rows,
            rank * span_rows + rows,
            (2 * inner_count - 2 - rank) * span_rows + rows,
        )

    mine = positions(rank_ref[0:1, :], my_rows)
    return jnp.concatenate(
        [positions(rank_ref[slot : slot + 1, :], key_rows) <= mine for slot in slots], axis=0
    )


def stacked(blocks_ref, which):
    return jnp.concatenate([blocks_ref[at, which] for at in range(blocks_ref.shape[0])], axis=0)


def near_kernel(sizes, inner_count, packet_ref, rank_ref, blocks_ref, query_ref, total_ref):
    count = blocks_ref.shape[0]
    visible = visible_rows(rank_ref, range(count), inner_count, sizes[1])
    key_terms, value_terms, query_terms = block_terms(
        stacked(blocks_ref, 0), stacked(blocks_ref, 1), visible, packet_ref, sizes
    )
    query_ref[...] = query_terms
    total_ref[0] = key_terms
    total_ref[1] = value_terms


def near_next_kernel(
    sizes, outer_count, next_ref, blocks_ref, total_in, next_query_ref, total_ref
):
    has_next = lax.axis_index("outer") < outer_count - 1
    total_ref[...] = total_in[...]

    @pl.when(has_next)
    def _():
        key_terms, value_terms, query_terms = block_terms(
            stacked(blocks_ref, 0), stacked(blocks_ref, 1), None, next_ref, sizes
        )
        next_query_ref[...] = query_terms
        total_ref[0] += key_terms
        total_ref[1] += value_terms


def far_kernel(
    sizes, inner_count, outer_count, packet_ref, next_ref, rank_ref, blocks_ref, query_in,
    next_query_in, query_ref, next_query_ref, sums_ref, total_ref,
):
    _, row_count, head_size = sizes
    count = blocks_ref.shape[0]
    inv_root = 1.0 / math.sqrt(head_size)
    has_next = lax.axis_index("outer") < outer_count - 1
    keys, values = stacked(blocks_ref, 0), stacked(blocks_ref, 1)
    total_ref[...] = jnp.zeros_like(total_ref)

    @pl.when(has_next)
    def _():
        key_terms, value_terms, query_terms = block_terms(keys, values, None, next_ref, sizes)
        next_query_ref[...] = (next_query_in[...] + query_terms).astype(jnp.bfloat16)
        total_ref[0] = key_terms
        total_ref[1] = value_terms

    visible = visible_rows(rank_ref, range(count, 2 * count), inner_count, row_count)
    key_terms, value_terms, query_terms = block_terms(keys, values, visible, packet_ref, sizes)
    query_ref[...] = query_in[...] + query_terms
    key_terms = (key_terms + total_ref[0]) * inv_root
    value_terms += total_ref[1]
    for slot in range(count):
        rows = slice(slot * row_count, (slot + 1) * row_count)
        sums_ref[slot, 0] = key_terms[rows].astype(jnp.bfloat16)
        sums_ref[slot, 1] = value_terms[rows].astype(jnp.bfloat16)


def query_kernel(sizes, query_ref, back_ref, result_hbm, total_ref, result_ref, sem):
    group_size, row_count, head_size = sizes
    inv_root = 1.0 / math.sqrt(head_size)
    has_prev = lax.axis_index("outer") > 0
    total_ref[...] = query_ref[...]

    @pl.when(has_prev)
    def _():
        total_ref[...] += back_ref[...].astype(jnp.float32)

    for head in range(group_size):
        rows = slice(head * row_count, (head + 1) * row_count)
        result_ref[rows, :] = (total_ref[:, rows] * inv_root).T.astype(jnp.bfloat16)
    copy = pltpu.make_async_copy(result_ref, result_hbm, sem)
    copy.start()
    copy.wait()


def turn_kernel(sizes, slots, total_ref, *refs):
    _, row_count, head_size = sizes
    inv_root = 1.0 / math.sqrt(head_size)
    returned, send_ref = refs[:-1], refs[-1]
    for at, slot in enumerate(slots):
        rows = slice(slot * row_count, (slot + 1) * row_count)
        for which, factor in ((0, inv_root), (1, 1.0)):
            total = total_ref[which, rows, :] * factor
            for ref in returned:
                total += ref[slot, which].astype(jnp.float32)
            send_ref[at, which] = total.astype(jnp.bfloat16)


def sum_kernel(sizes, *refs):
    _, row_count, head_size = sizes
    inv_root = 1.0 / math.sqrt(head_size)
    total_ref, returned = refs[0], refs[1:-5]
    key_hbm, value_hbm, key_ref, value_ref, sems = refs[-5:]
    key_total = total_ref[0, :row_count, :] * inv_root
    value_total = total_ref[1, :row_count, :]
    for ref in returned:
        key_total += ref[0, 0].astype(jnp.float32)
        value_total += ref[0, 1].astype(jnp.float32)
    key_ref[...] = key_total.astype(jnp.bfloat16)
    value_ref[...] = value_total.astype(jnp.bfloat16)
    copies = [
        pltpu.make_async_copy(key_ref, key_hbm, sems.at[0]),
        pltpu.make_async_copy(value_ref, value_hbm, sems.at[1]),
    ]
    for copy in copies:
        copy.start()
    for copy in copies:
        copy.wait()


def on_device(queries, key_rows, value_rows, attn_out, grad_out, log_norms, pair_order):
    row_count, group_size, head_size = queries.shape
    inner_count = lax.axis_size("inner")
    outer_count = lax.axis_size("outer")
    bits = inner_count.bit_length() - 1
    assert inner_count == 1 << bits and bits > 0
    sizes = (group_size, row_count, head_size)
    half = group_size * row_count
    near = inner_count // 2

    def flat(array):
        return jnp.swapaxes(array, 0, 1).reshape(-1, head_size)

    def in_hbm(array):
        return pltpu.with_memory_space_constraint(array, pltpu.HBM)

    def to_segment(block, ahead):
        route = [(at, (at + ahead) % outer_count) for at in range(outer_count)]
        return lax.ppermute(block, "outer", route)

    def exchange(block, step):
        route = []
        for inner in range(inner_count):
            for outer in range(outer_count):
                peer = inner ^ (1 << ((step + outer) % bits))
                route.append((inner * outer_count + outer, peer * outer_count + outer))
        return lax.ppermute(block, ("inner", "outer"), route)

    vmem = pl.BlockSpec(memory_space=pltpu.VMEM)
    hbm = pl.BlockSpec(memory_space=pltpu.HBM)
    roomy = pltpu.CompilerParams(vmem_limit_bytes=32 * 2**20)

    def shape(dims, dtype):
        return jax.ShapeDtypeStruct(dims, dtype)

    def cost(blocks, data=2**20):
        each = group_size * row_count * row_count
        return pl.CostEstimate(
            flops=10 * blocks * each * head_size, bytes_accessed=data, transcendentals=blocks * each
        )

    pair = pl.pallas_call(
        pair_kernel,
        out_shape=shape((1, 2, row_count, head_size), jnp.bfloat16),
        in_specs=[hbm] * 2,
        out_specs=vmem,
        scratch_shapes=[pltpu.SemaphoreType.DMA((2,))],
        compiler_params=roomy,
    )(in_hbm(flat(key_rows)), in_hbm(flat(value_rows)))
    first = exchange(pair, 0)
    pack_inputs = (flat(queries), flat(grad_out), flat(attn_out), log_norms, pair_order)
    pair, pack_inputs = lax.optimization_barrier((pair, pack_inputs))

    packet, rank = pl.pallas_call(
        functools.partial(pack_kernel, sizes, inner_count, bits),
        out_shape=(
            shape((packet_rows(sizes), head_size), jnp.bfloat16),
            shape((max(8, inner_count), row_count), jnp.int32),
        ),
        in_specs=[hbm] * 5,
        out_specs=(vmem, vmem),
        scratch_shapes=[
            pltpu.VMEM((half, head_size), jnp.bfloat16),
            pltpu.VMEM((group_size, row_count), jnp.float32),
            pltpu.VMEM((STAT_ROWS, row_count), jnp.float32),
            pltpu.SMEM((inner_count,), jnp.int32),
            pltpu.SemaphoreType.DMA((5,)),
        ],
        cost_estimate=cost(1),
        compiler_params=roomy,
    )(*(in_hbm(array) for array in pack_inputs))
    first, packet = lax.optimization_barrier((first, packet))

    near_blocks = jnp.concatenate([pair, first], axis=0)
    next_packet = to_segment(packet, -1)
    for step in range(1, bits - 1):
        near_blocks = jnp.concatenate([near_blocks, exchange(near_blocks, step)], axis=0)
    far_blocks = exchange(near_blocks, bits - 1) if bits > 1 else first
    if bits == 1:
        near_blocks = pair

    query_near, near_total = pl.pallas_call(
        functools.partial(near_kernel, sizes, inner_count),
        out_shape=(
            shape((head_size, half), jnp.float32),
            shape((2, near * row_count, head_size), jnp.float32),
        ),
        in_specs=[vmem] * 3,
        out_specs=(vmem,) * 2,
        cost_estimate=cost(near),
        compiler_params=roomy,
    )(packet, rank, near_blocks)

    next_near, near_total = pl.pallas_call(
        functools.partial(near_next_kernel, sizes, outer_count),
        out_shape=(
            shape((head_size, half), jnp.float32),
            shape((2, near * row_count, head_size), jnp.float32),
        ),
        in_specs=[vmem] * 3,
        out_specs=(vmem,) * 2,
        cost_estimate=cost(near),
        compiler_params=roomy,
    )(next_packet, near_blocks, near_total)

    query_own, query_next, sums = pl.pallas_call(
        functools.partial(far_kernel, sizes, inner_count, outer_count),
        out_shape=(
            shape((head_size, half), jnp.float32),
            shape((head_size, half), jnp.bfloat16),
            shape((near, 2, row_count, head_size), jnp.bfloat16),
        ),
        in_specs=[vmem] * 6,
        out_specs=(vmem,) * 3,
        scratch_shapes=[pltpu.VMEM((2, near * row_count, head_size), jnp.float32)],
        cost_estimate=cost(2 * near),
        compiler_params=roomy,
    )(packet, next_packet, rank, far_blocks, query_near, next_near)

    returned = [exchange(sums, bits - 1)]
    query_back = to_segment(query_next, 1)

    query_out = pl.pallas_call(
        functools.partial(query_kernel, sizes),
        out_shape=shape((half, head_size), jnp.bfloat16),
        in_specs=[vmem] * 2,
        out_specs=hbm,
        scratch_shapes=[
            pltpu.VMEM((head_size, half), jnp.float32),
            pltpu.VMEM((half, head_size), jnp.bfloat16),
            pltpu.SemaphoreType.DMA,
        ],
        cost_estimate=cost(1),
        compiler_params=roomy,
    )(query_own, query_back)

    for step in range(bits - 2, -1, -1):
        slots = range(1 << step, 2 << step)
        send = pl.pallas_call(
            functools.partial(turn_kernel, sizes, slots),
            out_shape=shape((len(slots), 2, row_count, head_size), jnp.bfloat16),
            in_specs=[vmem] * (1 + len(returned)),
            out_specs=vmem,
            compiler_params=roomy,
        )(near_total, *returned)
        returned.append(exchange(send, step))

    near_total, query_out = lax.optimization_barrier((near_total, query_out))
    key_out, value_out = pl.pallas_call(
        functools.partial(sum_kernel, sizes),
        out_shape=(shape((row_count, head_size), jnp.bfloat16),) * 2,
        in_specs=[vmem] * (1 + len(returned)),
        out_specs=(hbm, hbm),
        scratch_shapes=[
            pltpu.VMEM((row_count, head_size), jnp.bfloat16),
            pltpu.VMEM((row_count, head_size), jnp.bfloat16),
            pltpu.SemaphoreType.DMA((2,)),
        ],
        compiler_params=roomy,
    )(near_total, *returned)
    grad_queries = jnp.swapaxes(query_out.reshape(group_size, row_count, head_size), 0, 1)
    return (grad_queries, key_out[:, None, :], value_out[:, None, :])


def solution(mesh):
    in_specs = (
        P(("outer", "inner"), "head", None),
        P(("outer", "inner"), "head", None),
        P(("outer", "inner"), "head", None),
        P(("outer", "inner"), "head", None),
        P(("outer", "inner"), "head", None),
        P("head", ("outer", "inner")),
        P(),
    )
    out_specs = (
        P(("outer", "inner"), "head", None),
        P(("outer", "inner"), "head", None),
        P(("outer", "inner"), "head", None),
    )
    return jax.shard_map(
        on_device, mesh=mesh, in_specs=in_specs, out_specs=out_specs, check_vma=False
    )
```

time: 33.7 us -> 23.9 us (0.71)
  blocking collectives: 11.7 us -> 0 us
  local copies, waits for them, and re-layouts: 4.98 us -> 0.02 us
  starting transfers between devices: 6 us -> 9.34 us
  waiting for transfers between devices: 4.03 us -> 6.51 us
  Pallas kernels: 5.78 us -> 7.09 us
    all_to_all x1 -> x0, blocking collectives: 11.7 us -> none  [on_device(): gathered = lax.all_to_all(pairs, 'inner', 0, 0)]
    ppermute x0 -> x4, starting transfers between devices: none -> 9.26 us  [exchange(): return lax.ppermute(block, ('inner', 'outer'), route)]
    ppermute x0 -> x4, waiting for transfers between devices: none -> 6.51 us  [exchange(): return lax.ppermute(block, ('inner', 'outer'), route)]
    unnamed x14 -> x1, local copies, waits for them, and re-layouts: 4.98 us -> 0.01 us
    all_to_all x1 -> x0, waiting for transfers between devices: 4.03 us -> none  [on_device(): returned = lax.all_to_all(sums, 'inner', 0, 0)]
    all_to_all x1 -> x0, starting transfers between devices: 3.4 us -> none  [on_device(): returned = lax.all_to_all(sums, 'inner', 0, 0)]
    ppermute x2, starting transfers between devices: 2.59 us -> 0.07 us  [to_segment(): return lax.ppermute(block, 'outer', route)]
    pallas_call x3 -> x8, Pallas kernels: 5.78 us -> 7.09 us  [the longest x1 1.74 us: on_device(): pl.pallas_call(functools.partial(far_kernel, sizes, inner_count, outer_co...]
  transfers between devices with their start and end apart: 3 -> 6, of which waited for: 1 -> 4; matrix products, arithmetic and copies ran while one was open for 0% -> 0% of each run, Pallas kernels for 0% -> 16%
where the time goes in v2:
time: 23.9 us; the launch traced here: 23.7 us
  starting transfers between devices  9.34 us (39%)
  Pallas kernels  7.09 us (30%)
  waiting for transfers between devices  6.51 us (27%)
  between operations  0.7 us (3%)
    ppermute x4, starting transfers between devices, exchange(): return lax.ppermute(block, ('inner', 'outer'), route)  9.26 us
    ppermute x4, waiting for transfers between devices, exchange(): return lax.ppermute(block, ('inner', 'outer'), route)  6.51 us
    pallas_call x1, Pallas kernels, on_device(): pl.pallas_call(functools.partial(far_kernel, sizes, inner_count, outer_co...  1.74 us
    pallas_call x1, Pallas kernels, on_device(): pl.pallas_call(functools.partial(pack_kernel, sizes, inner_count, bits),...  1.29 us
    pallas_call x1, Pallas kernels, on_device(): pl.pallas_call(functools.partial(near_next_kernel, sizes, outer_count), o...  0.88 us
    pallas_call x1, Pallas kernels, on_device(): pl.pallas_call(functools.partial(near_kernel, sizes, inner_count), out_sh...  0.85 us
    pallas_call x1, Pallas kernels, on_device(): pl.pallas_call(functools.partial(query_kernel, sizes), out_shape=shape((h...  0.85 us
    pallas_call x1, Pallas kernels, on_device(): pl.pallas_call(pair_kernel, out_shape=shape((1, 2, row_count, head_size),...  0.79 us
  transfers between devices with their start and end apart: 6, of which 4 were waited for; matrix products, arithmetic and copies ran while one was open for 0% of the time, Pallas kernels for 16%

profile of v2, /device:TPU:0, one launch (start us, length us, event | category | flops | bytes accessed | tf_op | source)
XLA Modules:
  0.0 23.7 jit_solution(10784502089206253262)
XLA Ops:
  0.6 0.8 %shard_map.94 = bf16[1,2,128,128]{3,2,1,0:T(8,128)(2,1)S(1)} custom-call(bf16[128,128]{1,0:T(8,128)(2,1)} %bitcast.20, bf16[128,128]{1,0:T(8,128)(2,1)} %bitcast.21), custom_call_target="tpu_custom_call" | custom-call | tf_op jit(solution)/shard_map/pallas_call | solution.py:308
  1.4 3.0 %collective-permute-start = (bf16[1,2,128,128]{3,2,1,0:T(8,128)(2,1)S(1)}, bf16[1,2,128,128]{3,2,1,0:T(8,128)(2,1)S(1)}, u32[]{:S(2)}, u32[]{:S(2)}) collective-permute-start(bf16[1,2,128,128]{3,2,1,0:T(8,128)(2,1)S(1)} %shard_map.94), channel_id=1, source_target_pairs={{0,8},{4,20},{8,0},{12,28},{16,24},{20,4},{24,16},{28,12},{1,9},{5... | collective-permute-start | bytes 196616 | tf_op jit(solution)/shard_map/ppermute | solution.py:293
  4.4 1.3 %shard_map.95 = (bf16[1584,128]{1,0:T(8,128)(2,1)S(1)}, s32[8,128]{1,0:T(8,128)S(1)}) custom-call(bf16[768,128]{1,0:T(8,128)(2,1)} %bitcast.16, bf16[768,128]{1,0:T(8,128)(2,1)} %bitcast.17, bf16[768,128]{1,0:T(8,128)(2,1)} %bitcast.18, f32[6,128]{1,0:T(8,128)} %norm_hbm, s32[4]{0:T(128)} %order_hbm), custom_call_target="tpu_custom_call" | custom-call | flops 125829120 | bytes 1048576 | tf_op jit(solution)/shard_map/pallas_call | solution.py:320
  5.7 0.9 %collective-permute-done = bf16[1,2,128,128]{3,2,1,0:T(8,128)(2,1)S(1)} collective-permute-done((bf16[1,2,128,128]{3,2,1,0:T(8,128)(2,1)S(1)}, bf16[1,2,128,128]{3,2,1,0:T(8,128)(2,1)S(1)}, u32[]{:S(2)}, u32[]{:S(2)}) %collective-permute-start) | collective-permute-done | bytes 65568 | tf_op jit(solution)/shard_map/ppermute | solution.py:293
  6.7 0.0 collective-permute-start.1
  6.7 2.1 %collective-permute-start.2 = (bf16[2,2,128,128]{3,2,1,0:T(8,128)(2,1)S(1)}, bf16[2,2,128,128]{3,2,1,0:T(8,128)(2,1)S(1)}, u32[]{:S(2)}, u32[]{:S(2)}) collective-permute-start(bf16[2,2,128,128]{3,2,1,0:T(8,128)(2,1)S(1)} %constant_dynamic-update-slice_fusion.blocks_ref), channel_id=1, source_target_pairs={{0,16},{4,12},{8,24},{12,4},{16,0},{20,28},{24,8},{28,20},{1,17},{... | collective-permute-start | bytes 393224 | tf_op jit(solution)/shard_map/ppermute | solution.py:293
  8.8 0.9 %shard_map.96 = (f32[128,768]{1,0:T(8,128)S(1)}, f32[2,256,128]{2,1,0:T(8,128)S(1)}) custom-call(bf16[1584,128]{1,0:T(8,128)(2,1)S(1)} %get-tuple-element.30.packet_ref, s32[8,128]{1,0:T(8,128)S(1)} %get-tuple-element.33.rank_ref, bf16[2,2,128,128]{3,2,1,0:T(8,128)(2,1)S(1)} %constant_dynamic-update-slice_fusion.blocks_ref), custom_call_target="tpu_custom_call" | custom-call | flops 251658240 | bytes 1048576 | tf_op jit(solution)/shard_map/pallas_call | solution.py:348
  9.7 0.0 collective-permute-done.1.next_ref
  9.7 0.9 %shard_map.97 = (f32[128,768]{1,0:T(8,128)S(1)}, f32[2,256,128]{2,1,0:T(8,128)S(1)}) custom-call(bf16[1584,128]{1,0:T(8,128)(2,1)S(1)} %collective-permute-done.1.next_ref, bf16[2,2,128,128]{3,2,1,0:T(8,128)(2,1)S(1)} %constant_dynamic-update-slice_fusion.blocks_ref, f32[2,256,128]{2,1,0:T(8,128)S(1)} %get-tuple-element.34.total_in), custom_call_target="tpu_custom_call" | custom-call | flops 251658240 | bytes 1048576 | tf_op jit(solution)/shard_map/pallas_call | solution.py:360
  10.6 1.2 %collective-permute-done.2.blocks_ref = bf16[2,2,128,128]{3,2,1,0:T(8,128)(2,1)S(1)} collective-permute-done((bf16[2,2,128,128]{3,2,1,0:T(8,128)(2,1)S(1)}, bf16[2,2,128,128]{3,2,1,0:T(8,128)(2,1)S(1)}, u32[]{:S(2)}, u32[]{:S(2)}) %collective-permute-start.2) | collective-permute-done | bytes 131104 | tf_op jit(solution)/shard_map/ppermute | solution.py:293
  11.8 1.7 %shard_map.98 = (f32[128,768]{1,0:T(8,128)S(1)}, bf16[128,768]{1,0:T(8,128)(2,1)S(1)}, bf16[2,2,128,128]{3,2,1,0:T(8,128)(2,1)S(1)}) custom-call(bf16[1584,128]{1,0:T(8,128)(2,1)S(1)} %get-tuple-element.30.packet_ref, bf16[1584,128]{1,0:T(8,128)(2,1)S(1)} %collective-permute-done.1.next_ref, s32[8,128]{1,0:T(8,128)S(1)} %get-tuple-element.33.rank_ref, ...), custom_call_target="tpu_custom_call" | custom-call | flops 503316480 | bytes 1048576 | tf_op jit(solution)/shard_map/pallas_call | solution.py:372
  13.5 0.1 collective-permute-start.3
  13.6 2.1 %collective-permute-start.4 = (bf16[2,2,128,128]{3,2,1,0:T(8,128)(2,1)S(1)}, bf16[2,2,128,128]{3,2,1,0:T(8,128)(2,1)S(1)}, u32[]{:S(2)}, u32[]{:S(2)}) collective-permute-start(bf16[2,2,128,128]{3,2,1,0:T(8,128)(2,1)S(1)} %get-tuple-element.42), channel_id=1, source_target_pairs={{0,16},{4,12},{8,24},{12,4},{16,0},{20,28},{24,8},{28,20},{1,17},{... | collective-permute-start | bytes 393224 | tf_op jit(solution)/shard_map/ppermute | solution.py:293
  15.7 2.9 %collective-permute-done.4.refs_0_.refs_1_ = bf16[2,2,128,128]{3,2,1,0:T(8,128)(2,1)S(1)} collective-permute-done((bf16[2,2,128,128]{3,2,1,0:T(8,128)(2,1)S(1)}, bf16[2,2,128,128]{3,2,1,0:T(8,128)(2,1)S(1)}, u32[]{:S(2)}, u32[]{:S(2)}) %collective-permute-start.4) | collective-permute-done | bytes 131104 | tf_op jit(solution)/shard_map/ppermute | solution.py:293
  18.7 2.1 %collective-permute-start.5 = (bf16[1,2,128,128]{3,2,1,0:T(8,128)(2,1)S(1)}, bf16[1,2,128,128]{3,2,1,0:T(8,128)(2,1)S(1)}, u32[]{:S(2)}, u32[]{:S(2)}) collective-permute-start(bf16[1,2,128,128]{3,2,1,0:T(8,128)(2,1)S(1)} %shard_map.100), channel_id=1, source_target_pairs={{0,8},{4,20},{8,0},{12,28},{16,24},{20,4},{24,16},{28,12},{1,9},{5... | collective-permute-start | bytes 196616 | tf_op jit(solution)/shard_map/ppermute | solution.py:293
  20.7 0.0 collective-permute-done.3.back_ref
  20.7 0.8 %shard_map.99 = bf16[768,128]{1,0:T(8,128)(2,1)} custom-call(f32[128,768]{1,0:T(8,128)S(1)} %get-tuple-element.38.query_ref, bf16[128,768]{1,0:T(8,128)(2,1)S(1)} %collective-permute-done.3.back_ref), custom_call_target="tpu_custom_call" | custom-call | flops 125829120 | bytes 1048576 | tf_op jit(solution)/shard_map/pallas_call | solution.py:389
  21.6 1.4 %collective-permute-done.5.refs_2_ = bf16[1,2,128,128]{3,2,1,0:T(8,128)(2,1)S(1)} collective-permute-done((bf16[1,2,128,128]{3,2,1,0:T(8,128)(2,1)S(1)}, bf16[1,2,128,128]{3,2,1,0:T(8,128)(2,1)S(1)}, u32[]{:S(2)}, u32[]{:S(2)}) %collective-permute-start.5) | collective-permute-done | bytes 65568 | tf_op jit(solution)/shard_map/ppermute | solution.py:293
  23.0 0.7 %shard_map.101 = (bf16[128,128]{1,0:T(8,128)(2,1)}, bf16[128,128]{1,0:T(8,128)(2,1)}) custom-call(f32[2,256,128]{2,1,0:T(8,128)S(1)} %get-tuple-element.41.total_ref.refs_0_, bf16[2,2,128,128]{3,2,1,0:T(8,128)(2,1)S(1)} %collective-permute-done.4.refs_0_.refs_1_, bf16[1,2,128,128]{3,2,1,0:T(8,128)(2,1)S(1)} %collective-permute-done.5.refs_2_), custom_call_target="tpu_custom_call" | custom-call | tf_op jit(solution)/shard_map/pallas_call | solution.py:415
  (3 shorter events, 0.0 us)
Async XLA Ops:
  1.4 5.2 %collective-permute-start = (bf16[1,2,128,128]{3,2,1,0:T(8,128)(2,1)S(1)}, bf16[1,2,128,128]{3,2,1,0:T(8,128)(2,1)S(1)}, u32[]{:S(2)}, u32[]{:S(2)}) collective-permute-start(bf16[1,2,128,128]{3,2,1,0:T(8,128)(2,1)S(1)} %shard_map.94), channel_id=1, source_target_pairs={{0,8},{4,20},{8,0},{12,28},{16,24},{20,4},{24,16},{28,12},{1,9},{5... | collective-permute-start | bytes 196616 | tf_op jit(solution)/shard_map/ppermute | solution.py:293
  6.7 3.0 %collective-permute-start.1 = (bf16[1584,128]{1,0:T(8,128)(2,1)S(1)}, bf16[1584,128]{1,0:T(8,128)(2,1)S(1)}, u32[]{:S(2)}, u32[]{:S(2)}) collective-permute-start(bf16[1584,128]{1,0:T(8,128)(2,1)S(1)} %get-tuple-element.30.packet_ref), channel_id=1, source_target_pairs={{0,4},{4,0},{1,5},{5,1},{2,6},{6,2},{3,7},{7,3},{8,12},{12,8},{9,1... | collective-permute-start | bytes 1216520 | tf_op jit(solution)/shard_map/ppermute | solution.py:285
  6.7 5.1 %collective-permute-start.2 = (bf16[2,2,128,128]{3,2,1,0:T(8,128)(2,1)S(1)}, bf16[2,2,128,128]{3,2,1,0:T(8,128)(2,1)S(1)}, u32[]{:S(2)}, u32[]{:S(2)}) collective-permute-start(bf16[2,2,128,128]{3,2,1,0:T(8,128)(2,1)S(1)} %constant_dynamic-update-slice_fusion.blocks_ref), channel_id=1, source_target_pairs={{0,16},{4,12},{8,24},{12,4},{16,0},{20,28},{24,8},{28,20},{1,17},{... | collective-permute-start | bytes 393224 | tf_op jit(solution)/shard_map/ppermute | solution.py:293
  13.5 7.2 %collective-permute-start.3 = (bf16[128,768]{1,0:T(8,128)(2,1)S(1)}, bf16[128,768]{1,0:T(8,128)(2,1)S(1)}, u32[]{:S(2)}, u32[]{:S(2)}) collective-permute-start(bf16[128,768]{1,0:T(8,128)(2,1)S(1)} %get-tuple-element.39), channel_id=1, source_target_pairs={{0,4},{4,0},{1,5},{5,1},{2,6},{6,2},{3,7},{7,3},{8,12},{12,8},{9,1... | collective-permute-start | bytes 589832 | tf_op jit(solution)/shard_map/ppermute | solution.py:285
  13.6 5.0 %collective-permute-start.4 = (bf16[2,2,128,128]{3,2,1,0:T(8,128)(2,1)S(1)}, bf16[2,2,128,128]{3,2,1,0:T(8,128)(2,1)S(1)}, u32[]{:S(2)}, u32[]{:S(2)}) collective-permute-start(bf16[2,2,128,128]{3,2,1,0:T(8,128)(2,1)S(1)} %get-tuple-element.42), channel_id=1, source_target_pairs={{0,16},{4,12},{8,24},{12,4},{16,0},{20,28},{24,8},{28,20},{1,17},{... | collective-permute-start | bytes 393224 | tf_op jit(solution)/shard_map/ppermute | solution.py:293
  18.7 4.3 %collective-permute-start.5 = (bf16[1,2,128,128]{3,2,1,0:T(8,128)(2,1)S(1)}, bf16[1,2,128,128]{3,2,1,0:T(8,128)(2,1)S(1)}, u32[]{:S(2)}, u32[]{:S(2)}) collective-permute-start(bf16[1,2,128,128]{3,2,1,0:T(8,128)(2,1)S(1)} %shard_map.100), channel_id=1, source_target_pairs={{0,8},{4,20},{8,0},{12,28},{16,24},{20,4},{24,16},{28,12},{1,9},{5... | collective-permute-start | bytes 196616 | tf_op jit(solution)/shard_map/ppermute | solution.py:293

commit v3 on v2

v3 whole, which is shorter than its diff:
```python
import functools
import math

import jax
import jax.numpy as jnp
from jax import lax
from jax.experimental import pallas as pl
from jax.experimental.pallas import tpu as pltpu
from jax.sharding import PartitionSpec as P

LOG2E = math.log2(math.e)
STAT_ROWS = 16
SPLIT = 3


def contract(lhs, rhs, lhs_dim, rhs_dim):
    return lax.dot_general(
        lhs, rhs, (((lhs_dim,), (rhs_dim,)), ((), ())), preferred_element_type=jnp.float32
    )


def packet_rows(sizes):
    group_size, row_count, _ = sizes
    return 2 * group_size * row_count + SPLIT * STAT_ROWS


def load_kernel(
    sizes, inner_count, query_hbm, grad_hbm, out_hbm, norm_hbm, order_hbm, key_hbm, value_hbm,
    pair_ref, packet_ref, rank_ref, out_ref, norm_ref, stat_ref, order_ref, sems,
):
    group_size, row_count, _ = sizes
    half = group_size * row_count
    copies = [
        pltpu.make_async_copy(source, target, sems.at[at])
        for at, (source, target) in enumerate(
            [
                (order_hbm, order_ref),
                (norm_hbm, norm_ref),
                (grad_hbm, packet_ref.at[pl.ds(half, half)]),
                (out_hbm, out_ref),
                (key_hbm, pair_ref.at[0]),
                (value_hbm, pair_ref.at[1]),
                (query_hbm, packet_ref.at[pl.ds(0, half)]),
            ]
        )
    ]
    for copy in copies:
        copy.start()
    stat_ref[...] = jnp.zeros_like(stat_ref)
    copies[0].wait()
    my_index = lax.axis_index("inner")
    for step in range(inner_count):
        rank_ref[step : step + 1, :] = jnp.full((1, row_count), order_ref[my_index ^ step], jnp.int32)
    for copy in copies[1:4]:
        copy.wait()
    stat_ref[:group_size] = norm_ref[...]
    for head in range(group_size):
        rows = slice(head * row_count, (head + 1) * row_count)
        grads = packet_ref[half + head * row_count : half + (head + 1) * row_count, :]
        product = grads.astype(jnp.float32) * out_ref[rows, :].astype(jnp.float32)
        stat_ref[8 + head : 9 + head, :] = jnp.sum(product.T, axis=0, keepdims=True)
    rest = jnp.clip(stat_ref[...], -3.38e38, 3.38e38)
    for term in range(SPLIT):
        piece = rest.astype(jnp.bfloat16)
        start = 2 * half + term * STAT_ROWS
        packet_ref[start : start + STAT_ROWS, :] = piece
        rest = rest - piece.astype(jnp.float32)
    for copy in copies[4:]:
        copy.wait()


def packet_stats(packet_ref, sizes):
    group_size, row_count, _ = sizes
    start = 2 * group_size * row_count
    pieces = [
        packet_ref[start + term * STAT_ROWS : start + (term + 1) * STAT_ROWS, :].astype(jnp.float32)
        for term in range(SPLIT)
    ]
    stats = pieces[0] + (pieces[1] + pieces[2])
    return stats[:8] * LOG2E, stats[8:]


def block_terms(keys, values, visible, packet_ref, scores_ref, sizes):
    group_size, row_count, head_size = sizes
    half = group_size * row_count
    scale = LOG2E / math.sqrt(head_size)
    per_step = 2 if group_size % 2 == 0 else 1
    all_norms, all_dots = packet_stats(packet_ref, sizes)
    key_total = jnp.zeros((keys.shape[0], head_size), jnp.float32)
    value_total = jnp.zeros((keys.shape[0], head_size), jnp.float32)
    for first in range(0, group_size, per_step):
        start, stop = first * row_count, (first + per_step) * row_count
        queries = packet_ref[start:stop, :]
        grads = packet_ref[half + start : half + stop, :]
        scores = contract(keys, queries, 1, 1)
        grad_weights = contract(values, grads, 1, 1)
        weights_parts = []
        score_parts = []
        for at in range(per_step):
            head = first + at
            lanes = slice(at * row_count, (at + 1) * row_count)
            weights = jnp.exp2(scores[:, lanes] * scale - all_norms[head : head + 1, :])
            if visible is not None:
                weights = jnp.where(visible, weights, 0.0)
            weights_parts.append(weights.astype(jnp.bfloat16))
            score_parts.append(
                (weights * (grad_weights[:, lanes] - all_dots[head : head + 1, :])).astype(jnp.bfloat16)
            )
        weights_half = jnp.concatenate(weights_parts, axis=1)
        grad_scores = jnp.concatenate(score_parts, axis=1)
        scores_ref[:, start:stop] = grad_scores
        value_total += contract(weights_half, grads, 1, 0)
        key_total += contract(grad_scores, queries, 1, 0)
    return key_total, value_total


def visible_rows(rank_ref, steps, inner_count, row_count):
    span_rows = row_count // 2
    key_rows = lax.broadcasted_iota(jnp.int32, (row_count, row_count), 0)
    my_rows = lax.broadcasted_iota(jnp.int32, (row_count, row_count), 1)

    def positions(rank, rows):
        return jnp.where(
            rows < span_rows,
            rank * span_rows + rows,
            (2 * inner_count - 2 - rank) * span_rows + rows,
        )

    mine = positions(rank_ref[0:1, :], my_rows)
    return jnp.concatenate(
        [positions(rank_ref[step : step + 1, :], key_rows) <= mine for step in steps], axis=0
    )


def stacked(blocks, which):
    return jnp.concatenate([ref[which] for ref in blocks], axis=0)


def key_kernel(sizes, inner_count, outer_count, steps, packet_ref, next_ref, rank_ref, *refs):
    count = len(steps)
    _, row_count, _ = sizes
    blocks, (scores_ref, next_scores_ref, total_ref) = refs[:count], refs[count:]
    has_next = lax.axis_index("outer") < outer_count - 1
    keys, values = stacked(blocks, 0), stacked(blocks, 1)
    visible = visible_rows(rank_ref, steps, inner_count, row_count)
    key_terms, value_terms = block_terms(keys, values, visible, packet_ref, scores_ref, sizes)
    total_ref[0] = key_terms
    total_ref[1] = value_terms

    @pl.when(has_next)
    def _():
        key_terms, value_terms = block_terms(keys, values, None, next_ref, next_scores_ref, sizes)
        total_ref[0] += key_terms
        total_ref[1] += value_terms


def far_kernel(sizes, inner_count, outer_count, steps, packet_ref, next_ref, rank_ref, *refs):
    count = len(steps)
    _, row_count, head_size = sizes
    inv_root = 1.0 / math.sqrt(head_size)
    blocks, score_refs, sums, total_ref = refs[:count], refs[count : count + 2], refs[count + 2 : -1], refs[-1]
    key_kernel(
        sizes, inner_count, outer_count, steps, packet_ref, next_ref, rank_ref, *blocks, *score_refs, total_ref
    )
    for at, ref in enumerate(sums):
        rows = slice(at * row_count, (at + 1) * row_count)
        ref[0] = (total_ref[0, rows, :] * inv_root).astype(jnp.bfloat16)
        ref[1] = total_ref[1, rows, :].astype(jnp.bfloat16)


def query_terms(refs, lanes):
    scores = jnp.concatenate([refs[0][:, lanes], refs[1][:, lanes]], axis=0)
    return contract(stacked(refs[2:], 0), scores, 0, 0)


def back_kernel(sizes, outer_count, *refs):
    group_size, row_count, _ = sizes
    has_next = lax.axis_index("outer") < outer_count - 1

    @pl.when(has_next)
    def _():
        refs[-1][...] = query_terms(refs[:-1], slice(None)).astype(jnp.bfloat16)


def query_kernel(sizes, *refs):
    group_size, row_count, head_size = sizes
    inv_root = 1.0 / math.sqrt(head_size)
    back_ref, inputs = refs[0], refs[1:-4]
    result_hbm, total_ref, result_ref, sem = refs[-4:]
    has_prev = lax.axis_index("outer") > 0
    total_ref[...] = query_terms(inputs, slice(None))

    @pl.when(has_prev)
    def _():
        total_ref[...] += back_ref[...].astype(jnp.float32)

    for head in range(group_size):
        rows = slice(head * row_count, (head + 1) * row_count)
        result_ref[rows, :] = (total_ref[:, rows] * inv_root).T.astype(jnp.bfloat16)
    copy = pltpu.make_async_copy(result_ref, result_hbm, sem)
    copy.start()
    copy.wait()


def sum_kernel(sizes, *refs):
    _, _, head_size = sizes
    inv_root = 1.0 / math.sqrt(head_size)
    own_ref, returned = refs[0], refs[1:-5]
    key_hbm, value_hbm, key_ref, value_ref, sems = refs[-5:]
    key_total = own_ref[0] * inv_root
    value_total = own_ref[1]
    for ref in returned:
        key_total += ref[0].astype(jnp.float32)
        value_total += ref[1].astype(jnp.float32)
    key_ref[...] = key_total.astype(jnp.bfloat16)
    value_ref[...] = value_total.astype(jnp.bfloat16)
    copies = [
        pltpu.make_async_copy(key_ref, key_hbm, sems.at[0]),
        pltpu.make_async_copy(value_ref, value_hbm, sems.at[1]),
    ]
    for copy in copies:
        copy.start()
    for copy in copies:
        copy.wait()


def on_device(queries, key_rows, value_rows, attn_out, grad_out, log_norms, pair_order):
    row_count, group_size, head_size = queries.shape
    inner_count = lax.axis_size("inner")
    outer_count = lax.axis_size("outer")
    assert inner_count & (inner_count - 1) == 0 and inner_count > 1
    sizes = (group_size, row_count, head_size)
    half = group_size * row_count
    away = list(range(inner_count - 1, 0, -1))

    def flat(array):
        return jnp.swapaxes(array, 0, 1).reshape(-1, head_size)

    def in_hbm(array):
        return pltpu.with_memory_space_constraint(array, pltpu.HBM)

    def to_segment(block, ahead):
        route = [(at, (at + ahead) % outer_count) for at in range(outer_count)]
        return lax.ppermute(block, "outer", route)

    def exchange(block, step):
        return lax.ppermute(block, "inner", [(at, at ^ step) for at in range(inner_count)])

    vmem = pl.BlockSpec(memory_space=pltpu.VMEM)
    hbm = pl.BlockSpec(memory_space=pltpu.HBM)
    roomy = pltpu.CompilerParams(vmem_limit_bytes=32 * 2**20)

    def shape(dims, dtype):
        return jax.ShapeDtypeStruct(dims, dtype)

    def cost(blocks, data=2**20):
        each = group_size * row_count * row_count
        return pl.CostEstimate(
            flops=10 * blocks * each * head_size, bytes_accessed=data, transcendentals=blocks * each
        )

    block_shape = shape((2, row_count, head_size), jnp.bfloat16)

    pair, packet, rank = pl.pallas_call(
        functools.partial(load_kernel, sizes, inner_count),
        out_shape=(
            block_shape,
            shape((packet_rows(sizes), head_size), jnp.bfloat16),
            shape((max(8, inner_count), row_count), jnp.int32),
        ),
        in_specs=[hbm] * 7,
        out_specs=(vmem,) * 3,
        scratch_shapes=[
            pltpu.VMEM((half, head_size), jnp.bfloat16),
            pltpu.VMEM((group_size, row_count), jnp.float32),
            pltpu.VMEM((STAT_ROWS, row_count), jnp.float32),
            pltpu.SMEM((inner_count,), jnp.int32),
            pltpu.SemaphoreType.DMA((7,)),
        ],
        cost_estimate=cost(0),
        compiler_params=roomy,
    )(
        *(
            in_hbm(array)
            for array in (
                flat(queries), flat(grad_out), flat(attn_out), log_norms, pair_order,
                flat(key_rows), flat(value_rows),
            )
        )
    )
    next_packet = to_segment(packet, -1)
    blocks = {0: pair}
    for step in reversed(away):
        blocks[step] = exchange(pair, step)

    all_blocks = [blocks[step] for step in [0] + away]

    def scores_shape(count):
        return shape((count * row_count, half), jnp.bfloat16)

    near_scores, near_next_scores, own_total = pl.pallas_call(
        functools.partial(key_kernel, sizes, inner_count, outer_count, [0]),
        out_shape=(scores_shape(1), scores_shape(1), shape((2, row_count, head_size), jnp.float32)),
        in_specs=[vmem] * 4,
        out_specs=(vmem,) * 3,
        cost_estimate=cost(2),
        compiler_params=roomy,
    )(packet, next_packet, rank, pair)

    far_scores, far_next_scores, *sums = pl.pallas_call(
        functools.partial(far_kernel, sizes, inner_count, outer_count, away),
        out_shape=(scores_shape(len(away)),) * 2 + (block_shape,) * len(away),
        in_specs=[vmem] * (3 + len(away)),
        out_specs=(vmem,) * (2 + len(away)),
        scratch_shapes=[pltpu.VMEM((2, len(away) * row_count, head_size), jnp.float32)],
        cost_estimate=cost(2 * len(away)),
        compiler_params=roomy,
    )(packet, next_packet, rank, *all_blocks[1:])
    returned = [exchange(terms, step) for terms, step in zip(sums, away)]

    query_next = pl.pallas_call(
        functools.partial(back_kernel, sizes, outer_count),
        out_shape=shape((head_size, half), jnp.bfloat16),
        in_specs=[vmem] * (2 + inner_count),
        out_specs=vmem,
        cost_estimate=cost(inner_count),
        compiler_params=roomy,
    )(near_next_scores, far_next_scores, *all_blocks)
    query_back = to_segment(query_next, 1)

    query_out = pl.pallas_call(
        functools.partial(query_kernel, sizes),
        out_shape=shape((half, head_size), jnp.bfloat16),
        in_specs=[vmem] * (3 + inner_count),
        out_specs=hbm,
        scratch_shapes=[
            pltpu.VMEM((head_size, half), jnp.float32),
            pltpu.VMEM((half, head_size), jnp.bfloat16),
            pltpu.SemaphoreType.DMA,
        ],
        cost_estimate=cost(inner_count),
        compiler_params=roomy,
    )(query_back, near_scores, far_scores, *all_blocks)

    own_total, query_out = lax.optimization_barrier((own_total, query_out))
    key_out, value_out = pl.pallas_call(
        functools.partial(sum_kernel, sizes),
        out_shape=(shape((row_count, head_size), jnp.bfloat16),) * 2,
        in_specs=[vmem] * (1 + len(returned)),
        out_specs=(hbm, hbm),
        scratch_shapes=[
            pltpu.VMEM((row_count, head_size), jnp.bfloat16),
            pltpu.VMEM((row_count, head_size), jnp.bfloat16),
            pltpu.SemaphoreType.DMA((2,)),
        ],
        compiler_params=roomy,
    )(own_total, *returned)
    grad_queries = jnp.swapaxes(query_out.reshape(group_size, row_count, head_size), 0, 1)
    return (grad_queries, key_out[:, None, :], value_out[:, None, :])


def solution(mesh):
    in_specs = (
        P(("outer", "inner"), "head", None),
        P(("outer", "inner"), "head", None),
        P(("outer", "inner"), "head", None),
        P(("outer", "inner"), "head", None),
        P(("outer", "inner"), "head", None),
        P("head", ("outer", "inner")),
        P(),
    )
    out_specs = (
        P(("outer", "inner"), "head", None),
        P(("outer", "inner"), "head", None),
        P(("outer", "inner"), "head", None),
    )
    return jax.shard_map(
        on_device, mesh=mesh, in_specs=in_specs, out_specs=out_specs, check_vma=False
    )
```

time: 23.9 us -> 21.1 us (0.88)
  starting transfers between devices: 9.34 us -> 8.25 us
  waiting for transfers between devices: 6.51 us -> 5.6 us
  Pallas kernels: 7.09 us -> 6.37 us
    ppermute x4 -> x6, starting transfers between devices: 9.26 us -> 7.66 us  [exchange(): lax.ppermute(block, 'inner', [(at, at ^ step) for at in range(inner_count)])]
    pallas_call x5 -> x3, Pallas kernels: 3.84 us -> 2.79 us  [the longest x1 1.3 us: on_device(): pl.pallas_call(functools.partial(load_kernel, sizes, inner_count), out_sh...]
    ppermute x4 -> x6, waiting for transfers between devices: 6.51 us -> 5.6 us  [exchange(): lax.ppermute(block, 'inner', [(at, at ^ step) for at in range(inner_count)])]
    ppermute x2, starting transfers between devices: 0.07 us -> 0.59 us  [to_segment(): return lax.ppermute(block, 'outer', route)]
    pallas_call x1, Pallas kernels: 0.85 us -> 1.13 us  [on_device(): pl.pallas_call(functools.partial(query_kernel, sizes), out_shape=shape((h...]
  transfers between devices with their start and end apart: 6 -> 8, of which waited for: 4 -> 5; matrix products, arithmetic and copies ran while one was open for 0% -> 0% of each run, Pallas kernels for 16% -> 11%
where the time goes in v3:
time: 21.1 us; the launch traced here: 20.9 us
  starting transfers between devices  8.25 us (39%)
  Pallas kernels  6.37 us (30%)
  waiting for transfers between devices  5.6 us (27%)
  between operations  0.7 us (3%)
    ppermute x6, starting transfers between devices, exchange(): lax.ppermute(block, 'inner', [(at, at ^ step) for at in range(inner_count)])  7.66 us
    ppermute x6, waiting for transfers between devices, exchange(): lax.ppermute(block, 'inner', [(at, at ^ step) for at in range(inner_count)])  5.6 us
    pallas_call x1, Pallas kernels, on_device(): pl.pallas_call(functools.partial(far_kernel, sizes, inner_count, outer_co...  1.78 us
    pallas_call x1, Pallas kernels, on_device(): pl.pallas_call(functools.partial(load_kernel, sizes, inner_count), out_sh...  1.3 us
    pallas_call x1, Pallas kernels, on_device(): pl.pallas_call(functools.partial(key_kernel, sizes, inner_count, outer_co...  1.16 us
    pallas_call x1, Pallas kernels, on_device(): pl.pallas_call(functools.partial(query_kernel, sizes), out_shape=shape((h...  1.13 us
    pallas_call x1, Pallas kernels, on_device(): pl.pallas_call(functools.partial(sum_kernel, sizes), out_shape=(shape((ro...  0.67 us
    ppermute x2, starting transfers between devices, to_segment(): return lax.ppermute(block, 'outer', route)  0.59 us
  transfers between devices with their start and end apart: 8, of which 5 were waited for; matrix products, arithmetic and copies ran while one was open for 0% of the time, Pallas kernels for 11%

profile of v3, /device:TPU:0, one launch (start us, length us, event | category | flops | bytes accessed | tf_op | source)
XLA Modules:
  0.0 20.9 jit_solution(7099276258580452715)
XLA Ops:
  0.6 1.3 %shard_map.94 = (bf16[2,128,128]{2,1,0:T(8,128)(2,1)S(1)}, bf16[1584,128]{1,0:T(8,128)(2,1)S(1)}, s32[8,128]{1,0:T(8,128)S(1)}) custom-call(bf16[768,128]{1,0:T(8,128)(2,1)} %bitcast.16, bf16[768,128]{1,0:T(8,128)(2,1)} %bitcast.17, bf16[768,128]{1,0:T(8,128)(2,1)} %bitcast.18, f32[6,128]{1,0:T(8,128)} %norm_hbm.1, s32[4]{0:T(128)} %order_hbm.1, ...), custom_call_target="tpu_custom_call" | custom-call | bytes 1048576 | tf_op jit(solution)/shard_map/pallas_call | solution.py:264
  1.9 0.5 %collective-permute-start = (bf16[1584,128]{1,0:T(8,128)(2,1)S(1)}, bf16[1584,128]{1,0:T(8,128)(2,1)S(1)}, u32[]{:S(2)}, u32[]{:S(2)}) collective-permute-start(bf16[1584,128]{1,0:T(8,128)(2,1)S(1)} %get-tuple-element.18.packet_ref), channel_id=1, source_target_pairs={{0,4},{4,0},{1,5},{5,1},{2,6},{6,2},{3,7},{7,3},{8,12},{12,8},{9,1... | collective-permute-start | bytes 1216520 | tf_op jit(solution)/shard_map/ppermute | solution.py:244
  2.5 2.6 %collective-permute-start.3 = (bf16[2,128,128]{2,1,0:T(8,128)(2,1)S(1)}, bf16[2,128,128]{2,1,0:T(8,128)(2,1)S(1)}, u32[]{:S(2)}, u32[]{:S(2)}) collective-permute-start(bf16[2,128,128]{2,1,0:T(8,128)(2,1)S(1)} %get-tuple-element.20.refs_0_.refs_2_.refs_3_), channel_id=1, source_target_pairs={{0,8},{8,0},{16,24},{24,16},{1,9},{9,1},{17,25},{25,17},{2,10},{10... | collective-permute-start | bytes 196616 | tf_op jit(solution)/shard_map/ppermute | solution.py:247
  5.0 1.5 %collective-permute-start.2 = (bf16[2,128,128]{2,1,0:T(8,128)(2,1)S(1)}, bf16[2,128,128]{2,1,0:T(8,128)(2,1)S(1)}, u32[]{:S(2)}, u32[]{:S(2)}) collective-permute-start(bf16[2,128,128]{2,1,0:T(8,128)(2,1)S(1)} %get-tuple-element.20.refs_0_.refs_2_.refs_3_), channel_id=1, source_target_pairs={{0,16},{8,24},{16,0},{24,8},{1,17},{9,25},{17,1},{25,9},{2,18},{10... | collective-permute-start | bytes 196616 | tf_op jit(solution)/shard_map/ppermute | solution.py:247
  6.5 0.0 collective-permute-start.1
  6.6 0.0 collective-permute-done.next_ref
  6.6 1.2 %shard_map.95 = (bf16[128,768]{1,0:T(8,128)(2,1)S(1)}, bf16[128,768]{1,0:T(8,128)(2,1)S(1)}, f32[2,128,128]{2,1,0:T(8,128)S(1)}) custom-call(bf16[1584,128]{1,0:T(8,128)(2,1)S(1)} %get-tuple-element.18.packet_ref, bf16[1584,128]{1,0:T(8,128)(2,1)S(1)} %collective-permute-done.next_ref, s32[8,128]{1,0:T(8,128)S(1)} %get-tuple-element.19.rank_ref, ...), custom_call_target="tpu_custom_call" | custom-call | flops 251658240 | bytes 1048576 | tf_op jit(solution)/shard_map/pallas_call | solution.py:301
  7.7 0.0 collective-permute-done.3.refs_2_.refs_5_.refs_6_
  7.8 1.5 %collective-permute-done.2.refs_1_.refs_4_.refs_5_ = bf16[2,128,128]{2,1,0:T(8,128)(2,1)S(1)} collective-permute-done((bf16[2,128,128]{2,1,0:T(8,128)(2,1)S(1)}, bf16[2,128,128]{2,1,0:T(8,128)(2,1)S(1)}, u32[]{:S(2)}, u32[]{:S(2)}) %collective-permute-start.2) | collective-permute-done | bytes 65568 | tf_op jit(solution)/shard_map/ppermute | solution.py:247
  9.3 2.4 %collective-permute-done.1.refs_0_.refs_3_.refs_4_ = bf16[2,128,128]{2,1,0:T(8,128)(2,1)S(1)} collective-permute-done((bf16[2,128,128]{2,1,0:T(8,128)(2,1)S(1)}, bf16[2,128,128]{2,1,0:T(8,128)(2,1)S(1)}, u32[]{:S(2)}, u32[]{:S(2)}) %collective-permute-start.1) | collective-permute-done | bytes 65568 | tf_op jit(solution)/shard_map/ppermute | solution.py:247
  11.7 1.8 %shard_map.96 = (bf16[384,768]{1,0:T(8,128)(2,1)S(1)}, bf16[384,768]{1,0:T(8,128)(2,1)S(1)}, bf16[2,128,128]{2,1,0:T(8,128)(2,1)S(1)}, bf16[2,128,128]{2,1,0:T(8,128)(2,1)S(1)}, bf16[2,128,128]{2,1,0:T(8,128)(2,1)S(1)}) custom-call(bf16[1584,128]{1,0:T(8,128)(2,1)S(1)} %get-tuple-element.18.packet_ref, bf16[1584,128]{1,0:T(8,128)(2,1)S(1)} %collective-permute-done.next_ref, ...), custom_call_target="tpu_custom_call" | custom-call | flops 754974720 | bytes 1048576 | tf_op jit(solution)/shard_map/pallas_call | solution.py:310
  13.5 0.3 %shard_map.97 = bf16[128,768]{1,0:T(8,128)(2,1)S(1)} custom-call(bf16[128,768]{1,0:T(8,128)(2,1)S(1)} %get-tuple-element.22.refs_0_, bf16[384,768]{1,0:T(8,128)(2,1)S(1)} %get-tuple-element.23.refs_1_, bf16[2,128,128]{2,1,0:T(8,128)(2,1)S(1)} %get-tuple-element.20.refs_0_.refs_2_.refs_3_, ...), custom_call_target="tpu_custom_call" | custom-call | flops 503316480 | bytes 1048576 | tf_op jit(solution)/shard_map/pallas_call | solution.py:321
  13.8 0.1 collective-permute-start.4
  13.9 0.5 %collective-permute-start.5 = (bf16[2,128,128]{2,1,0:T(8,128)(2,1)S(1)}, bf16[2,128,128]{2,1,0:T(8,128)(2,1)S(1)}, u32[]{:S(2)}, u32[]{:S(2)}) collective-permute-start(bf16[2,128,128]{2,1,0:T(8,128)(2,1)S(1)} %get-tuple-element.28), channel_id=1, source_target_pairs={{0,24},{8,16},{16,8},{24,0},{1,25},{9,17},{17,9},{25,1},{2,26},{10... | collective-permute-start | bytes 196616 | tf_op jit(solution)/shard_map/ppermute | solution.py:247
  14.5 1.5 %collective-permute-start.6 = (bf16[2,128,128]{2,1,0:T(8,128)(2,1)S(1)}, bf16[2,128,128]{2,1,0:T(8,128)(2,1)S(1)}, u32[]{:S(2)}, u32[]{:S(2)}) collective-permute-start(bf16[2,128,128]{2,1,0:T(8,128)(2,1)S(1)} %get-tuple-element.29), channel_id=1, source_target_pairs={{0,16},{8,24},{16,0},{24,8},{1,17},{9,25},{17,1},{25,9},{2,18},{10... | collective-permute-start | bytes 196616 | tf_op jit(solution)/shard_map/ppermute | solution.py:247
  16.0 1.5 %collective-permute-start.7 = (bf16[2,128,128]{2,1,0:T(8,128)(2,1)S(1)}, bf16[2,128,128]{2,1,0:T(8,128)(2,1)S(1)}, u32[]{:S(2)}, u32[]{:S(2)}) collective-permute-start(bf16[2,128,128]{2,1,0:T(8,128)(2,1)S(1)} %get-tuple-element.30), channel_id=1, source_target_pairs={{0,8},{8,0},{16,24},{24,16},{1,9},{9,1},{17,25},{25,17},{2,10},{10... | collective-permute-start | bytes 196616 | tf_op jit(solution)/shard_map/ppermute | solution.py:247
  17.5 0.0 collective-permute-done.4.refs_0_
  17.5 1.1 %shard_map.98 = bf16[768,128]{1,0:T(8,128)(2,1)} custom-call(bf16[128,768]{1,0:T(8,128)(2,1)S(1)} %collective-permute-done.4.refs_0_, bf16[128,768]{1,0:T(8,128)(2,1)S(1)} %get-tuple-element.24.refs_1_, bf16[384,768]{1,0:T(8,128)(2,1)S(1)} %get-tuple-element.25.refs_2_, bf16[2,128,128]{2,1,0:T(8,128)(2,1)S(1)} %get-tuple-element.20.refs_0_.refs_2_.refs_3_, ...), custom_call_target="tpu_custom_call" | custom-call | flops 503316480 | bytes 1048576 | tf_op jit(solution)/shard_map/pallas_call | solution.py:331
  18.6 1.2 %collective-permute-done.5.refs_1_ = bf16[2,128,128]{2,1,0:T(8,128)(2,1)S(1)} collective-permute-done((bf16[2,128,128]{2,1,0:T(8,128)(2,1)S(1)}, bf16[2,128,128]{2,1,0:T(8,128)(2,1)S(1)}, u32[]{:S(2)}, u32[]{:S(2)}) %collective-permute-start.5) | collective-permute-done | bytes 65568 | tf_op jit(solution)/shard_map/ppermute | solution.py:247
  19.8 0.3 %collective-permute-done.6.refs_2_ = bf16[2,128,128]{2,1,0:T(8,128)(2,1)S(1)} collective-permute-done((bf16[2,128,128]{2,1,0:T(8,128)(2,1)S(1)}, bf16[2,128,128]{2,1,0:T(8,128)(2,1)S(1)}, u32[]{:S(2)}, u32[]{:S(2)}) %collective-permute-start.6) | collective-permute-done | bytes 65568 | tf_op jit(solution)/shard_map/ppermute | solution.py:247
  20.0 0.2 %collective-permute-done.7.refs_3_ = bf16[2,128,128]{2,1,0:T(8,128)(2,1)S(1)} collective-permute-done((bf16[2,128,128]{2,1,0:T(8,128)(2,1)S(1)}, bf16[2,128,128]{2,1,0:T(8,128)(2,1)S(1)}, u32[]{:S(2)}, u32[]{:S(2)}) %collective-permute-start.7) | collective-permute-done | bytes 65568 | tf_op jit(solution)/shard_map/ppermute | solution.py:247
  20.2 0.7 %shard_map.99 = (bf16[128,128]{1,0:T(8,128)(2,1)}, bf16[128,128]{1,0:T(8,128)(2,1)}) custom-call(f32[2,128,128]{2,1,0:T(8,128)S(1)} %get-tuple-element.27.refs_0_, bf16[2,128,128]{2,1,0:T(8,128)(2,1)S(1)} %collective-permute-done.5.refs_1_, bf16[2,128,128]{2,1,0:T(8,128)(2,1)S(1)} %collective-permute-done.6.refs_2_, ...), custom_call_target="tpu_custom_call" | custom-call | tf_op jit(solution)/shard_map/pallas_call | solution.py:346
Async XLA Ops:
  1.9 4.6 %collective-permute-start = (bf16[1584,128]{1,0:T(8,128)(2,1)S(1)}, bf16[1584,128]{1,0:T(8,128)(2,1)S(1)}, u32[]{:S(2)}, u32[]{:S(2)}) collective-permute-start(bf16[1584,128]{1,0:T(8,128)(2,1)S(1)} %get-tuple-element.18.packet_ref), channel_id=1, source_target_pairs={{0,4},{4,0},{1,5},{5,1},{2,6},{6,2},{3,7},{7,3},{8,12},{12,8},{9,1... | collective-permute-start | bytes 1216520 | tf_op jit(solution)/shard_map/ppermute | solution.py:244
  2.5 5.3 %collective-permute-start.3 = (bf16[2,128,128]{2,1,0:T(8,128)(2,1)S(1)}, bf16[2,128,128]{2,1,0:T(8,128)(2,1)S(1)}, u32[]{:S(2)}, u32[]{:S(2)}) collective-permute-start(bf16[2,128,128]{2,1,0:T(8,128)(2,1)S(1)} %get-tuple-element.20.refs_0_.refs_2_.refs_3_), channel_id=1, source_target_pairs={{0,8},{8,0},{16,24},{24,16},{1,9},{9,1},{17,25},{25,17},{2,10},{10... | collective-permute-start | bytes 196616 | tf_op jit(solution)/shard_map/ppermute | solution.py:247
  5.0 4.3 %collective-permute-start.2 = (bf16[2,128,128]{2,1,0:T(8,128)(2,1)S(1)}, bf16[2,128,128]{2,1,0:T(8,128)(2,1)S(1)}, u32[]{:S(2)}, u32[]{:S(2)}) collective-permute-start(bf16[2,128,128]{2,1,0:T(8,128)(2,1)S(1)} %get-tuple-element.20.refs_0_.refs_2_.refs_3_), channel_id=1, source_target_pairs={{0,16},{8,24},{16,0},{24,8},{1,17},{9,25},{17,1},{25,9},{2,18},{10... | collective-permute-start | bytes 196616 | tf_op jit(solution)/shard_map/ppermute | solution.py:247
  6.5 5.2 %collective-permute-start.1 = (bf16[2,128,128]{2,1,0:T(8,128)(2,1)S(1)}, bf16[2,128,128]{2,1,0:T(8,128)(2,1)S(1)}, u32[]{:S(2)}, u32[]{:S(2)}) collective-permute-start(bf16[2,128,128]{2,1,0:T(8,128)(2,1)S(1)} %get-tuple-element.20.refs_0_.refs_2_.refs_3_), channel_id=1, source_target_pairs={{0,24},{8,16},{16,8},{24,0},{1,25},{9,17},{17,9},{25,1},{2,26},{10... | collective-permute-start | bytes 196616 | tf_op jit(solution)/shard_map/ppermute | solution.py:247
  13.8 3.6 %collective-permute-start.4 = (bf16[128,768]{1,0:T(8,128)(2,1)S(1)}, bf16[128,768]{1,0:T(8,128)(2,1)S(1)}, u32[]{:S(2)}, u32[]{:S(2)}) collective-permute-start(bf16[128,768]{1,0:T(8,128)(2,1)S(1)} %shard_map.97), channel_id=1, source_target_pairs={{0,4},{4,0},{1,5},{5,1},{2,6},{6,2},{3,7},{7,3},{8,12},{12,8},{9,1... | collective-permute-start | bytes 589832 | tf_op jit(solution)/shard_map/ppermute | solution.py:244
  13.9 5.9 %collective-permute-start.5 = (bf16[2,128,128]{2,1,0:T(8,128)(2,1)S(1)}, bf16[2,128,128]{2,1,0:T(8,128)(2,1)S(1)}, u32[]{:S(2)}, u32[]{:S(2)}) collective-permute-start(bf16[2,128,128]{2,1,0:T(8,128)(2,1)S(1)} %get-tuple-element.28), channel_id=1, source_target_pairs={{0,24},{8,16},{16,8},{24,0},{1,25},{9,17},{17,9},{25,1},{2,26},{10... | collective-permute-start | bytes 196616 | tf_op jit(solution)/shard_map/ppermute | solution.py:247
  14.5 5.6 %collective-permute-start.6 = (bf16[2,128,128]{2,1,0:T(8,128)(2,1)S(1)}, bf16[2,128,128]{2,1,0:T(8,128)(2,1)S(1)}, u32[]{:S(2)}, u32[]{:S(2)}) collective-permute-start(bf16[2,128,128]{2,1,0:T(8,128)(2,1)S(1)} %get-tuple-element.29), channel_id=1, source_target_pairs={{0,16},{8,24},{16,0},{24,8},{1,17},{9,25},{17,1},{25,9},{2,18},{10... | collective-permute-start | bytes 196616 | tf_op jit(solution)/shard_map/ppermute | solution.py:247
  16.0 4.3 %collective-permute-start.7 = (bf16[2,128,128]{2,1,0:T(8,128)(2,1)S(1)}, bf16[2,128,128]{2,1,0:T(8,128)(2,1)S(1)}, u32[]{:S(2)}, u32[]{:S(2)}) collective-permute-start(bf16[2,128,128]{2,1,0:T(8,128)(2,1)S(1)} %get-tuple-element.30), channel_id=1, source_target_pairs={{0,8},{8,0},{16,24},{24,16},{1,9},{9,1},{17,25},{25,17},{2,10},{10... | collective-permute-start | bytes 196616 | tf_op jit(solution)/shard_map/ppermute | solution.py:247

commit v4 on v3

--- a/solution.py
+++ b/solution.py
@@ -22,6 +22,12 @@
 def packet_rows(sizes):
     group_size, row_count, _ = sizes
     return 2 * group_size * row_count + SPLIT * STAT_ROWS
+
+
+def peer_offset(step, outer, inner_count):
+    bits = inner_count.bit_length() - 1
+    turn = outer % 2
+    return ((step << turn) | (step >> (bits - turn))) & (inner_count - 1)
 
 
 def load_kernel(
@@ -49,8 +55,10 @@
     stat_ref[...] = jnp.zeros_like(stat_ref)
     copies[0].wait()
     my_index = lax.axis_index("inner")
+    turned = lax.rem(lax.axis_index("outer"), 2) == 1
     for step in range(inner_count):
-        rank_ref[step : step + 1, :] = jnp.full((1, row_count), order_ref[my_index ^ step], jnp.int32)
+        offset = jnp.where(turned, peer_offset(step, 1, inner_count), peer_offset(step, 0, inner_count))
+        rank_ref[step : step + 1, :] = jnp.full((1, row_count), order_ref[my_index ^ offset], jnp.int32)
     for copy in copies[1:4]:
         copy.wait()
     stat_ref[:group_size] = norm_ref[...]
@@ -244,7 +252,12 @@
         return lax.ppermute(block, "outer", route)
 
     def exchange(block, step):
-        return lax.ppermute(block, "inner", [(at, at ^ step) for at in range(inner_count)])
+        route = []
+        for inner in range(inner_count):
+            for outer in range(outer_count):
+                peer = inner ^ peer_offset(step, outer, inner_count)
+                route.append((inner * outer_count + outer, peer * outer_count + outer))
+        return lax.ppermute(block, ("inner", "outer"), route)
 
     vmem = pl.BlockSpec(memory_space=pltpu.VMEM)
     hbm = pl.BlockSpec(memory_space=pltpu.HBM)
@@ -290,10 +303,11 @@
     )
     next_packet = to_segment(packet, -1)
     blocks = {0: pair}
-    for step in reversed(away):
+    for step in away:
         blocks[step] = exchange(pair, step)
 
-    all_blocks = [blocks[step] for step in [0] + away]
+    arrival = away[::-1]
+    all_blocks = [blocks[step] for step in [0] + arrival]
 
     def scores_shape(count):
         return shape((count * row_count, half), jnp.bfloat16)
@@ -308,7 +322,7 @@
     )(packet, next_packet, rank, pair)
 
     far_scores, far_next_scores, *sums = pl.pallas_call(
-        functools.partial(far_kernel, sizes, inner_count, outer_count, away),
+        functools.partial(far_kernel, sizes, inner_count, outer_count, arrival),
         out_shape=(scores_shape(len(away)),) * 2 + (block_shape,) * len(away),
         in_specs=[vmem] * (3 + len(away)),
         out_specs=(vmem,) * (2 + len(away)),
@@ -316,7 +330,7 @@
         cost_estimate=cost(2 * len(away)),
         compiler_params=roomy,
     )(packet, next_packet, rank, *all_blocks[1:])
-    returned = [exchange(terms, step) for terms, step in zip(sums, away)]
+    returned = [exchange(terms, step) for terms, step in zip(sums[::-1], away)]
 
     query_next = pl.pallas_call(
         functools.partial(back_kernel, sizes, outer_count),

time: 21.1 us -> 20.7 us (0.981)
  waiting for transfers between devices: 5.6 us -> 5.16 us
    ppermute x6, waiting for transfers between devices: 5.6 us -> 5.16 us  [exchange(): return lax.ppermute(block, ('inner', 'outer'), route)]
  transfers between devices with their start and end apart: 8 -> 8, of which waited for: 5 -> 6; matrix products, arithmetic and copies ran while one was open for 0% -> 0% of each run, Pallas kernels for 11% -> 11%
where the time goes in v4:
time: 20.7 us; the launch traced here: 20.5 us
  starting transfers between devices  8.3 us (40%)
  Pallas kernels  6.36 us (31%)
  waiting for transfers between devices  5.16 us (25%)
  between operations  0.69 us (3%)
    ppermute x6, starting transfers between devices, exchange(): return lax.ppermute(block, ('inner', 'outer'), route)  7.72 us
    ppermute x6, waiting for transfers between devices, exchange(): return lax.ppermute(block, ('inner', 'outer'), route)  5.16 us
    pallas_call x1, Pallas kernels, on_device(): pl.pallas_call(functools.partial(far_kernel, sizes, inner_count, outer_co...  1.77 us
    pallas_call x1, Pallas kernels, on_device(): pl.pallas_call(functools.partial(load_kernel, sizes, inner_count), out_sh...  1.3 us
    pallas_call x1, Pallas kernels, on_device(): pl.pallas_call(functools.partial(key_kernel, sizes, inner_count, outer_co...  1.16 us
    pallas_call x1, Pallas kernels, on_device(): pl.pallas_call(functools.partial(query_kernel, sizes), out_shape=shape((h...  1.13 us
    pallas_call x1, Pallas kernels, on_device(): pl.pallas_call(functools.partial(sum_kernel, sizes), out_shape=(shape((ro...  0.67 us
    ppermute x2, starting transfers between devices, to_segment(): return lax.ppermute(block, 'outer', route)  0.59 us
  transfers between devices with their start and end apart: 8, of which 6 were waited for; matrix products, arithmetic and copies ran while one was open for 0% of the time, Pallas kernels for 11%

profile of v4, /device:TPU:0, one launch (start us, length us, event | category | flops | bytes accessed | tf_op | source)
XLA Modules:
  0.0 20.5 jit_solution(13759582086701925829)
XLA Ops:
  0.6 1.3 %shard_map.94 = (bf16[2,128,128]{2,1,0:T(8,128)(2,1)S(1)}, bf16[1584,128]{1,0:T(8,128)(2,1)S(1)}, s32[8,128]{1,0:T(8,128)S(1)}) custom-call(bf16[768,128]{1,0:T(8,128)(2,1)} %bitcast.16, bf16[768,128]{1,0:T(8,128)(2,1)} %bitcast.17, bf16[768,128]{1,0:T(8,128)(2,1)} %bitcast.18, f32[6,128]{1,0:T(8,128)} %norm_hbm.1, s32[4]{0:T(128)} %order_hbm.1, ...), custom_call_target="tpu_custom_call" | custom-call | bytes 1048576 | tf_op jit(solution)/shard_map/pallas_call | solution.py:277
  1.9 0.5 %collective-permute-start = (bf16[1584,128]{1,0:T(8,128)(2,1)S(1)}, bf16[1584,128]{1,0:T(8,128)(2,1)S(1)}, u32[]{:S(2)}, u32[]{:S(2)}) collective-permute-start(bf16[1584,128]{1,0:T(8,128)(2,1)S(1)} %get-tuple-element.18.packet_ref), channel_id=1, source_target_pairs={{0,4},{4,0},{1,5},{5,1},{2,6},{6,2},{3,7},{7,3},{8,12},{12,8},{9,1... | collective-permute-start | bytes 1216520 | tf_op jit(solution)/shard_map/ppermute | solution.py:252
  2.5 3.5 %collective-permute-start.3 = (bf16[2,128,128]{2,1,0:T(8,128)(2,1)S(1)}, bf16[2,128,128]{2,1,0:T(8,128)(2,1)S(1)}, u32[]{:S(2)}, u32[]{:S(2)}) collective-permute-start(bf16[2,128,128]{2,1,0:T(8,128)(2,1)S(1)} %get-tuple-element.20.refs_0_.refs_2_.refs_3_), channel_id=1, source_target_pairs={{0,24},{4,28},{8,16},{12,20},{16,8},{20,12},{24,0},{28,4},{1,25},{... | collective-permute-start | bytes 196616 | tf_op jit(solution)/shard_map/ppermute | solution.py:260
  6.0 0.5 %collective-permute-start.2 = (bf16[2,128,128]{2,1,0:T(8,128)(2,1)S(1)}, bf16[2,128,128]{2,1,0:T(8,128)(2,1)S(1)}, u32[]{:S(2)}, u32[]{:S(2)}) collective-permute-start(bf16[2,128,128]{2,1,0:T(8,128)(2,1)S(1)} %get-tuple-element.20.refs_0_.refs_2_.refs_3_), channel_id=1, source_target_pairs={{0,16},{4,12},{8,24},{12,4},{16,0},{20,28},{24,8},{28,20},{1,17},{... | collective-permute-start | bytes 196616 | tf_op jit(solution)/shard_map/ppermute | solution.py:260
  6.5 0.1 collective-permute-start.1
  6.6 0.0 collective-permute-done.next_ref
  6.6 1.2 %shard_map.95 = (bf16[128,768]{1,0:T(8,128)(2,1)S(1)}, bf16[128,768]{1,0:T(8,128)(2,1)S(1)}, f32[2,128,128]{2,1,0:T(8,128)S(1)}) custom-call(bf16[1584,128]{1,0:T(8,128)(2,1)S(1)} %get-tuple-element.18.packet_ref, bf16[1584,128]{1,0:T(8,128)(2,1)S(1)} %collective-permute-done.next_ref, s32[8,128]{1,0:T(8,128)S(1)} %get-tuple-element.19.rank_ref, ...), custom_call_target="tpu_custom_call" | custom-call | flops 251658240 | bytes 1048576 | tf_op jit(solution)/shard_map/pallas_call | solution.py:315
  7.8 0.9 %collective-permute-done.3.refs_2_.refs_5_.refs_6_ = bf16[2,128,128]{2,1,0:T(8,128)(2,1)S(1)} collective-permute-done((bf16[2,128,128]{2,1,0:T(8,128)(2,1)S(1)}, bf16[2,128,128]{2,1,0:T(8,128)(2,1)S(1)}, u32[]{:S(2)}, u32[]{:S(2)}) %collective-permute-start.3) | collective-permute-done | bytes 65568 | tf_op jit(solution)/shard_map/ppermute | solution.py:260
  8.7 1.7 %collective-permute-done.2.refs_1_.refs_4_.refs_5_ = bf16[2,128,128]{2,1,0:T(8,128)(2,1)S(1)} collective-permute-done((bf16[2,128,128]{2,1,0:T(8,128)(2,1)S(1)}, bf16[2,128,128]{2,1,0:T(8,128)(2,1)S(1)}, u32[]{:S(2)}, u32[]{:S(2)}) %collective-permute-start.2) | collective-permute-done | bytes 65568 | tf_op jit(solution)/shard_map/ppermute | solution.py:260
  10.4 0.3 %collective-permute-done.1.refs_0_.refs_3_.refs_4_ = bf16[2,128,128]{2,1,0:T(8,128)(2,1)S(1)} collective-permute-done((bf16[2,128,128]{2,1,0:T(8,128)(2,1)S(1)}, bf16[2,128,128]{2,1,0:T(8,128)(2,1)S(1)}, u32[]{:S(2)}, u32[]{:S(2)}) %collective-permute-start.1) | collective-permute-done | bytes 65568 | tf_op jit(solution)/shard_map/ppermute | solution.py:260
  10.8 1.8 %shard_map.96 = (bf16[384,768]{1,0:T(8,128)(2,1)S(1)}, bf16[384,768]{1,0:T(8,128)(2,1)S(1)}, bf16[2,128,128]{2,1,0:T(8,128)(2,1)S(1)}, bf16[2,128,128]{2,1,0:T(8,128)(2,1)S(1)}, bf16[2,128,128]{2,1,0:T(8,128)(2,1)S(1)}) custom-call(bf16[1584,128]{1,0:T(8,128)(2,1)S(1)} %get-tuple-element.18.packet_ref, bf16[1584,128]{1,0:T(8,128)(2,1)S(1)} %collective-permute-done.next_ref, ...), custom_call_target="tpu_custom_call" | custom-call | flops 754974720 | bytes 1048576 | tf_op jit(solution)/shard_map/pallas_call | solution.py:324
  12.5 0.3 %shard_map.97 = bf16[128,768]{1,0:T(8,128)(2,1)S(1)} custom-call(bf16[128,768]{1,0:T(8,128)(2,1)S(1)} %get-tuple-element.22.refs_0_, bf16[384,768]{1,0:T(8,128)(2,1)S(1)} %get-tuple-element.23.refs_1_, bf16[2,128,128]{2,1,0:T(8,128)(2,1)S(1)} %get-tuple-element.20.refs_0_.refs_2_.refs_3_, ...), custom_call_target="tpu_custom_call" | custom-call | flops 503316480 | bytes 1048576 | tf_op jit(solution)/shard_map/pallas_call | solution.py:335
  12.9 0.1 collective-permute-start.4
  12.9 1.6 %collective-permute-start.5 = (bf16[2,128,128]{2,1,0:T(8,128)(2,1)S(1)}, bf16[2,128,128]{2,1,0:T(8,128)(2,1)S(1)}, u32[]{:S(2)}, u32[]{:S(2)}) collective-permute-start(bf16[2,128,128]{2,1,0:T(8,128)(2,1)S(1)} %get-tuple-element.28), channel_id=1, source_target_pairs={{0,24},{4,28},{8,16},{12,20},{16,8},{20,12},{24,0},{28,4},{1,25},{... | collective-permute-start | bytes 196616 | tf_op jit(solution)/shard_map/ppermute | solution.py:260
  14.5 1.1 %collective-permute-start.6 = (bf16[2,128,128]{2,1,0:T(8,128)(2,1)S(1)}, bf16[2,128,128]{2,1,0:T(8,128)(2,1)S(1)}, u32[]{:S(2)}, u32[]{:S(2)}) collective-permute-start(bf16[2,128,128]{2,1,0:T(8,128)(2,1)S(1)} %get-tuple-element.29), channel_id=1, source_target_pairs={{0,16},{4,12},{8,24},{12,4},{16,0},{20,28},{24,8},{28,20},{1,17},{... | collective-permute-start | bytes 196616 | tf_op jit(solution)/shard_map/ppermute | solution.py:260
  15.6 0.9 %collective-permute-start.7 = (bf16[2,128,128]{2,1,0:T(8,128)(2,1)S(1)}, bf16[2,128,128]{2,1,0:T(8,128)(2,1)S(1)}, u32[]{:S(2)}, u32[]{:S(2)}) collective-permute-start(bf16[2,128,128]{2,1,0:T(8,128)(2,1)S(1)} %get-tuple-element.30), channel_id=1, source_target_pairs={{0,8},{4,20},{8,0},{12,28},{16,24},{20,4},{24,16},{28,12},{1,9},{5... | collective-permute-start | bytes 196616 | tf_op jit(solution)/shard_map/ppermute | solution.py:260
  16.5 0.0 collective-permute-done.4.refs_0_
  16.5 1.1 %shard_map.98 = bf16[768,128]{1,0:T(8,128)(2,1)} custom-call(bf16[128,768]{1,0:T(8,128)(2,1)S(1)} %collective-permute-done.4.refs_0_, bf16[128,768]{1,0:T(8,128)(2,1)S(1)} %get-tuple-element.24.refs_1_, bf16[384,768]{1,0:T(8,128)(2,1)S(1)} %get-tuple-element.25.refs_2_, bf16[2,128,128]{2,1,0:T(8,128)(2,1)S(1)} %get-tuple-element.20.refs_0_.refs_2_.refs_3_, ...), custom_call_target="tpu_custom_call" | custom-call | flops 503316480 | bytes 1048576 | tf_op jit(solution)/shard_map/pallas_call | solution.py:345
  17.6 1.2 %collective-permute-done.5.refs_1_ = bf16[2,128,128]{2,1,0:T(8,128)(2,1)S(1)} collective-permute-done((bf16[2,128,128]{2,1,0:T(8,128)(2,1)S(1)}, bf16[2,128,128]{2,1,0:T(8,128)(2,1)S(1)}, u32[]{:S(2)}, u32[]{:S(2)}) %collective-permute-start.5) | collective-permute-done | bytes 65568 | tf_op jit(solution)/shard_map/ppermute | solution.py:260
  18.8 0.8 %collective-permute-done.6.refs_2_ = bf16[2,128,128]{2,1,0:T(8,128)(2,1)S(1)} collective-permute-done((bf16[2,128,128]{2,1,0:T(8,128)(2,1)S(1)}, bf16[2,128,128]{2,1,0:T(8,128)(2,1)S(1)}, u32[]{:S(2)}, u32[]{:S(2)}) %collective-permute-start.6) | collective-permute-done | bytes 65568 | tf_op jit(solution)/shard_map/ppermute | solution.py:260
  19.6 0.2 %collective-permute-done.7.refs_3_ = bf16[2,128,128]{2,1,0:T(8,128)(2,1)S(1)} collective-permute-done((bf16[2,128,128]{2,1,0:T(8,128)(2,1)S(1)}, bf16[2,128,128]{2,1,0:T(8,128)(2,1)S(1)}, u32[]{:S(2)}, u32[]{:S(2)}) %collective-permute-start.7) | collective-permute-done | bytes 65568 | tf_op jit(solution)/shard_map/ppermute | solution.py:260
  19.8 0.7 %shard_map.99 = (bf16[128,128]{1,0:T(8,128)(2,1)}, bf16[128,128]{1,0:T(8,128)(2,1)}) custom-call(f32[2,128,128]{2,1,0:T(8,128)S(1)} %get-tuple-element.27.refs_0_, bf16[2,128,128]{2,1,0:T(8,128)(2,1)S(1)} %collective-permute-done.5.refs_1_, bf16[2,128,128]{2,1,0:T(8,128)(2,1)S(1)} %collective-permute-done.6.refs_2_, ...), custom_call_target="tpu_custom_call" | custom-call | tf_op jit(solution)/shard_map/pallas_call | solution.py:360
Async XLA Ops:
  1.9 4.7 %collective-permute-start = (bf16[1584,128]{1,0:T(8,128)(2,1)S(1)}, bf16[1584,128]{1,0:T(8,128)(2,1)S(1)}, u32[]{:S(2)}, u32[]{:S(2)}) collective-permute-start(bf16[1584,128]{1,0:T(8,128)(2,1)S(1)} %get-tuple-element.18.packet_ref), channel_id=1, source_target_pairs={{0,4},{4,0},{1,5},{5,1},{2,6},{6,2},{3,7},{7,3},{8,12},{12,8},{9,1... | collective-permute-start | bytes 1216520 | tf_op jit(solution)/shard_map/ppermute | solution.py:252
  2.5 6.2 %collective-permute-start.3 = (bf16[2,128,128]{2,1,0:T(8,128)(2,1)S(1)}, bf16[2,128,128]{2,1,0:T(8,128)(2,1)S(1)}, u32[]{:S(2)}, u32[]{:S(2)}) collective-permute-start(bf16[2,128,128]{2,1,0:T(8,128)(2,1)S(1)} %get-tuple-element.20.refs_0_.refs_2_.refs_3_), channel_id=1, source_target_pairs={{0,24},{4,28},{8,16},{12,20},{16,8},{20,12},{24,0},{28,4},{1,25},{... | collective-permute-start | bytes 196616 | tf_op jit(solution)/shard_map/ppermute | solution.py:260
  6.0 4.4 %collective-permute-start.2 = (bf16[2,128,128]{2,1,0:T(8,128)(2,1)S(1)}, bf16[2,128,128]{2,1,0:T(8,128)(2,1)S(1)}, u32[]{:S(2)}, u32[]{:S(2)}) collective-permute-start(bf16[2,128,128]{2,1,0:T(8,128)(2,1)S(1)} %get-tuple-element.20.refs_0_.refs_2_.refs_3_), channel_id=1, source_target_pairs={{0,16},{4,12},{8,24},{12,4},{16,0},{20,28},{24,8},{28,20},{1,17},{... | collective-permute-start | bytes 196616 | tf_op jit(solution)/shard_map/ppermute | solution.py:260
  6.5 4.3 %collective-permute-start.1 = (bf16[2,128,128]{2,1,0:T(8,128)(2,1)S(1)}, bf16[2,128,128]{2,1,0:T(8,128)(2,1)S(1)}, u32[]{:S(2)}, u32[]{:S(2)}) collective-permute-start(bf16[2,128,128]{2,1,0:T(8,128)(2,1)S(1)} %get-tuple-element.20.refs_0_.refs_2_.refs_3_), channel_id=1, source_target_pairs={{0,8},{4,20},{8,0},{12,28},{16,24},{20,4},{24,16},{28,12},{1,9},{5... | collective-permute-start | bytes 196616 | tf_op jit(solution)/shard_map/ppermute | solution.py:260
  12.9 3.6 %collective-permute-start.4 = (bf16[128,768]{1,0:T(8,128)(2,1)S(1)}, bf16[128,768]{1,0:T(8,128)(2,1)S(1)}, u32[]{:S(2)}, u32[]{:S(2)}) collective-permute-start(bf16[128,768]{1,0:T(8,128)(2,1)S(1)} %shard_map.97), channel_id=1, source_target_pairs={{0,4},{4,0},{1,5},{5,1},{2,6},{6,2},{3,7},{7,3},{8,12},{12,8},{9,1... | collective-permute-start | bytes 589832 | tf_op jit(solution)/shard_map/ppermute | solution.py:252
  12.9 5.9 %collective-permute-start.5 = (bf16[2,128,128]{2,1,0:T(8,128)(2,1)S(1)}, bf16[2,128,128]{2,1,0:T(8,128)(2,1)S(1)}, u32[]{:S(2)}, u32[]{:S(2)}) collective-permute-start(bf16[2,128,128]{2,1,0:T(8,128)(2,1)S(1)} %get-tuple-element.28), channel_id=1, source_target_pairs={{0,24},{4,28},{8,16},{12,20},{16,8},{20,12},{24,0},{28,4},{1,25},{... | collective-permute-start | bytes 196616 | tf_op jit(solution)/shard_map/ppermute | solution.py:260
  14.5 5.1 %collective-permute-start.6 = (bf16[2,128,128]{2,1,0:T(8,128)(2,1)S(1)}, bf16[2,128,128]{2,1,0:T(8,128)(2,1)S(1)}, u32[]{:S(2)}, u32[]{:S(2)}) collective-permute-start(bf16[2,128,128]{2,1,0:T(8,128)(2,1)S(1)} %get-tuple-element.29), channel_id=1, source_target_pairs={{0,16},{4,12},{8,24},{12,4},{16,0},{20,28},{24,8},{28,20},{1,17},{... | collective-permute-start | bytes 196616 | tf_op jit(solution)/shard_map/ppermute | solution.py:260
  15.6 4.3 %collective-permute-start.7 = (bf16[2,128,128]{2,1,0:T(8,128)(2,1)S(1)}, bf16[2,128,128]{2,1,0:T(8,128)(2,1)S(1)}, u32[]{:S(2)}, u32[]{:S(2)}) collective-permute-start(bf16[2,128,128]{2,1,0:T(8,128)(2,1)S(1)} %get-tuple-element.30), channel_id=1, source_target_pairs={{0,8},{4,20},{8,0},{12,28},{16,24},{20,4},{24,16},{28,12},{1,9},{5... | collective-permute-start | bytes 196616 | tf_op jit(solution)/shard_map/ppermute | solution.py:260

commit v5 on v4

v5 whole, which is shorter than its diff:
```python
import functools
import math

import jax
import jax.numpy as jnp
from jax import lax
from jax.experimental import pallas as pl
from jax.experimental.pallas import tpu as pltpu
from jax.sharding import PartitionSpec as P

LOG2E = math.log2(math.e)
STAT_ROWS = 16
SPLIT = 3


def contract(lhs, rhs, lhs_dim, rhs_dim):
    return lax.dot_general(
        lhs, rhs, (((lhs_dim,), (rhs_dim,)), ((), ())), preferred_element_type=jnp.float32
    )


def packet_rows(sizes):
    group_size, row_count, _ = sizes
    return 3 * group_size * row_count + SPLIT * STAT_ROWS


def peer_offset(step, outer, inner_count):
    bits = inner_count.bit_length() - 1
    turn = outer % 2
    return ((step << turn) | (step >> (bits - turn))) & (inner_count - 1)


def load_kernel(
    sizes, query_hbm, grad_hbm, out_hbm, norm_hbm, key_hbm, value_hbm, pair_ref, packet_ref, norm_ref, sems
):
    group_size, row_count, _ = sizes
    half = group_size * row_count
    copies = [
        pltpu.make_async_copy(source, target, sems.at[at])
        for at, (source, target) in enumerate(
            [
                (norm_hbm, norm_ref.at[pl.ds(0, group_size)]),
                (key_hbm, pair_ref.at[0]),
                (value_hbm, pair_ref.at[1]),
                (query_hbm, packet_ref.at[pl.ds(0, half)]),
                (grad_hbm, packet_ref.at[pl.ds(half, half)]),
                (out_hbm, packet_ref.at[pl.ds(2 * half, half)]),
            ]
        )
    ]
    for copy in copies:
        copy.start()
    copies[0].wait()
    held = lax.broadcasted_iota(jnp.int32, (STAT_ROWS, row_count), 0) < group_size
    rest = jnp.where(held, jnp.clip(norm_ref[...], -3.38e38, 3.38e38), 0.0)
    for term in range(SPLIT):
        piece = rest.astype(jnp.bfloat16)
        start = 3 * half + term * STAT_ROWS
        packet_ref[start : start + STAT_ROWS, :] = piece
        rest = rest - piece.astype(jnp.float32)
    for copy in copies[1:]:
        copy.wait()


def row_stats(packet_ref, stat_ref, sizes):
    group_size, row_count, _ = sizes
    half = group_size * row_count
    start = 3 * half
    pieces = [
        packet_ref[start + term * STAT_ROWS : start + (term + 1) * STAT_ROWS, :].astype(jnp.float32)
        for term in range(SPLIT)
    ]
    stat_ref[...] = (pieces[0] + (pieces[1] + pieces[2])) * LOG2E
    for head in range(group_size):
        first = head * row_count
        grads = packet_ref[half + first : half + first + row_count, :].astype(jnp.float32)
        outs = packet_ref[2 * half + first : 2 * half + first + row_count, :].astype(jnp.float32)
        stat_ref[8 + head : 9 + head, :] = jnp.sum((grads * outs).T, axis=0, keepdims=True)


def block_terms(keys, values, parts, sizes):
    group_size, row_count, head_size = sizes
    half = group_size * row_count
    scale = LOG2E / math.sqrt(head_size)
    per_step = 2 if group_size % 2 == 0 else 1
    key_total = 0.0
    value_total = 0.0
    for packet_ref, stats, visible, scores_ref in parts:
        weights_parts = []
        score_parts = []
        for first in range(0, group_size, per_step):
            start, stop = first * row_count, (first + per_step) * row_count
            queries = packet_ref[start:stop, :]
            grads = packet_ref[half + start : half + stop, :]
            scores = contract(keys, queries, 1, 1)
            grad_weights = contract(values, grads, 1, 1)
            for at in range(per_step):
                head = first + at
                lanes = slice(at * row_count, (at + 1) * row_count)
                weights = jnp.exp2(scores[:, lanes] * scale - stats[head : head + 1, :])
                if visible is not None:
                    weights = jnp.where(visible, weights, 0.0)
                weights_parts.append(weights.astype(jnp.bfloat16))
                score_parts.append(
                    (weights * (grad_weights[:, lanes] - stats[8 + head : 9 + head, :])).astype(jnp.bfloat16)
                )
        grad_scores = jnp.concatenate(score_parts, axis=1)
        scores_ref[...] = grad_scores
        value_total += contract(jnp.concatenate(weights_parts, axis=1), packet_ref[half : 2 * half, :], 1, 0)
        key_total += contract(grad_scores, packet_ref[:half, :], 1, 0)
    return key_total, value_total


def visible_rows(rank_ref, steps, inner_count, row_count):
    span_rows = row_count // 2
    key_rows = lax.broadcasted_iota(jnp.int32, (row_count, row_count), 0)
    my_rows = lax.broadcasted_iota(jnp.int32, (row_count, row_count), 1)

    def positions(rank, rows):
        return jnp.where(
            rows < span_rows,
            rank * span_rows + rows,
            (2 * inner_count - 2 - rank) * span_rows + rows,
        )

    mine = positions(rank_ref[0:1, :], my_rows)
    return jnp.concatenate(
        [positions(rank_ref[step : step + 1, :], key_rows) <= mine for step in steps], axis=0
    )


def stacked(blocks, which):
    return jnp.concatenate([ref[which] for ref in blocks], axis=0)


def near_kernel(
    sizes, inner_count, outer_count, packet_ref, next_ref, order_hbm, pair_ref, scores_ref,
    next_scores_ref, total_ref, stat_ref, rank_ref, order_ref, sem,
):
    _, row_count, _ = sizes
    copy = pltpu.make_async_copy(order_hbm, order_ref, sem)
    copy.start()
    has_next = lax.axis_index("outer") < outer_count - 1
    row_stats(packet_ref, stat_ref.at[0], sizes)
    row_stats(next_ref, stat_ref.at[1], sizes)

    @pl.when(jnp.logical_not(has_next))
    def _():
        stat_ref[1, :8, :] = jnp.full((8, row_count), 1e30, jnp.float32)

    key_rows = lax.broadcasted_iota(jnp.int32, (row_count, row_count), 0)
    visible = key_rows <= lax.broadcasted_iota(jnp.int32, (row_count, row_count), 1)
    parts = ((packet_ref, stat_ref[0], visible, scores_ref), (next_ref, stat_ref[1], None, next_scores_ref))
    total_ref[0], total_ref[1] = block_terms(pair_ref[0], pair_ref[1], parts, sizes)
    copy.wait()
    my_index = lax.axis_index("inner")
    turned = lax.rem(lax.axis_index("outer"), 2) == 1
    for step in range(inner_count):
        offset = jnp.where(turned, peer_offset(step, 1, inner_count), peer_offset(step, 0, inner_count))
        rank_ref[step : step + 1, :] = jnp.full((1, row_count), order_ref[my_index ^ offset], jnp.int32)


def far_kernel(sizes, inner_count, steps, packet_ref, next_ref, rank_ref, stat_ref, *refs):
    count = len(steps)
    _, row_count, head_size = sizes
    inv_root = 1.0 / math.sqrt(head_size)
    blocks, (scores_ref, next_scores_ref), sums = refs[:count], refs[count : count + 2], refs[count + 2 :]
    visible = visible_rows(rank_ref, steps, inner_count, row_count)
    parts = ((packet_ref, stat_ref[0], visible, scores_ref), (next_ref, stat_ref[1], None, next_scores_ref))
    key_total, value_total = block_terms(stacked(blocks, 0), stacked(blocks, 1), parts, sizes)
    for at, ref in enumerate(sums):
        rows = slice(at * row_count, (at + 1) * row_count)
        ref[0] = (key_total[rows] * inv_root).astype(jnp.bfloat16)
        ref[1] = value_total[rows].astype(jnp.bfloat16)


def query_terms(refs, groups, lanes):
    scores = jnp.concatenate([ref[:, lanes] for ref in refs[:groups]], axis=0)
    return contract(stacked(refs[groups:], 0), scores, 0, 0)


def back_kernel(sizes, outer_count, groups, *refs):
    group_size, row_count, _ = sizes
    has_next = lax.axis_index("outer") < outer_count - 1

    @pl.when(has_next)
    def _():
        refs[-1][...] = query_terms(refs[:-1], groups, slice(None)).astype(jnp.bfloat16)


def query_kernel(sizes, groups, *refs):
    group_size, row_count, head_size = sizes
    inv_root = 1.0 / math.sqrt(head_size)
    back_ref, inputs = refs[0], refs[1:-4]
    result_hbm, total_ref, result_ref, sem = refs[-4:]
    has_prev = lax.axis_index("outer") > 0
    total_ref[...] = query_terms(inputs, groups, slice(None))

    @pl.when(has_prev)
    def _():
        total_ref[...] += back_ref[...].astype(jnp.float32)

    for head in range(group_size):
        rows = slice(head * row_count, (head + 1) * row_count)
        result_ref[rows, :] = (total_ref[:, rows] * inv_root).T.astype(jnp.bfloat16)
    copy = pltpu.make_async_copy(result_ref, result_hbm, sem)
    copy.start()
    copy.wait()


def early_kernel(sizes, *refs):
    inv_root = 1.0 / math.sqrt(sizes[2])
    own_ref, returned, total_ref = refs[0], refs[1:-1], refs[-1]
    for which, factor in ((0, inv_root), (1, 1.0)):
        total = own_ref[which] * factor
        for ref in returned:
            total += ref[which].astype(jnp.float32)
        total_ref[which] = total


def sum_kernel(*refs):
    total_ref, returned = refs[0], refs[1:-5]
    key_hbm, value_hbm, key_ref, value_ref, sems = refs[-5:]
    key_total = total_ref[0]
    value_total = total_ref[1]
    for ref in returned:
        key_total += ref[0].astype(jnp.float32)
        value_total += ref[1].astype(jnp.float32)
    key_ref[...] = key_total.astype(jnp.bfloat16)
    value_ref[...] = value_total.astype(jnp.bfloat16)
    copies = [
        pltpu.make_async_copy(key_ref, key_hbm, sems.at[0]),
        pltpu.make_async_copy(value_ref, value_hbm, sems.at[1]),
    ]
    for copy in copies:
        copy.start()
    for copy in copies:
        copy.wait()


def on_device(queries, key_rows, value_rows, attn_out, grad_out, log_norms, pair_order):
    row_count, group_size, head_size = queries.shape
    inner_count = lax.axis_size("inner")
    outer_count = lax.axis_size("outer")
    assert inner_count & (inner_count - 1) == 0 and inner_count > 1
    sizes = (group_size, row_count, head_size)
    half = group_size * row_count
    away = list(range(inner_count - 1, 0, -1))

    def flat(array):
        return jnp.swapaxes(array, 0, 1).reshape(-1, head_size)

    def in_hbm(array):
        return pltpu.with_memory_space_constraint(array, pltpu.HBM)

    def to_segment(block, ahead):
        route = [(at, (at + ahead) % outer_count) for at in range(outer_count)]
        return lax.ppermute(block, "outer", route)

    def exchange(block, step):
        route = []
        for inner in range(inner_count):
            for outer in range(outer_count):
                peer = inner ^ peer_offset(step, outer, inner_count)
                route.append((inner * outer_count + outer, peer * outer_count + outer))
        return lax.ppermute(block, ("inner", "outer"), route)

    vmem = pl.BlockSpec(memory_space=pltpu.VMEM)
    hbm = pl.BlockSpec(memory_space=pltpu.HBM)
    roomy = pltpu.CompilerParams(vmem_limit_bytes=32 * 2**20)

    def shape(dims, dtype):
        return jax.ShapeDtypeStruct(dims, dtype)

    def cost(blocks, data=2**20):
        each = group_size * row_count * row_count
        return pl.CostEstimate(
            flops=10 * blocks * each * head_size, bytes_accessed=data, transcendentals=blocks * each
        )

    block_shape = shape((2, row_count, head_size), jnp.bfloat16)

    pair, packet = pl.pallas_call(
        functools.partial(load_kernel, sizes),
        out_shape=(
            block_shape,
            shape((packet_rows(sizes), head_size), jnp.bfloat16),
        ),
        in_specs=[hbm] * 6,
        out_specs=(vmem,) * 2,
        scratch_shapes=[pltpu.VMEM((STAT_ROWS, row_count), jnp.float32), pltpu.SemaphoreType.DMA((6,))],
        cost_estimate=cost(0),
        compiler_params=roomy,
    )(
        *(
            in_hbm(array)
            for array in (
                flat(queries), flat(grad_out), flat(attn_out), log_norms, flat(key_rows), flat(value_rows)
            )
        )
    )
    next_packet = to_segment(packet, -1)
    blocks = {0: pair}
    for step in away:
        blocks[step] = exchange(pair, step)

    def scores_shape(count):
        return shape((count * row_count, half), jnp.bfloat16)

    near_scores, near_next_scores, own_total, stats, rank = pl.pallas_call(
        functools.partial(near_kernel, sizes, inner_count, outer_count),
        out_shape=(
            scores_shape(1),
            scores_shape(1),
            shape((2, row_count, head_size), jnp.float32),
            shape((2, STAT_ROWS, row_count), jnp.float32),
            shape((max(8, inner_count), row_count), jnp.int32),
        ),
        in_specs=[vmem] * 2 + [hbm, vmem],
        out_specs=(vmem,) * 5,
        scratch_shapes=[pltpu.SMEM((inner_count,), jnp.int32), pltpu.SemaphoreType.DMA],
        cost_estimate=cost(2),
        compiler_params=roomy,
    )(packet, next_packet, in_hbm(pair_order), pair)

    scores, next_scores, sums = [near_scores], [near_next_scores], {}
    middle = inner_count // 2 - 1
    held = [0]
    for steps in (away[:middle][::-1], away[middle:][::-1]):
        if steps:
            far_scores, far_next_scores, *terms = pl.pallas_call(
                functools.partial(far_kernel, sizes, inner_count, steps),
                out_shape=(scores_shape(len(steps)),) * 2 + (block_shape,) * len(steps),
                in_specs=[vmem] * (4 + len(steps)),
                out_specs=(vmem,) * (2 + len(steps)),
                cost_estimate=cost(2 * len(steps)),
                compiler_params=roomy,
            )(packet, next_packet, rank, stats, *(blocks[step] for step in steps))
            scores.append(far_scores)
            next_scores.append(far_next_scores)
            sums.update(zip(steps, terms))
            held += steps
    all_blocks = [blocks[step] for step in held]
    groups = len(scores)
    returned = [exchange(sums[step], step) for step in away]

    query_next = pl.pallas_call(
        functools.partial(back_kernel, sizes, outer_count, groups),
        out_shape=shape((head_size, half), jnp.bfloat16),
        in_specs=[vmem] * (groups + inner_count),
        out_specs=vmem,
        cost_estimate=cost(inner_count),
        compiler_params=roomy,
    )(*next_scores, *all_blocks)
    query_back = to_segment(query_next, 1)

    early_total = pl.pallas_call(
        functools.partial(early_kernel, sizes),
        out_shape=shape((2, row_count, head_size), jnp.float32),
        in_specs=[vmem] * (1 + middle),
        out_specs=vmem,
        cost_estimate=cost(8 * inner_count),
        compiler_params=roomy,
    )(own_total, *returned[:middle])
    early_total, scores[0] = lax.optimization_barrier((early_total, scores[0]))

    query_out = pl.pallas_call(
        functools.partial(query_kernel, sizes, groups),
        out_shape=shape((half, head_size), jnp.bfloat16),
        in_specs=[vmem] * (1 + groups + inner_count),
        out_specs=hbm,
        scratch_shapes=[
            pltpu.VMEM((head_size, half), jnp.float32),
            pltpu.VMEM((half, head_size), jnp.bfloat16),
            pltpu.SemaphoreType.DMA,
        ],
        cost_estimate=cost(inner_count),
        compiler_params=roomy,
    )(query_back, *scores, *all_blocks)

    early_total, query_out = lax.optimization_barrier((early_total, query_out))
    key_out, value_out = pl.pallas_call(
        sum_kernel,
        out_shape=(shape((row_count, head_size), jnp.bfloat16),) * 2,
        in_specs=[vmem] * (1 + len(away) - middle),
        out_specs=(hbm, hbm),
        scratch_shapes=[
            pltpu.VMEM((row_count, head_size), jnp.bfloat16),
            pltpu.VMEM((row_count, head_size), jnp.bfloat16),
            pltpu.SemaphoreType.DMA((2,)),
        ],
        compiler_params=roomy,
    )(early_total, *returned[middle:])
    grad_queries = jnp.swapaxes(query_out.reshape(group_size, row_count, head_size), 0, 1)
    return (grad_queries, key_out[:, None, :], value_out[:, None, :])


def solution(mesh):
    in_specs = (
        P(("outer", "inner"), "head", None),
        P(("outer", "inner"), "head", None),
        P(("outer", "inner"), "head", None),
        P(("outer", "inner"), "head", None),
        P(("outer", "inner"), "head", None),
        P("head", ("outer", "inner")),
        P(),
    )
    out_specs = (
        P(("outer", "inner"), "head", None),
        P(("outer", "inner"), "head", None),
        P(("outer", "inner"), "head", None),
    )
    return jax.shard_map(
        on_device, mesh=mesh, in_specs=in_specs, out_specs=out_specs, check_vma=False
    )
```

time: 20.7 us -> 19.2 us (0.928)
  waiting for transfers between devices: 5.16 us -> 3.76 us
  Pallas kernels: 6.36 us -> 5.98 us
  starting transfers between devices: 8.3 us -> 8.58 us
    ppermute x6, waiting for transfers between devices: 5.16 us -> 3.16 us  [exchange(): return lax.ppermute(block, ('inner', 'outer'), route)]
    ppermute x2, waiting for transfers between devices: 0.01 us -> 0.6 us  [to_segment(): return lax.ppermute(block, 'outer', route)]
    pallas_call x6 -> x8, Pallas kernels: 6.36 us -> 5.98 us  [the longest x2 1.66 us: on_device(): pl.pallas_call(functools.partial(far_kernel, sizes, inner_count, steps),...]
    ppermute x6, starting transfers between devices: 7.72 us -> 7.99 us  [exchange(): return lax.ppermute(block, ('inner', 'outer'), route)]
  transfers between devices with their start and end apart: 8 -> 8, of which waited for: 6 -> 4; matrix products, arithmetic and copies ran while one was open for 0% -> 0% of each run, Pallas kernels for 11% -> 22%
where the time goes in v5:
time: 19.2 us; the launch traced here: 19 us
  starting transfers between devices  8.58 us (45%)
  Pallas kernels  5.98 us (31%)
  waiting for transfers between devices  3.76 us (20%)
  between operations  0.69 us (4%)
    ppermute x6, starting transfers between devices, exchange(): return lax.ppermute(block, ('inner', 'outer'), route)  7.99 us
    ppermute x6, waiting for transfers between devices, exchange(): return lax.ppermute(block, ('inner', 'outer'), route)  3.16 us
    pallas_call x2, Pallas kernels, on_device(): pl.pallas_call(functools.partial(far_kernel, sizes, inner_count, steps),...  1.66 us
    pallas_call x1, Pallas kernels, on_device(): pl.pallas_call(functools.partial(load_kernel, sizes), out_shape=(block_sh...  1.22 us
    pallas_call x1, Pallas kernels, on_device(): pl.pallas_call(functools.partial(query_kernel, sizes, groups), out_shape=...  1.13 us
    pallas_call x1, Pallas kernels, on_device(): pl.pallas_call(functools.partial(near_kernel, sizes, inner_count, outer_c...  0.96 us
    pallas_call x1, Pallas kernels, on_device(): pl.pallas_call(sum_kernel, out_shape=(shape((row_count, head_size), jnp.b...  0.66 us
    ppermute x2, waiting for transfers between devices, to_segment(): return lax.ppermute(block, 'outer', route)  0.6 us
  transfers between devices with their start and end apart: 8, of which 4 were waited for; matrix products, arithmetic and copies ran while one was open for 0% of the time, Pallas kernels for 22%

profile of v5, /device:TPU:0, one launch (start us, length us, event | category | flops | bytes accessed | tf_op | source)
XLA Modules:
  0.0 19.0 jit_solution(12011723429173342749)
XLA Ops:
  0.6 1.2 %shard_map.94 = (bf16[2,128,128]{2,1,0:T(8,128)(2,1)S(1)}, bf16[2352,128]{1,0:T(8,128)(2,1)S(1)}) custom-call(bf16[768,128]{1,0:T(8,128)(2,1)} %bitcast.16, bf16[768,128]{1,0:T(8,128)(2,1)} %bitcast.17, bf16[768,128]{1,0:T(8,128)(2,1)} %bitcast.18, f32[6,128]{1,0:T(8,128)} %norm_hbm.1, bf16[128,128]{1,0:T(8,128)(2,1)} %bitcast.19, bf16[128,128]{1,0:T(8,128)(2,1)} %bitcast.20), custom_call_target="tpu_custom_call" | custom-call | bytes 1048576 | tf_op jit(solution)/shard_map/pallas_call | solution.py:283
  1.9 0.5 %collective-permute-start = (bf16[2352,128]{1,0:T(8,128)(2,1)S(1)}, bf16[2352,128]{1,0:T(8,128)(2,1)S(1)}, u32[]{:S(2)}, u32[]{:S(2)}) collective-permute-start(bf16[2352,128]{1,0:T(8,128)(2,1)S(1)} %get-tuple-element.23.packet_ref), channel_id=1, source_target_pairs={{0,4},{4,0},{1,5},{5,1},{2,6},{6,2},{3,7},{7,3},{8,12},{12,8},{9,1... | collective-permute-start | bytes 1806344 | tf_op jit(solution)/shard_map/ppermute | solution.py:258
  2.4 3.5 %collective-permute-start.1 = (bf16[2,128,128]{2,1,0:T(8,128)(2,1)S(1)}, bf16[2,128,128]{2,1,0:T(8,128)(2,1)S(1)}, u32[]{:S(2)}, u32[]{:S(2)}) collective-permute-start(bf16[2,128,128]{2,1,0:T(8,128)(2,1)S(1)} %get-tuple-element.24.pair_ref.refs_3_.refs_4_), channel_id=1, source_target_pairs={{0,24},{4,28},{8,16},{12,20},{16,8},{20,12},{24,0},{28,4},{1,25},{... | collective-permute-start | bytes 196616 | tf_op jit(solution)/shard_map/ppermute | solution.py:266
  5.9 0.5 %collective-permute-start.3 = (bf16[2,128,128]{2,1,0:T(8,128)(2,1)S(1)}, bf16[2,128,128]{2,1,0:T(8,128)(2,1)S(1)}, u32[]{:S(2)}, u32[]{:S(2)}) collective-permute-start(bf16[2,128,128]{2,1,0:T(8,128)(2,1)S(1)} %get-tuple-element.24.pair_ref.refs_3_.refs_4_), channel_id=1, source_target_pairs={{0,8},{4,20},{8,0},{12,28},{16,24},{20,4},{24,16},{28,12},{1,9},{5... | collective-permute-start | bytes 196616 | tf_op jit(solution)/shard_map/ppermute | solution.py:266
  6.4 0.1 collective-permute-start.4
  6.5 0.0 collective-permute-done.next_ref
  6.5 1.0 %shard_map.95 = (bf16[128,768]{1,0:T(8,128)(2,1)S(1)}, bf16[128,768]{1,0:T(8,128)(2,1)S(1)}, f32[2,128,128]{2,1,0:T(8,128)S(1)}, f32[2,16,128]{2,1,0:T(8,128)S(1)}, s32[8,128]{1,0:T(8,128)S(1)}) custom-call(bf16[2352,128]{1,0:T(8,128)(2,1)S(1)} %get-tuple-element.23.packet_ref, bf16[2352,128]{1,0:T(8,128)(2,1)S(1)} %collective-permute-done.next_ref, ...), custom_call_target="tpu_custom_call" | custom-call | flops 251658240 | bytes 1048576 | tf_op jit(solution)/shard_map/pallas_call | solution.py:310
  7.5 1.1 %collective-permute-done.1.refs_0_.refs_4_.refs_5_ = bf16[2,128,128]{2,1,0:T(8,128)(2,1)S(1)} collective-permute-done((bf16[2,128,128]{2,1,0:T(8,128)(2,1)S(1)}, bf16[2,128,128]{2,1,0:T(8,128)(2,1)S(1)}, u32[]{:S(2)}, u32[]{:S(2)}) %collective-permute-start.1) | collective-permute-done | bytes 65568 | tf_op jit(solution)/shard_map/ppermute | solution.py:266
  8.6 0.7 %shard_map.96 = (bf16[128,768]{1,0:T(8,128)(2,1)S(1)}, bf16[128,768]{1,0:T(8,128)(2,1)S(1)}, bf16[2,128,128]{2,1,0:T(8,128)(2,1)S(1)}) custom-call(bf16[2352,128]{1,0:T(8,128)(2,1)S(1)} %get-tuple-element.23.packet_ref, bf16[2352,128]{1,0:T(8,128)(2,1)S(1)} %collective-permute-done.next_ref, s32[8,128]{1,0:T(8,128)S(1)} %get-tuple-element.26.rank_ref, ...), custom_call_target="tpu_custom_call" | custom-call | flops 251658240 | bytes 1048576 | tf_op jit(solution)/shard_map/pallas_call | solution.py:331
  9.2 3.2 %collective-permute-start.2 = (bf16[2,128,128]{2,1,0:T(8,128)(2,1)S(1)}, bf16[2,128,128]{2,1,0:T(8,128)(2,1)S(1)}, u32[]{:S(2)}, u32[]{:S(2)}) collective-permute-start(bf16[2,128,128]{2,1,0:T(8,128)(2,1)S(1)} %get-tuple-element.28), channel_id=1, source_target_pairs={{0,24},{4,28},{8,16},{12,20},{16,8},{20,12},{24,0},{28,4},{1,25},{... | collective-permute-start | bytes 196616 | tf_op jit(solution)/shard_map/ppermute | solution.py:266
  12.4 0.0 collective-permute-done.3.refs_0_.refs_5_.refs_6_
  12.4 0.0 collective-permute-done.4.refs_1_.refs_6_.refs_7_
  12.4 1.0 %shard_map.98 = (bf16[256,768]{1,0:T(8,128)(2,1)S(1)}, bf16[256,768]{1,0:T(8,128)(2,1)S(1)}, bf16[2,128,128]{2,1,0:T(8,128)(2,1)S(1)}, bf16[2,128,128]{2,1,0:T(8,128)(2,1)S(1)}) custom-call(bf16[2352,128]{1,0:T(8,128)(2,1)S(1)} %get-tuple-element.23.packet_ref, bf16[2352,128]{1,0:T(8,128)(2,1)S(1)} %collective-permute-done.next_ref, ...), custom_call_target="tpu_custom_call" | custom-call | flops 503316480 | bytes 1048576 | tf_op jit(solution)/shard_map/pallas_call | solution.py:331
  13.4 0.3 %shard_map.99 = bf16[128,768]{1,0:T(8,128)(2,1)S(1)} custom-call(bf16[128,768]{1,0:T(8,128)(2,1)S(1)} %get-tuple-element.31.refs_0_, bf16[128,768]{1,0:T(8,128)(2,1)S(1)} %get-tuple-element.32.refs_1_, bf16[256,768]{1,0:T(8,128)(2,1)S(1)} %get-tuple-element.33.refs_2_, bf16[2,128,128]{2,1,0:T(8,128)(2,1)S(1)} %get-tuple-element.24.pair_ref.refs_3_.refs_4_, ...), custom_call_target="tpu_custom_call" | custom-call | flops 503316480 | bytes 1048576 | tf_op jit(solution)/shard_map/pallas_call | solution.py:347
  13.8 0.1 collective-permute-start.5
  13.9 0.2 %collective-permute-start.6 = (bf16[2,128,128]{2,1,0:T(8,128)(2,1)S(1)}, bf16[2,128,128]{2,1,0:T(8,128)(2,1)S(1)}, u32[]{:S(2)}, u32[]{:S(2)}) collective-permute-start(bf16[2,128,128]{2,1,0:T(8,128)(2,1)S(1)} %get-tuple-element.39), channel_id=1, source_target_pairs={{0,16},{4,12},{8,24},{12,4},{16,0},{20,28},{24,8},{28,20},{1,17},{... | collective-permute-start | bytes 196616 | tf_op jit(solution)/shard_map/ppermute | solution.py:266
  14.1 0.4 %collective-permute-start.7 = (bf16[2,128,128]{2,1,0:T(8,128)(2,1)S(1)}, bf16[2,128,128]{2,1,0:T(8,128)(2,1)S(1)}, u32[]{:S(2)}, u32[]{:S(2)}) collective-permute-start(bf16[2,128,128]{2,1,0:T(8,128)(2,1)S(1)} %get-tuple-element.40), channel_id=1, source_target_pairs={{0,8},{4,20},{8,0},{12,28},{16,24},{20,4},{24,16},{28,12},{1,9},{5... | collective-permute-start | bytes 196616 | tf_op jit(solution)/shard_map/ppermute | solution.py:266
  14.5 0.2 collective-permute-done.2.refs_1_
  14.7 0.6 %collective-permute-done.5.refs_0_ = bf16[128,768]{1,0:T(8,128)(2,1)S(1)} collective-permute-done((bf16[128,768]{1,0:T(8,128)(2,1)S(1)}, bf16[128,768]{1,0:T(8,128)(2,1)S(1)}, u32[]{:S(2)}, u32[]{:S(2)}) %collective-permute-start.5) | collective-permute-done | bytes 196640 | tf_op jit(solution)/shard_map/ppermute | solution.py:258
  15.3 1.1 %shard_map.100 = bf16[768,128]{1,0:T(8,128)(2,1)} custom-call(bf16[128,768]{1,0:T(8,128)(2,1)S(1)} %collective-permute-done.5.refs_0_, bf16[128,768]{1,0:T(8,128)(2,1)S(1)} %get-tuple-element.34.refs_1_, bf16[128,768]{1,0:T(8,128)(2,1)S(1)} %get-tuple-element.35.refs_2_, bf16[256,768]{1,0:T(8,128)(2,1)S(1)} %get-tuple-element.36.refs_3_, ...), custom_call_target="tpu_custom_call" | custom-call | flops 503316480 | bytes 1048576 | tf_op jit(solution)/shard_map/pallas_call | solution.py:367
  16.4 1.9 %collective-permute-done.6.refs_1_ = bf16[2,128,128]{2,1,0:T(8,128)(2,1)S(1)} collective-permute-done((bf16[2,128,128]{2,1,0:T(8,128)(2,1)S(1)}, bf16[2,128,128]{2,1,0:T(8,128)(2,1)S(1)}, u32[]{:S(2)}, u32[]{:S(2)}) %collective-permute-start.6) | collective-permute-done | bytes 65568 | tf_op jit(solution)/shard_map/ppermute | solution.py:266
  18.4 0.0 collective-permute-done.7.refs_2_
  18.4 0.7 %shard_map.101 = (bf16[128,128]{1,0:T(8,128)(2,1)}, bf16[128,128]{1,0:T(8,128)(2,1)}) custom-call(f32[2,128,128]{2,1,0:T(8,128)S(1)} %shard_map.97.refs_0_, bf16[2,128,128]{2,1,0:T(8,128)(2,1)S(1)} %collective-permute-done.6.refs_1_, bf16[2,128,128]{2,1,0:T(8,128)(2,1)S(1)} %collective-permute-done.7.refs_2_), custom_call_target="tpu_custom_call" | custom-call | tf_op jit(solution)/shard_map/pallas_call | solution.py:382
  (1 shorter events, 0.0 us)
Async XLA Ops:
  1.9 4.7 %collective-permute-start = (bf16[2352,128]{1,0:T(8,128)(2,1)S(1)}, bf16[2352,128]{1,0:T(8,128)(2,1)S(1)}, u32[]{:S(2)}, u32[]{:S(2)}) collective-permute-start(bf16[2352,128]{1,0:T(8,128)(2,1)S(1)} %get-tuple-element.23.packet_ref), channel_id=1, source_target_pairs={{0,4},{4,0},{1,5},{5,1},{2,6},{6,2},{3,7},{7,3},{8,12},{12,8},{9,1... | collective-permute-start | bytes 1806344 | tf_op jit(solution)/shard_map/ppermute | solution.py:258
  2.4 6.2 %collective-permute-start.1 = (bf16[2,128,128]{2,1,0:T(8,128)(2,1)S(1)}, bf16[2,128,128]{2,1,0:T(8,128)(2,1)S(1)}, u32[]{:S(2)}, u32[]{:S(2)}) collective-permute-start(bf16[2,128,128]{2,1,0:T(8,128)(2,1)S(1)} %get-tuple-element.24.pair_ref.refs_3_.refs_4_), channel_id=1, source_target_pairs={{0,24},{4,28},{8,16},{12,20},{16,8},{20,12},{24,0},{28,4},{1,25},{... | collective-permute-start | bytes 196616 | tf_op jit(solution)/shard_map/ppermute | solution.py:266
  5.9 6.5 %collective-permute-start.3 = (bf16[2,128,128]{2,1,0:T(8,128)(2,1)S(1)}, bf16[2,128,128]{2,1,0:T(8,128)(2,1)S(1)}, u32[]{:S(2)}, u32[]{:S(2)}) collective-permute-start(bf16[2,128,128]{2,1,0:T(8,128)(2,1)S(1)} %get-tuple-element.24.pair_ref.refs_3_.refs_4_), channel_id=1, source_target_pairs={{0,8},{4,20},{8,0},{12,28},{16,24},{20,4},{24,16},{28,12},{1,9},{5... | collective-permute-start | bytes 196616 | tf_op jit(solution)/shard_map/ppermute | solution.py:266
  6.4 6.0 %collective-permute-start.4 = (bf16[2,128,128]{2,1,0:T(8,128)(2,1)S(1)}, bf16[2,128,128]{2,1,0:T(8,128)(2,1)S(1)}, u32[]{:S(2)}, u32[]{:S(2)}) collective-permute-start(bf16[2,128,128]{2,1,0:T(8,128)(2,1)S(1)} %get-tuple-element.24.pair_ref.refs_3_.refs_4_), channel_id=1, source_target_pairs={{0,16},{4,12},{8,24},{12,4},{16,0},{20,28},{24,8},{28,20},{1,17},{... | collective-permute-start | bytes 196616 | tf_op jit(solution)/shard_map/ppermute | solution.py:266
  9.2 5.4 %collective-permute-start.2 = (bf16[2,128,128]{2,1,0:T(8,128)(2,1)S(1)}, bf16[2,128,128]{2,1,0:T(8,128)(2,1)S(1)}, u32[]{:S(2)}, u32[]{:S(2)}) collective-permute-start(bf16[2,128,128]{2,1,0:T(8,128)(2,1)S(1)} %get-tuple-element.28), channel_id=1, source_target_pairs={{0,24},{4,28},{8,16},{12,20},{16,8},{20,12},{24,0},{28,4},{1,25},{... | collective-permute-start | bytes 196616 | tf_op jit(solution)/shard_map/ppermute | solution.py:266
  13.8 1.5 %collective-permute-start.5 = (bf16[128,768]{1,0:T(8,128)(2,1)S(1)}, bf16[128,768]{1,0:T(8,128)(2,1)S(1)}, u32[]{:S(2)}, u32[]{:S(2)}) collective-permute-start(bf16[128,768]{1,0:T(8,128)(2,1)S(1)} %shard_map.99), channel_id=1, source_target_pairs={{0,4},{4,0},{1,5},{5,1},{2,6},{6,2},{3,7},{7,3},{8,12},{12,8},{9,1... | collective-permute-start | bytes 589832 | tf_op jit(solution)/shard_map/ppermute | solution.py:258
  13.9 4.5 %collective-permute-start.6 = (bf16[2,128,128]{2,1,0:T(8,128)(2,1)S(1)}, bf16[2,128,128]{2,1,0:T(8,128)(2,1)S(1)}, u32[]{:S(2)}, u32[]{:S(2)}) collective-permute-start(bf16[2,128,128]{2,1,0:T(8,128)(2,1)S(1)} %get-tuple-element.39), channel_id=1, source_target_pairs={{0,16},{4,12},{8,24},{12,4},{16,0},{20,28},{24,8},{28,20},{1,17},{... | collective-permute-start | bytes 196616 | tf_op jit(solution)/shard_map/ppermute | solution.py:266
  14.1 4.3 %collective-permute-start.7 = (bf16[2,128,128]{2,1,0:T(8,128)(2,1)S(1)}, bf16[2,128,128]{2,1,0:T(8,128)(2,1)S(1)}, u32[]{:S(2)}, u32[]{:S(2)}) collective-permute-start(bf16[2,128,128]{2,1,0:T(8,128)(2,1)S(1)} %get-tuple-element.40), channel_id=1, source_target_pairs={{0,8},{4,20},{8,0},{12,28},{16,24},{20,4},{24,16},{28,12},{1,9},{5... | collective-permute-start | bytes 196616 | tf_op jit(solution)/shard_map/ppermute | solution.py:266

commit v6 on v5

--- a/solution.py
+++ b/solution.py
@@ -179,33 +179,24 @@
     return contract(stacked(refs[groups:], 0), scores, 0, 0)
 
 
+def store_queries(result_ref, refs, groups, sizes):
+    group_size, row_count, _ = sizes
+    terms = query_terms(refs, groups, slice(None))
+    for head in range(group_size):
+        rows = slice(head * row_count, (head + 1) * row_count)
+        result_ref[rows, :] = terms[:, rows].T.astype(result_ref.dtype)
+
+
 def back_kernel(sizes, outer_count, groups, *refs):
-    group_size, row_count, _ = sizes
     has_next = lax.axis_index("outer") < outer_count - 1
 
     @pl.when(has_next)
     def _():
-        refs[-1][...] = query_terms(refs[:-1], groups, slice(None)).astype(jnp.bfloat16)
+        store_queries(refs[-1], refs[:-1], groups, sizes)
 
 
 def query_kernel(sizes, groups, *refs):
-    group_size, row_count, head_size = sizes
-    inv_root = 1.0 / math.sqrt(head_size)
-    back_ref, inputs = refs[0], refs[1:-4]
-    result_hbm, total_ref, result_ref, sem = refs[-4:]
-    has_prev = lax.axis_index("outer") > 0
-    total_ref[...] = query_terms(inputs, groups, slice(None))
-
-    @pl.when(has_prev)
-    def _():
-        total_ref[...] += back_ref[...].astype(jnp.float32)
-
-    for head in range(group_size):
-        rows = slice(head * row_count, (head + 1) * row_count)
-        result_ref[rows, :] = (total_ref[:, rows] * inv_root).T.astype(jnp.bfloat16)
-    copy = pltpu.make_async_copy(result_ref, result_hbm, sem)
-    copy.start()
-    copy.wait()
+    store_queries(refs[-1], refs[:-1], groups, sizes)
 
 
 def early_kernel(sizes, *refs):
@@ -218,22 +209,30 @@
         total_ref[which] = total
 
 
-def sum_kernel(*refs):
-    total_ref, returned = refs[0], refs[1:-5]
-    key_hbm, value_hbm, key_ref, value_ref, sems = refs[-5:]
-    key_total = total_ref[0]
-    value_total = total_ref[1]
-    for ref in returned:
-        key_total += ref[0].astype(jnp.float32)
-        value_total += ref[1].astype(jnp.float32)
-    key_ref[...] = key_total.astype(jnp.bfloat16)
-    value_ref[...] = value_total.astype(jnp.bfloat16)
+def late_kernel(*refs):
+    total_ref, returned, sum_ref = refs[0], refs[1:-1], refs[-1]
+    for which in range(2):
+        total = total_ref[which]
+        for ref in returned:
+            total += ref[which].astype(jnp.float32)
+        sum_ref[which] = total.astype(jnp.bfloat16)
+
+
+def final_kernel(
+    sizes, sum_ref, query_ref, back_ref, query_hbm, key_hbm, value_hbm, result_ref, sems
+):
+    inv_root = 1.0 / math.sqrt(sizes[2])
     copies = [
-        pltpu.make_async_copy(key_ref, key_hbm, sems.at[0]),
-        pltpu.make_async_copy(value_ref, value_hbm, sems.at[1]),
+        pltpu.make_async_copy(sum_ref.at[0], key_hbm, sems.at[0]),
+        pltpu.make_async_copy(sum_ref.at[1], value_hbm, sems.at[1]),
+        pltpu.make_async_copy(result_ref, query_hbm, sems.at[2]),
     ]
-    for copy in copies:
-        copy.start()
+    copies[0].start()
+    copies[1].start()
+    has_prev = lax.axis_index("outer") > 0
+    back = jnp.where(has_prev, back_ref[...].astype(jnp.float32), 0.0)
+    result_ref[...] = ((query_ref[...] + back) * inv_root).astype(jnp.bfloat16)
+    copies[2].start()
     for copy in copies:
         copy.wait()
 
@@ -344,16 +343,6 @@
     groups = len(scores)
     returned = [exchange(sums[step], step) for step in away]
 
-    query_next = pl.pallas_call(
-        functools.partial(back_kernel, sizes, outer_count, groups),
-        out_shape=shape((head_size, half), jnp.bfloat16),
-        in_specs=[vmem] * (groups + inner_count),
-        out_specs=vmem,
-        cost_estimate=cost(inner_count),
-        compiler_params=roomy,
-    )(*next_scores, *all_blocks)
-    query_back = to_segment(query_next, 1)
-
     early_total = pl.pallas_call(
         functools.partial(early_kernel, sizes),
         out_shape=shape((2, row_count, head_size), jnp.float32),
@@ -362,35 +351,48 @@
         cost_estimate=cost(8 * inner_count),
         compiler_params=roomy,
     )(own_total, *returned[:middle])
-    early_total, scores[0] = lax.optimization_barrier((early_total, scores[0]))
-
-    query_out = pl.pallas_call(
+    early_total, next_scores[0] = lax.optimization_barrier((early_total, next_scores[0]))
+
+    query_next = pl.pallas_call(
+        functools.partial(back_kernel, sizes, outer_count, groups),
+        out_shape=shape((half, head_size), jnp.bfloat16),
+        in_specs=[vmem] * (groups + inner_count),
+        out_specs=vmem,
+        cost_estimate=cost(0, 0),
+        compiler_params=roomy,
+    )(*next_scores, *all_blocks)
+    query_back = to_segment(query_next, 1)
+
+    query_own = pl.pallas_call(
         functools.partial(query_kernel, sizes, groups),
-        out_shape=shape((half, head_size), jnp.bfloat16),
-        in_specs=[vmem] * (1 + groups + inner_count),
-        out_specs=hbm,
-        scratch_shapes=[
-            pltpu.VMEM((head_size, half), jnp.float32),
-            pltpu.VMEM((half, head_size), jnp.bfloat16),
-            pltpu.SemaphoreType.DMA,
-        ],
-        cost_estimate=cost(inner_count),
-        compiler_params=roomy,
-    )(query_back, *scores, *all_blocks)
-
-    early_total, query_out = lax.optimization_barrier((early_total, query_out))
-    key_out, value_out = pl.pallas_call(
-        sum_kernel,
-        out_shape=(shape((row_count, head_size), jnp.bfloat16),) * 2,
+        out_shape=shape((half, head_size), jnp.float32),
+        in_specs=[vmem] * (groups + inner_count),
+        out_specs=vmem,
+        cost_estimate=cost(0, 0),
+        compiler_params=roomy,
+    )(*scores, *all_blocks)
+
+    late_sum = pl.pallas_call(
+        late_kernel,
+        out_shape=block_shape,
         in_specs=[vmem] * (1 + len(away) - middle),
-        out_specs=(hbm, hbm),
-        scratch_shapes=[
-            pltpu.VMEM((row_count, head_size), jnp.bfloat16),
-            pltpu.VMEM((row_count, head_size), jnp.bfloat16),
-            pltpu.SemaphoreType.DMA((2,)),
-        ],
+        out_specs=vmem,
+        cost_estimate=cost(8 * inner_count),
         compiler_params=roomy,
     )(early_total, *returned[middle:])
+
+    query_out, key_out, value_out = pl.pallas_call(
+        functools.partial(final_kernel, sizes),
+        out_shape=(
+            shape((half, head_size), jnp.bfloat16),
+            shape((row_count, head_size), jnp.bfloat16),
+            shape((row_count, head_size), jnp.bfloat16),
+        ),
+        in_specs=[vmem] * 3,
+        out_specs=(hbm,) * 3,
+        scratch_shapes=[pltpu.VMEM((half, head_size), jnp.bfloat16), pltpu.SemaphoreType.DMA((3,))],
+        compiler_params=roomy,
+    )(late_sum, query_own, query_back)
     grad_queries = jnp.swapaxes(query_out.reshape(group_size, row_count, head_size), 0, 1)
     return (grad_queries, key_out[:, None, :], value_out[:, None, :])
 

time: 19.2 us -> 18.9 us (0.984)
  Pallas kernels: 5.98 us -> 5.47 us
  waiting for transfers between devices: 3.76 us -> 3.99 us
    ppermute x6, waiting for transfers between devices: 3.16 us -> 3.98 us  [exchange(): return lax.ppermute(block, ('inner', 'outer'), route)]
    pallas_call x1, Pallas kernels: 1.13 us -> 0.41 us  [on_device(): pl.pallas_call(functools.partial(query_kernel, sizes, groups), out_shape=...]
    ppermute x2, waiting for transfers between devices: 0.6 us -> 0.01 us  [to_segment(): return lax.ppermute(block, 'outer', route)]
    pallas_call x1 -> x2, Pallas kernels: 0.66 us -> 0.8 us  [the longest x1 0.77 us: on_device(): pl.pallas_call(functools.partial(final_kernel, sizes), out_shape=(shape((...]
  transfers between devices with their start and end apart: 8 -> 8, of which waited for: 4 -> 4; matrix products, arithmetic and copies ran while one was open for 0% -> 0% of each run, Pallas kernels for 22% -> 19%
where the time goes in v6:
time: 18.9 us; the launch traced here: 18.7 us
  starting transfers between devices  8.58 us (45%)
  Pallas kernels  5.47 us (29%)
  waiting for transfers between devices  3.99 us (21%)
  between operations  0.7 us (4%)
    ppermute x6, starting transfers between devices, exchange(): return lax.ppermute(block, ('inner', 'outer'), route)  7.99 us
    ppermute x6, waiting for transfers between devices, exchange(): return lax.ppermute(block, ('inner', 'outer'), route)  3.98 us
    pallas_call x2, Pallas kernels, on_device(): pl.pallas_call(functools.partial(far_kernel, sizes, inner_count, steps),...  1.66 us
    pallas_call x1, Pallas kernels, on_device(): pl.pallas_call(functools.partial(load_kernel, sizes), out_shape=(block_sh...  1.22 us
    pallas_call x1, Pallas kernels, on_device(): pl.pallas_call(functools.partial(near_kernel, sizes, inner_count, outer_c...  0.96 us
    pallas_call x1, Pallas kernels, on_device(): pl.pallas_call(functools.partial(final_kernel, sizes), out_shape=(shape((...  0.77 us
    ppermute x2, starting transfers between devices, to_segment(): return lax.ppermute(block, 'outer', route)  0.59 us
    pallas_call x1, Pallas kernels, on_device(): pl.pallas_call(functools.partial(query_kernel, sizes, groups), out_shape=...  0.41 us
  transfers between devices with their start and end apart: 8, of which 4 were waited for; matrix products, arithmetic and copies ran while one was open for 0% of the time, Pallas kernels for 19%

profile of v6, /device:TPU:0, one launch (start us, length us, event | category | flops | bytes accessed | tf_op | source)
XLA Modules:
  0.0 18.7 jit_solution(11189817546043947951)
XLA Ops:
  0.6 1.2 %shard_map.94 = (bf16[2,128,128]{2,1,0:T(8,128)(2,1)S(1)}, bf16[2352,128]{1,0:T(8,128)(2,1)S(1)}) custom-call(bf16[768,128]{1,0:T(8,128)(2,1)} %bitcast.16, bf16[768,128]{1,0:T(8,128)(2,1)} %bitcast.17, bf16[768,128]{1,0:T(8,128)(2,1)} %bitcast.18, f32[6,128]{1,0:T(8,128)} %norm_hbm.1, bf16[128,128]{1,0:T(8,128)(2,1)} %bitcast.19, bf16[128,128]{1,0:T(8,128)(2,1)} %bitcast.20), custom_call_target="tpu_custom_call" | custom-call | bytes 1048576 | tf_op jit(solution)/shard_map/pallas_call | solution.py:282
  1.9 0.5 %collective-permute-start = (bf16[2352,128]{1,0:T(8,128)(2,1)S(1)}, bf16[2352,128]{1,0:T(8,128)(2,1)S(1)}, u32[]{:S(2)}, u32[]{:S(2)}) collective-permute-start(bf16[2352,128]{1,0:T(8,128)(2,1)S(1)} %get-tuple-element.22.packet_ref), channel_id=1, source_target_pairs={{0,4},{4,0},{1,5},{5,1},{2,6},{6,2},{3,7},{7,3},{8,12},{12,8},{9,1... | collective-permute-start | bytes 1806344 | tf_op jit(solution)/shard_map/ppermute | solution.py:257
  2.4 3.5 %collective-permute-start.1 = (bf16[2,128,128]{2,1,0:T(8,128)(2,1)S(1)}, bf16[2,128,128]{2,1,0:T(8,128)(2,1)S(1)}, u32[]{:S(2)}, u32[]{:S(2)}) collective-permute-start(bf16[2,128,128]{2,1,0:T(8,128)(2,1)S(1)} %get-tuple-element.23.pair_ref.refs_3_), channel_id=1, source_target_pairs={{0,24},{4,28},{8,16},{12,20},{16,8},{20,12},{24,0},{28,4},{1,25},{... | collective-permute-start | bytes 196616 | tf_op jit(solution)/shard_map/ppermute | solution.py:265
  5.9 0.5 %collective-permute-start.3 = (bf16[2,128,128]{2,1,0:T(8,128)(2,1)S(1)}, bf16[2,128,128]{2,1,0:T(8,128)(2,1)S(1)}, u32[]{:S(2)}, u32[]{:S(2)}) collective-permute-start(bf16[2,128,128]{2,1,0:T(8,128)(2,1)S(1)} %get-tuple-element.23.pair_ref.refs_3_), channel_id=1, source_target_pairs={{0,8},{4,20},{8,0},{12,28},{16,24},{20,4},{24,16},{28,12},{1,9},{5... | collective-permute-start | bytes 196616 | tf_op jit(solution)/shard_map/ppermute | solution.py:265
  6.4 0.1 collective-permute-start.4
  6.5 0.0 collective-permute-done.next_ref
  6.5 1.0 %shard_map.95 = (bf16[128,768]{1,0:T(8,128)(2,1)S(1)}, bf16[128,768]{1,0:T(8,128)(2,1)S(1)}, f32[2,128,128]{2,1,0:T(8,128)S(1)}, f32[2,16,128]{2,1,0:T(8,128)S(1)}, s32[8,128]{1,0:T(8,128)S(1)}) custom-call(bf16[2352,128]{1,0:T(8,128)(2,1)S(1)} %get-tuple-element.22.packet_ref, bf16[2352,128]{1,0:T(8,128)(2,1)S(1)} %collective-permute-done.next_ref, ...), custom_call_target="tpu_custom_call" | custom-call | flops 251658240 | bytes 1048576 | tf_op jit(solution)/shard_map/pallas_call | solution.py:309
  7.5 1.1 %collective-permute-done.1.refs_0_.refs_4_ = bf16[2,128,128]{2,1,0:T(8,128)(2,1)S(1)} collective-permute-done((bf16[2,128,128]{2,1,0:T(8,128)(2,1)S(1)}, bf16[2,128,128]{2,1,0:T(8,128)(2,1)S(1)}, u32[]{:S(2)}, u32[]{:S(2)}) %collective-permute-start.1) | collective-permute-done | bytes 65568 | tf_op jit(solution)/shard_map/ppermute | solution.py:265
  8.6 0.7 %shard_map.96 = (bf16[128,768]{1,0:T(8,128)(2,1)S(1)}, bf16[128,768]{1,0:T(8,128)(2,1)S(1)}, bf16[2,128,128]{2,1,0:T(8,128)(2,1)S(1)}) custom-call(bf16[2352,128]{1,0:T(8,128)(2,1)S(1)} %get-tuple-element.22.packet_ref, bf16[2352,128]{1,0:T(8,128)(2,1)S(1)} %collective-permute-done.next_ref, s32[8,128]{1,0:T(8,128)S(1)} %get-tuple-element.25.rank_ref, ...), custom_call_target="tpu_custom_call" | custom-call | flops 251658240 | bytes 1048576 | tf_op jit(solution)/shard_map/pallas_call | solution.py:330
  9.2 3.2 %collective-permute-start.2 = (bf16[2,128,128]{2,1,0:T(8,128)(2,1)S(1)}, bf16[2,128,128]{2,1,0:T(8,128)(2,1)S(1)}, u32[]{:S(2)}, u32[]{:S(2)}) collective-permute-start(bf16[2,128,128]{2,1,0:T(8,128)(2,1)S(1)} %get-tuple-element.27), channel_id=1, source_target_pairs={{0,24},{4,28},{8,16},{12,20},{16,8},{20,12},{24,0},{28,4},{1,25},{... | collective-permute-start | bytes 196616 | tf_op jit(solution)/shard_map/ppermute | solution.py:265
  12.4 0.0 collective-permute-done.3.refs_0_.refs_5_
  12.4 0.0 collective-permute-done.4.refs_1_.refs_6_
  12.4 1.0 %shard_map.98 = (bf16[256,768]{1,0:T(8,128)(2,1)S(1)}, bf16[256,768]{1,0:T(8,128)(2,1)S(1)}, bf16[2,128,128]{2,1,0:T(8,128)(2,1)S(1)}, bf16[2,128,128]{2,1,0:T(8,128)(2,1)S(1)}) custom-call(bf16[2352,128]{1,0:T(8,128)(2,1)S(1)} %get-tuple-element.22.packet_ref, bf16[2352,128]{1,0:T(8,128)(2,1)S(1)} %collective-permute-done.next_ref, ...), custom_call_target="tpu_custom_call" | custom-call | flops 503316480 | bytes 1048576 | tf_op jit(solution)/shard_map/pallas_call | solution.py:330
  13.4 0.2 %collective-permute-start.5 = (bf16[2,128,128]{2,1,0:T(8,128)(2,1)S(1)}, bf16[2,128,128]{2,1,0:T(8,128)(2,1)S(1)}, u32[]{:S(2)}, u32[]{:S(2)}) collective-permute-start(bf16[2,128,128]{2,1,0:T(8,128)(2,1)S(1)} %get-tuple-element.30), channel_id=1, source_target_pairs={{0,16},{4,12},{8,24},{12,4},{16,0},{20,28},{24,8},{28,20},{1,17},{... | collective-permute-start | bytes 196616 | tf_op jit(solution)/shard_map/ppermute | solution.py:265
  13.7 0.4 %collective-permute-start.6 = (bf16[2,128,128]{2,1,0:T(8,128)(2,1)S(1)}, bf16[2,128,128]{2,1,0:T(8,128)(2,1)S(1)}, u32[]{:S(2)}, u32[]{:S(2)}) collective-permute-start(bf16[2,128,128]{2,1,0:T(8,128)(2,1)S(1)} %get-tuple-element.31), channel_id=1, source_target_pairs={{0,8},{4,20},{8,0},{12,28},{16,24},{20,4},{24,16},{28,12},{1,9},{5... | collective-permute-start | bytes 196616 | tf_op jit(solution)/shard_map/ppermute | solution.py:265
  14.1 0.4 %shard_map.100.query_ref = f32[768,128]{1,0:T(8,128)S(1)} custom-call(bf16[128,768]{1,0:T(8,128)(2,1)S(1)} %get-tuple-element.32.refs_0_, bf16[128,768]{1,0:T(8,128)(2,1)S(1)} %get-tuple-element.33.refs_1_, bf16[256,768]{1,0:T(8,128)(2,1)S(1)} %get-tuple-element.34.refs_2_, bf16[2,128,128]{2,1,0:T(8,128)(2,1)S(1)} %get-tuple-element.23.pair_ref.refs_3_, ...), custom_call_target="tpu_custom_call" | custom-call | tf_op jit(solution)/shard_map/pallas_call | solution.py:366
  14.5 0.2 collective-permute-done.2.refs_1_
  14.7 0.4 %shard_map.101 = bf16[768,128]{1,0:T(8,128)(2,1)S(1)} custom-call(bf16[128,768]{1,0:T(8,128)(2,1)S(1)} %get-tuple-element.35.refs_0_, bf16[128,768]{1,0:T(8,128)(2,1)S(1)} %get-tuple-element.36.refs_1_, bf16[256,768]{1,0:T(8,128)(2,1)S(1)} %get-tuple-element.37.refs_2_, bf16[2,128,128]{2,1,0:T(8,128)(2,1)S(1)} %get-tuple-element.23.pair_ref.refs_3_, ...), custom_call_target="tpu_custom_call" | custom-call | tf_op jit(solution)/shard_map/pallas_call | solution.py:356
  15.1 0.1 collective-permute-start.7
  15.2 2.6 %collective-permute-done.5.refs_1_ = bf16[2,128,128]{2,1,0:T(8,128)(2,1)S(1)} collective-permute-done((bf16[2,128,128]{2,1,0:T(8,128)(2,1)S(1)}, bf16[2,128,128]{2,1,0:T(8,128)(2,1)S(1)}, u32[]{:S(2)}, u32[]{:S(2)}) %collective-permute-start.5) | collective-permute-done | bytes 65568 | tf_op jit(solution)/shard_map/ppermute | solution.py:265
  17.8 0.2 collective-permute-done.6.refs_2_
  18.0 0.0 collective-permute-done.7.back_ref
  18.0 0.8 %shard_map.102 = (bf16[768,128]{1,0:T(8,128)(2,1)}, bf16[128,128]{1,0:T(8,128)(2,1)}, bf16[128,128]{1,0:T(8,128)(2,1)}) custom-call(bf16[2,128,128]{2,1,0:T(8,128)(2,1)S(1)} %shard_map.99.sum_ref, f32[768,128]{1,0:T(8,128)S(1)} %shard_map.100.query_ref, bf16[768,128]{1,0:T(8,128)(2,1)S(1)} %collective-permute-done.7.back_ref), custom_call_target="tpu_custom_call" | custom-call | tf_op jit(solution)/shard_map/pallas_call | solution.py:384
  (2 shorter events, 0.0 us)
Async XLA Ops:
  1.9 4.7 %collective-permute-start = (bf16[2352,128]{1,0:T(8,128)(2,1)S(1)}, bf16[2352,128]{1,0:T(8,128)(2,1)S(1)}, u32[]{:S(2)}, u32[]{:S(2)}) collective-permute-start(bf16[2352,128]{1,0:T(8,128)(2,1)S(1)} %get-tuple-element.22.packet_ref), channel_id=1, source_target_pairs={{0,4},{4,0},{1,5},{5,1},{2,6},{6,2},{3,7},{7,3},{8,12},{12,8},{9,1... | collective-permute-start | bytes 1806344 | tf_op jit(solution)/shard_map/ppermute | solution.py:257
  2.4 6.2 %collective-permute-start.1 = (bf16[2,128,128]{2,1,0:T(8,128)(2,1)S(1)}, bf16[2,128,128]{2,1,0:T(8,128)(2,1)S(1)}, u32[]{:S(2)}, u32[]{:S(2)}) collective-permute-start(bf16[2,128,128]{2,1,0:T(8,128)(2,1)S(1)} %get-tuple-element.23.pair_ref.refs_3_), channel_id=1, source_target_pairs={{0,24},{4,28},{8,16},{12,20},{16,8},{20,12},{24,0},{28,4},{1,25},{... | collective-permute-start | bytes 196616 | tf_op jit(solution)/shard_map/ppermute | solution.py:265
  5.9 6.5 %collective-permute-start.3 = (bf16[2,128,128]{2,1,0:T(8,128)(2,1)S(1)}, bf16[2,128,128]{2,1,0:T(8,128)(2,1)S(1)}, u32[]{:S(2)}, u32[]{:S(2)}) collective-permute-start(bf16[2,128,128]{2,1,0:T(8,128)(2,1)S(1)} %get-tuple-element.23.pair_ref.refs_3_), channel_id=1, source_target_pairs={{0,8},{4,20},{8,0},{12,28},{16,24},{20,4},{24,16},{28,12},{1,9},{5... | collective-permute-start | bytes 196616 | tf_op jit(solution)/shard_map/ppermute | solution.py:265
  6.4 6.0 %collective-permute-start.4 = (bf16[2,128,128]{2,1,0:T(8,128)(2,1)S(1)}, bf16[2,128,128]{2,1,0:T(8,128)(2,1)S(1)}, u32[]{:S(2)}, u32[]{:S(2)}) collective-permute-start(bf16[2,128,128]{2,1,0:T(8,128)(2,1)S(1)} %get-tuple-element.23.pair_ref.refs_3_), channel_id=1, source_target_pairs={{0,16},{4,12},{8,24},{12,4},{16,0},{20,28},{24,8},{28,20},{1,17},{... | collective-permute-start | bytes 196616 | tf_op jit(solution)/shard_map/ppermute | solution.py:265
  9.2 5.4 %collective-permute-start.2 = (bf16[2,128,128]{2,1,0:T(8,128)(2,1)S(1)}, bf16[2,128,128]{2,1,0:T(8,128)(2,1)S(1)}, u32[]{:S(2)}, u32[]{:S(2)}) collective-permute-start(bf16[2,128,128]{2,1,0:T(8,128)(2,1)S(1)} %get-tuple-element.27), channel_id=1, source_target_pairs={{0,24},{4,28},{8,16},{12,20},{16,8},{20,12},{24,0},{28,4},{1,25},{... | collective-permute-start | bytes 196616 | tf_op jit(solution)/shard_map/ppermute | solution.py:265
  13.4 4.3 %collective-permute-start.5 = (bf16[2,128,128]{2,1,0:T(8,128)(2,1)S(1)}, bf16[2,128,128]{2,1,0:T(8,128)(2,1)S(1)}, u32[]{:S(2)}, u32[]{:S(2)}) collective-permute-start(bf16[2,128,128]{2,1,0:T(8,128)(2,1)S(1)} %get-tuple-element.30), channel_id=1, source_target_pairs={{0,16},{4,12},{8,24},{12,4},{16,0},{20,28},{24,8},{28,20},{1,17},{... | collective-permute-start | bytes 196616 | tf_op jit(solution)/shard_map/ppermute | solution.py:265
  13.7 4.3 %collective-permute-start.6 = (bf16[2,128,128]{2,1,0:T(8,128)(2,1)S(1)}, bf16[2,128,128]{2,1,0:T(8,128)(2,1)S(1)}, u32[]{:S(2)}, u32[]{:S(2)}) collective-permute-start(bf16[2,128,128]{2,1,0:T(8,128)(2,1)S(1)} %get-tuple-element.31), channel_id=1, source_target_pairs={{0,8},{4,20},{8,0},{12,28},{16,24},{20,4},{24,16},{28,12},{1,9},{5... | collective-permute-start | bytes 196616 | tf_op jit(solution)/shard_map/ppermute | solution.py:265
  15.1 2.9 %collective-permute-start.7 = (bf16[768,128]{1,0:T(8,128)(2,1)S(1)}, bf16[768,128]{1,0:T(8,128)(2,1)S(1)}, u32[]{:S(2)}, u32[]{:S(2)}) collective-permute-start(bf16[768,128]{1,0:T(8,128)(2,1)S(1)} %shard_map.101), channel_id=1, source_target_pairs={{0,4},{4,0},{1,5},{5,1},{2,6},{6,2},{3,7},{7,3},{8,12},{12,8},{9,1... | collective-permute-start | bytes 589832 | tf_op jit(solution)/shard_map/ppermute | solution.py:257

commit v7 on v6

--- a/solution.py
+++ b/solution.py
@@ -25,9 +25,10 @@
 
 
 def peer_offset(step, outer, inner_count):
-    bits = inner_count.bit_length() - 1
-    turn = outer % 2
-    return ((step << turn) | (step >> (bits - turn))) & (inner_count - 1)
+    if step == 0 or outer % 2 == 0:
+        return step
+    order = [inner_count - 1] + list(range(1, inner_count - 1))
+    return order[order.index(step) - 1]
 
 
 def load_kernel(

time: 18.9 us -> 18.9 us (level)
  waiting for transfers between devices: 3.99 us -> 3.7 us
  starting transfers between devices: 8.58 us -> 8.85 us
    ppermute x6, waiting for transfers between devices: 3.98 us -> 3.7 us  [exchange(): return lax.ppermute(block, ('inner', 'outer'), route)]
    ppermute x6, starting transfers between devices: 7.99 us -> 8.26 us  [exchange(): return lax.ppermute(block, ('inner', 'outer'), route)]
where the time goes in v7:
time: 18.9 us; the launch traced here: 18.7 us
  starting transfers between devices  8.85 us (47%)
  Pallas kernels  5.47 us (29%)
  waiting for transfers between devices  3.7 us (20%)
  between operations  0.71 us (4%)
    ppermute x6, starting transfers between devices, exchange(): return lax.ppermute(block, ('inner', 'outer'), route)  8.26 us
    ppermute x6, waiting for transfers between devices, exchange(): return lax.ppermute(block, ('inner', 'outer'), route)  3.7 us
    pallas_call x2, Pallas kernels, on_device(): pl.pallas_call(functools.partial(far_kernel, sizes, inner_count, steps),...  1.66 us
    pallas_call x1, Pallas kernels, on_device(): pl.pallas_call(functools.partial(load_kernel, sizes), out_shape=(block_sh...  1.22 us
    pallas_call x1, Pallas kernels, on_device(): pl.pallas_call(functools.partial(near_kernel, sizes, inner_count, outer_c...  0.97 us
    pallas_call x1, Pallas kernels, on_device(): pl.pallas_call(functools.partial(final_kernel, sizes), out_shape=(shape((...  0.77 us
    ppermute x2, starting transfers between devices, to_segment(): return lax.ppermute(block, 'outer', route)  0.59 us
    pallas_call x1, Pallas kernels, on_device(): pl.pallas_call(functools.partial(query_kernel, sizes, groups), out_shape=...  0.41 us
  transfers between devices with their start and end apart: 8, of which 4 were waited for; matrix products, arithmetic and copies ran while one was open for 0% of the time, Pallas kernels for 19%

profile of v7, /device:TPU:0, one launch (start us, length us, event | category | flops | bytes accessed | tf_op | source)
XLA Modules:
  0.0 18.7 jit_solution(11242785146380371738)
XLA Ops:
  0.6 1.2 %shard_map.94 = (bf16[2,128,128]{2,1,0:T(8,128)(2,1)S(1)}, bf16[2352,128]{1,0:T(8,128)(2,1)S(1)}) custom-call(bf16[768,128]{1,0:T(8,128)(2,1)} %bitcast.16, bf16[768,128]{1,0:T(8,128)(2,1)} %bitcast.17, bf16[768,128]{1,0:T(8,128)(2,1)} %bitcast.18, f32[6,128]{1,0:T(8,128)} %norm_hbm.1, bf16[128,128]{1,0:T(8,128)(2,1)} %bitcast.19, bf16[128,128]{1,0:T(8,128)(2,1)} %bitcast.20), custom_call_target="tpu_custom_call" | custom-call | bytes 1048576 | tf_op jit(solution)/shard_map/pallas_call | solution.py:283
  1.9 0.5 %collective-permute-start = (bf16[2352,128]{1,0:T(8,128)(2,1)S(1)}, bf16[2352,128]{1,0:T(8,128)(2,1)S(1)}, u32[]{:S(2)}, u32[]{:S(2)}) collective-permute-start(bf16[2352,128]{1,0:T(8,128)(2,1)S(1)} %get-tuple-element.22.packet_ref), channel_id=1, source_target_pairs={{0,4},{4,0},{1,5},{5,1},{2,6},{6,2},{3,7},{7,3},{8,12},{12,8},{9,1... | collective-permute-start | bytes 1806344 | tf_op jit(solution)/shard_map/ppermute | solution.py:258
  2.4 3.5 %collective-permute-start.1 = (bf16[2,128,128]{2,1,0:T(8,128)(2,1)S(1)}, bf16[2,128,128]{2,1,0:T(8,128)(2,1)S(1)}, u32[]{:S(2)}, u32[]{:S(2)}) collective-permute-start(bf16[2,128,128]{2,1,0:T(8,128)(2,1)S(1)} %get-tuple-element.23.pair_ref.refs_3_), channel_id=1, source_target_pairs={{0,24},{4,20},{8,16},{12,28},{16,8},{20,4},{24,0},{28,12},{1,25},{... | collective-permute-start | bytes 196616 | tf_op jit(solution)/shard_map/ppermute | solution.py:266
  5.9 0.5 %collective-permute-start.3 = (bf16[2,128,128]{2,1,0:T(8,128)(2,1)S(1)}, bf16[2,128,128]{2,1,0:T(8,128)(2,1)S(1)}, u32[]{:S(2)}, u32[]{:S(2)}) collective-permute-start(bf16[2,128,128]{2,1,0:T(8,128)(2,1)S(1)} %get-tuple-element.23.pair_ref.refs_3_), channel_id=1, source_target_pairs={{0,8},{4,28},{8,0},{12,20},{16,24},{20,12},{24,16},{28,4},{1,9},{5... | collective-permute-start | bytes 196616 | tf_op jit(solution)/shard_map/ppermute | solution.py:266
  6.4 0.1 collective-permute-start.4
  6.5 0.0 collective-permute-done.next_ref
  6.5 1.0 %shard_map.95 = (bf16[128,768]{1,0:T(8,128)(2,1)S(1)}, bf16[128,768]{1,0:T(8,128)(2,1)S(1)}, f32[2,128,128]{2,1,0:T(8,128)S(1)}, f32[2,16,128]{2,1,0:T(8,128)S(1)}, s32[8,128]{1,0:T(8,128)S(1)}) custom-call(bf16[2352,128]{1,0:T(8,128)(2,1)S(1)} %get-tuple-element.22.packet_ref, bf16[2352,128]{1,0:T(8,128)(2,1)S(1)} %collective-permute-done.next_ref, ...), custom_call_target="tpu_custom_call" | custom-call | flops 251658240 | bytes 1048576 | tf_op jit(solution)/shard_map/pallas_call | solution.py:310
  7.5 0.9 %collective-permute-done.1.refs_0_.refs_4_ = bf16[2,128,128]{2,1,0:T(8,128)(2,1)S(1)} collective-permute-done((bf16[2,128,128]{2,1,0:T(8,128)(2,1)S(1)}, bf16[2,128,128]{2,1,0:T(8,128)(2,1)S(1)}, u32[]{:S(2)}, u32[]{:S(2)}) %collective-permute-start.1) | collective-permute-done | bytes 65568 | tf_op jit(solution)/shard_map/ppermute | solution.py:266
  8.4 0.7 %shard_map.96 = (bf16[128,768]{1,0:T(8,128)(2,1)S(1)}, bf16[128,768]{1,0:T(8,128)(2,1)S(1)}, bf16[2,128,128]{2,1,0:T(8,128)(2,1)S(1)}) custom-call(bf16[2352,128]{1,0:T(8,128)(2,1)S(1)} %get-tuple-element.22.packet_ref, bf16[2352,128]{1,0:T(8,128)(2,1)S(1)} %collective-permute-done.next_ref, s32[8,128]{1,0:T(8,128)S(1)} %get-tuple-element.25.rank_ref, ...), custom_call_target="tpu_custom_call" | custom-call | flops 251658240 | bytes 1048576 | tf_op jit(solution)/shard_map/pallas_call | solution.py:331
  9.0 3.4 %collective-permute-start.2 = (bf16[2,128,128]{2,1,0:T(8,128)(2,1)S(1)}, bf16[2,128,128]{2,1,0:T(8,128)(2,1)S(1)}, u32[]{:S(2)}, u32[]{:S(2)}) collective-permute-start(bf16[2,128,128]{2,1,0:T(8,128)(2,1)S(1)} %get-tuple-element.27), channel_id=1, source_target_pairs={{0,24},{4,20},{8,16},{12,28},{16,8},{20,4},{24,0},{28,12},{1,25},{... | collective-permute-start | bytes 196616 | tf_op jit(solution)/shard_map/ppermute | solution.py:266
  12.5 0.0 collective-permute-done.3.refs_0_.refs_5_
  12.5 0.0 collective-permute-done.4.refs_1_.refs_6_
  12.5 1.0 %shard_map.98 = (bf16[256,768]{1,0:T(8,128)(2,1)S(1)}, bf16[256,768]{1,0:T(8,128)(2,1)S(1)}, bf16[2,128,128]{2,1,0:T(8,128)(2,1)S(1)}, bf16[2,128,128]{2,1,0:T(8,128)(2,1)S(1)}) custom-call(bf16[2352,128]{1,0:T(8,128)(2,1)S(1)} %get-tuple-element.22.packet_ref, bf16[2352,128]{1,0:T(8,128)(2,1)S(1)} %collective-permute-done.next_ref, ...), custom_call_target="tpu_custom_call" | custom-call | flops 503316480 | bytes 1048576 | tf_op jit(solution)/shard_map/pallas_call | solution.py:331
  13.5 0.1 collective-permute-start.5
  13.6 0.6 %collective-permute-start.6 = (bf16[2,128,128]{2,1,0:T(8,128)(2,1)S(1)}, bf16[2,128,128]{2,1,0:T(8,128)(2,1)S(1)}, u32[]{:S(2)}, u32[]{:S(2)}) collective-permute-start(bf16[2,128,128]{2,1,0:T(8,128)(2,1)S(1)} %get-tuple-element.31), channel_id=1, source_target_pairs={{0,8},{4,28},{8,0},{12,20},{16,24},{20,12},{24,16},{28,4},{1,9},{5... | collective-permute-start | bytes 196616 | tf_op jit(solution)/shard_map/ppermute | solution.py:266
  14.2 0.4 %shard_map.100.query_ref = f32[768,128]{1,0:T(8,128)S(1)} custom-call(bf16[128,768]{1,0:T(8,128)(2,1)S(1)} %get-tuple-element.32.refs_0_, bf16[128,768]{1,0:T(8,128)(2,1)S(1)} %get-tuple-element.33.refs_1_, bf16[256,768]{1,0:T(8,128)(2,1)S(1)} %get-tuple-element.34.refs_2_, bf16[2,128,128]{2,1,0:T(8,128)(2,1)S(1)} %get-tuple-element.23.pair_ref.refs_3_, ...), custom_call_target="tpu_custom_call" | custom-call | tf_op jit(solution)/shard_map/pallas_call | solution.py:367
  14.6 0.6 %collective-permute-done.2.refs_1_ = bf16[2,128,128]{2,1,0:T(8,128)(2,1)S(1)} collective-permute-done((bf16[2,128,128]{2,1,0:T(8,128)(2,1)S(1)}, bf16[2,128,128]{2,1,0:T(8,128)(2,1)S(1)}, u32[]{:S(2)}, u32[]{:S(2)}) %collective-permute-start.2) | collective-permute-done | bytes 65568 | tf_op jit(solution)/shard_map/ppermute | solution.py:266
  15.2 0.4 %shard_map.101 = bf16[768,128]{1,0:T(8,128)(2,1)S(1)} custom-call(bf16[128,768]{1,0:T(8,128)(2,1)S(1)} %get-tuple-element.35.refs_0_, bf16[128,768]{1,0:T(8,128)(2,1)S(1)} %get-tuple-element.36.refs_1_, bf16[256,768]{1,0:T(8,128)(2,1)S(1)} %get-tuple-element.37.refs_2_, bf16[2,128,128]{2,1,0:T(8,128)(2,1)S(1)} %get-tuple-element.23.pair_ref.refs_3_, ...), custom_call_target="tpu_custom_call" | custom-call | tf_op jit(solution)/shard_map/pallas_call | solution.py:357
  15.6 0.1 collective-permute-start.7
  15.7 2.2 %collective-permute-done.5.refs_1_ = bf16[2,128,128]{2,1,0:T(8,128)(2,1)S(1)} collective-permute-done((bf16[2,128,128]{2,1,0:T(8,128)(2,1)S(1)}, bf16[2,128,128]{2,1,0:T(8,128)(2,1)S(1)}, u32[]{:S(2)}, u32[]{:S(2)}) %collective-permute-start.5) | collective-permute-done | bytes 65568 | tf_op jit(solution)/shard_map/ppermute | solution.py:266
  17.8 0.1 collective-permute-done.6.refs_2_
  17.9 0.0 collective-permute-done.7.back_ref
  18.0 0.8 %shard_map.102 = (bf16[768,128]{1,0:T(8,128)(2,1)}, bf16[128,128]{1,0:T(8,128)(2,1)}, bf16[128,128]{1,0:T(8,128)(2,1)}) custom-call(bf16[2,128,128]{2,1,0:T(8,128)(2,1)S(1)} %shard_map.99.sum_ref, f32[768,128]{1,0:T(8,128)S(1)} %shard_map.100.query_ref, bf16[768,128]{1,0:T(8,128)(2,1)S(1)} %collective-permute-done.7.back_ref), custom_call_target="tpu_custom_call" | custom-call | tf_op jit(solution)/shard_map/pallas_call | solution.py:385
  (2 shorter events, 0.0 us)
Async XLA Ops:
  1.9 4.7 %collective-permute-start = (bf16[2352,128]{1,0:T(8,128)(2,1)S(1)}, bf16[2352,128]{1,0:T(8,128)(2,1)S(1)}, u32[]{:S(2)}, u32[]{:S(2)}) collective-permute-start(bf16[2352,128]{1,0:T(8,128)(2,1)S(1)} %get-tuple-element.22.packet_ref), channel_id=1, source_target_pairs={{0,4},{4,0},{1,5},{5,1},{2,6},{6,2},{3,7},{7,3},{8,12},{12,8},{9,1... | collective-permute-start | bytes 1806344 | tf_op jit(solution)/shard_map/ppermute | solution.py:258
  2.4 6.0 %collective-permute-start.1 = (bf16[2,128,128]{2,1,0:T(8,128)(2,1)S(1)}, bf16[2,128,128]{2,1,0:T(8,128)(2,1)S(1)}, u32[]{:S(2)}, u32[]{:S(2)}) collective-permute-start(bf16[2,128,128]{2,1,0:T(8,128)(2,1)S(1)} %get-tuple-element.23.pair_ref.refs_3_), channel_id=1, source_target_pairs={{0,24},{4,20},{8,16},{12,28},{16,8},{20,4},{24,0},{28,12},{1,25},{... | collective-permute-start | bytes 196616 | tf_op jit(solution)/shard_map/ppermute | solution.py:266
  5.9 6.6 %collective-permute-start.3 = (bf16[2,128,128]{2,1,0:T(8,128)(2,1)S(1)}, bf16[2,128,128]{2,1,0:T(8,128)(2,1)S(1)}, u32[]{:S(2)}, u32[]{:S(2)}) collective-permute-start(bf16[2,128,128]{2,1,0:T(8,128)(2,1)S(1)} %get-tuple-element.23.pair_ref.refs_3_), channel_id=1, source_target_pairs={{0,8},{4,28},{8,0},{12,20},{16,24},{20,12},{24,16},{28,4},{1,9},{5... | collective-permute-start | bytes 196616 | tf_op jit(solution)/shard_map/ppermute | solution.py:266
  6.4 6.1 %collective-permute-start.4 = (bf16[2,128,128]{2,1,0:T(8,128)(2,1)S(1)}, bf16[2,128,128]{2,1,0:T(8,128)(2,1)S(1)}, u32[]{:S(2)}, u32[]{:S(2)}) collective-permute-start(bf16[2,128,128]{2,1,0:T(8,128)(2,1)S(1)} %get-tuple-element.23.pair_ref.refs_3_), channel_id=1, source_target_pairs={{0,16},{4,12},{8,24},{12,4},{16,0},{20,28},{24,8},{28,20},{1,17},{... | collective-permute-start | bytes 196616 | tf_op jit(solution)/shard_map/ppermute | solution.py:266
  9.0 6.1 %collective-permute-start.2 = (bf16[2,128,128]{2,1,0:T(8,128)(2,1)S(1)}, bf16[2,128,128]{2,1,0:T(8,128)(2,1)S(1)}, u32[]{:S(2)}, u32[]{:S(2)}) collective-permute-start(bf16[2,128,128]{2,1,0:T(8,128)(2,1)S(1)} %get-tuple-element.27), channel_id=1, source_target_pairs={{0,24},{4,20},{8,16},{12,28},{16,8},{20,4},{24,0},{28,12},{1,25},{... | collective-permute-start | bytes 196616 | tf_op jit(solution)/shard_map/ppermute | solution.py:266
  13.5 4.3 %collective-permute-start.5 = (bf16[2,128,128]{2,1,0:T(8,128)(2,1)S(1)}, bf16[2,128,128]{2,1,0:T(8,128)(2,1)S(1)}, u32[]{:S(2)}, u32[]{:S(2)}) collective-permute-start(bf16[2,128,128]{2,1,0:T(8,128)(2,1)S(1)} %get-tuple-element.30), channel_id=1, source_target_pairs={{0,16},{4,12},{8,24},{12,4},{16,0},{20,28},{24,8},{28,20},{1,17},{... | collective-permute-start | bytes 196616 | tf_op jit(solution)/shard_map/ppermute | solution.py:266
  13.6 4.3 %collective-permute-start.6 = (bf16[2,128,128]{2,1,0:T(8,128)(2,1)S(1)}, bf16[2,128,128]{2,1,0:T(8,128)(2,1)S(1)}, u32[]{:S(2)}, u32[]{:S(2)}) collective-permute-start(bf16[2,128,128]{2,1,0:T(8,128)(2,1)S(1)} %get-tuple-element.31), channel_id=1, source_target_pairs={{0,8},{4,28},{8,0},{12,20},{16,24},{20,12},{24,16},{28,4},{1,9},{5... | collective-permute-start | bytes 196616 | tf_op jit(solution)/shard_map/ppermute | solution.py:266
  15.6 2.4 %collective-permute-start.7 = (bf16[768,128]{1,0:T(8,128)(2,1)S(1)}, bf16[768,128]{1,0:T(8,128)(2,1)S(1)}, u32[]{:S(2)}, u32[]{:S(2)}) collective-permute-start(bf16[768,128]{1,0:T(8,128)(2,1)S(1)} %shard_map.101), channel_id=1, source_target_pairs={{0,4},{4,0},{1,5},{5,1},{2,6},{6,2},{3,7},{7,3},{8,12},{12,8},{9,1... | collective-permute-start | bytes 589832 | tf_op jit(solution)/shard_map/ppermute | solution.py:258

commit v8 on v6

--- a/solution.py
+++ b/solution.py
@@ -25,9 +25,10 @@
 
 
 def peer_offset(step, outer, inner_count):
-    bits = inner_count.bit_length() - 1
-    turn = outer % 2
-    return ((step << turn) | (step >> (bits - turn))) & (inner_count - 1)
+    last = inner_count - 1
+    if outer % 2 == 1:
+        return {0: 0, 1: last}.get(step, step - 1)
+    return {0: 0, 1: last - 1, 2: last}.get(step, step - 2) if last > 1 else step
 
 
 def load_kernel(
@@ -244,7 +245,7 @@
     assert inner_count & (inner_count - 1) == 0 and inner_count > 1
     sizes = (group_size, row_count, head_size)
     half = group_size * row_count
-    away = list(range(inner_count - 1, 0, -1))
+    away = list(range(1, inner_count))
 
     def flat(array):
         return jnp.swapaxes(array, 0, 1).reshape(-1, head_size)
@@ -325,7 +326,7 @@
     scores, next_scores, sums = [near_scores], [near_next_scores], {}
     middle = inner_count // 2 - 1
     held = [0]
-    for steps in (away[:middle][::-1], away[middle:][::-1]):
+    for steps in (away[:middle], away[middle:]):
         if steps:
             far_scores, far_next_scores, *terms = pl.pallas_call(
                 functools.partial(far_kernel, sizes, inner_count, steps),

time: 18.9 us -> 18.9 us (level)
  waiting for transfers between devices: 3.99 us -> 3.01 us
  starting transfers between devices: 8.58 us -> 9.53 us
    ppermute x6, waiting for transfers between devices: 3.98 us -> 3.01 us  [exchange(): return lax.ppermute(block, ('inner', 'outer'), route)]
    ppermute x6, starting transfers between devices: 7.99 us -> 8.94 us  [exchange(): return lax.ppermute(block, ('inner', 'outer'), route)]
  transfers between devices with their start and end apart: 8 -> 8, of which waited for: 4 -> 2; matrix products, arithmetic and copies ran while one was open for 0% -> 0% of each run, Pallas kernels for 19% -> 19%
where the time goes in v8:
time: 18.9 us; the launch traced here: 18.7 us
  starting transfers between devices  9.53 us (50%)
  Pallas kernels  5.47 us (29%)
  waiting for transfers between devices  3.01 us (16%)
  between operations  0.72 us (4%)
    ppermute x6, starting transfers between devices, exchange(): return lax.ppermute(block, ('inner', 'outer'), route)  8.94 us
    ppermute x6, waiting for transfers between devices, exchange(): return lax.ppermute(block, ('inner', 'outer'), route)  3.01 us
    pallas_call x2, Pallas kernels, on_device(): pl.pallas_call(functools.partial(far_kernel, sizes, inner_count, steps),...  1.66 us
    pallas_call x1, Pallas kernels, on_device(): pl.pallas_call(functools.partial(load_kernel, sizes), out_shape=(block_sh...  1.22 us
    pallas_call x1, Pallas kernels, on_device(): pl.pallas_call(functools.partial(near_kernel, sizes, inner_count, outer_c...  0.97 us
    pallas_call x1, Pallas kernels, on_device(): pl.pallas_call(functools.partial(final_kernel, sizes), out_shape=(shape((...  0.77 us
    ppermute x2, starting transfers between devices, to_segment(): return lax.ppermute(block, 'outer', route)  0.59 us
    pallas_call x1, Pallas kernels, on_device(): pl.pallas_call(functools.partial(query_kernel, sizes, groups), out_shape=...  0.41 us
  transfers between devices with their start and end apart: 8, of which 2 were waited for; matrix products, arithmetic and copies ran while one was open for 0% of the time, Pallas kernels for 19%

profile of v8, /device:TPU:0, one launch (start us, length us, event | category | flops | bytes accessed | tf_op | source)
XLA Modules:
  0.0 18.7 jit_solution(15573672795375854936)
XLA Ops:
  0.6 1.2 %shard_map.94 = (bf16[2,128,128]{2,1,0:T(8,128)(2,1)S(1)}, bf16[2352,128]{1,0:T(8,128)(2,1)S(1)}) custom-call(bf16[768,128]{1,0:T(8,128)(2,1)} %bitcast.16, bf16[768,128]{1,0:T(8,128)(2,1)} %bitcast.17, bf16[768,128]{1,0:T(8,128)(2,1)} %bitcast.18, f32[6,128]{1,0:T(8,128)} %norm_hbm.1, bf16[128,128]{1,0:T(8,128)(2,1)} %bitcast.19, bf16[128,128]{1,0:T(8,128)(2,1)} %bitcast.20), custom_call_target="tpu_custom_call" | custom-call | bytes 1048576 | tf_op jit(solution)/shard_map/pallas_call | solution.py:283
  1.9 0.5 %collective-permute-start = (bf16[2352,128]{1,0:T(8,128)(2,1)S(1)}, bf16[2352,128]{1,0:T(8,128)(2,1)S(1)}, u32[]{:S(2)}, u32[]{:S(2)}) collective-permute-start(bf16[2352,128]{1,0:T(8,128)(2,1)S(1)} %get-tuple-element.22.packet_ref), channel_id=1, source_target_pairs={{0,4},{4,0},{1,5},{5,1},{2,6},{6,2},{3,7},{7,3},{8,12},{12,8},{9,1... | collective-permute-start | bytes 1806344 | tf_op jit(solution)/shard_map/ppermute | solution.py:258
  2.4 2.6 %collective-permute-start.1 = (bf16[2,128,128]{2,1,0:T(8,128)(2,1)S(1)}, bf16[2,128,128]{2,1,0:T(8,128)(2,1)S(1)}, u32[]{:S(2)}, u32[]{:S(2)}) collective-permute-start(bf16[2,128,128]{2,1,0:T(8,128)(2,1)S(1)} %get-tuple-element.23.pair_ref.refs_3_), channel_id=1, source_target_pairs={{0,16},{4,28},{8,24},{12,20},{16,0},{20,12},{24,8},{28,4},{1,17},{... | collective-permute-start | bytes 196616 | tf_op jit(solution)/shard_map/ppermute | solution.py:266
  5.0 1.4 %collective-permute-start.3 = (bf16[2,128,128]{2,1,0:T(8,128)(2,1)S(1)}, bf16[2,128,128]{2,1,0:T(8,128)(2,1)S(1)}, u32[]{:S(2)}, u32[]{:S(2)}) collective-permute-start(bf16[2,128,128]{2,1,0:T(8,128)(2,1)S(1)} %get-tuple-element.23.pair_ref.refs_3_), channel_id=1, source_target_pairs={{0,24},{4,12},{8,16},{12,4},{16,8},{20,28},{24,0},{28,20},{1,25},{... | collective-permute-start | bytes 196616 | tf_op jit(solution)/shard_map/ppermute | solution.py:266
  6.4 0.1 collective-permute-start.4
  6.5 0.0 collective-permute-done.next_ref
  6.5 1.0 %shard_map.95 = (bf16[128,768]{1,0:T(8,128)(2,1)S(1)}, bf16[128,768]{1,0:T(8,128)(2,1)S(1)}, f32[2,128,128]{2,1,0:T(8,128)S(1)}, f32[2,16,128]{2,1,0:T(8,128)S(1)}, s32[8,128]{1,0:T(8,128)S(1)}) custom-call(bf16[2352,128]{1,0:T(8,128)(2,1)S(1)} %get-tuple-element.22.packet_ref, bf16[2352,128]{1,0:T(8,128)(2,1)S(1)} %collective-permute-done.next_ref, ...), custom_call_target="tpu_custom_call" | custom-call | flops 251658240 | bytes 1048576 | tf_op jit(solution)/shard_map/pallas_call | solution.py:310
  7.5 0.8 %collective-permute-done.1.refs_0_.refs_4_ = bf16[2,128,128]{2,1,0:T(8,128)(2,1)S(1)} collective-permute-done((bf16[2,128,128]{2,1,0:T(8,128)(2,1)S(1)}, bf16[2,128,128]{2,1,0:T(8,128)(2,1)S(1)}, u32[]{:S(2)}, u32[]{:S(2)}) %collective-permute-start.1) | collective-permute-done | bytes 65568 | tf_op jit(solution)/shard_map/ppermute | solution.py:266
  8.2 0.7 %shard_map.96 = (bf16[128,768]{1,0:T(8,128)(2,1)S(1)}, bf16[128,768]{1,0:T(8,128)(2,1)S(1)}, bf16[2,128,128]{2,1,0:T(8,128)(2,1)S(1)}) custom-call(bf16[2352,128]{1,0:T(8,128)(2,1)S(1)} %get-tuple-element.22.packet_ref, bf16[2352,128]{1,0:T(8,128)(2,1)S(1)} %collective-permute-done.next_ref, s32[8,128]{1,0:T(8,128)S(1)} %get-tuple-element.25.rank_ref, ...), custom_call_target="tpu_custom_call" | custom-call | flops 251658240 | bytes 1048576 | tf_op jit(solution)/shard_map/pallas_call | solution.py:331
  8.9 2.8 %collective-permute-start.2 = (bf16[2,128,128]{2,1,0:T(8,128)(2,1)S(1)}, bf16[2,128,128]{2,1,0:T(8,128)(2,1)S(1)}, u32[]{:S(2)}, u32[]{:S(2)}) collective-permute-start(bf16[2,128,128]{2,1,0:T(8,128)(2,1)S(1)} %get-tuple-element.27), channel_id=1, source_target_pairs={{0,16},{4,28},{8,24},{12,20},{16,0},{20,12},{24,8},{28,4},{1,17},{... | collective-permute-start | bytes 196616 | tf_op jit(solution)/shard_map/ppermute | solution.py:266
  11.7 0.0 collective-permute-done.3.refs_0_.refs_5_
  11.7 0.0 collective-permute-done.4.refs_1_.refs_6_
  11.7 1.0 %shard_map.98 = (bf16[256,768]{1,0:T(8,128)(2,1)S(1)}, bf16[256,768]{1,0:T(8,128)(2,1)S(1)}, bf16[2,128,128]{2,1,0:T(8,128)(2,1)S(1)}, bf16[2,128,128]{2,1,0:T(8,128)(2,1)S(1)}) custom-call(bf16[2352,128]{1,0:T(8,128)(2,1)S(1)} %get-tuple-element.22.packet_ref, bf16[2352,128]{1,0:T(8,128)(2,1)S(1)} %collective-permute-done.next_ref, ...), custom_call_target="tpu_custom_call" | custom-call | flops 503316480 | bytes 1048576 | tf_op jit(solution)/shard_map/pallas_call | solution.py:331
  12.7 0.7 %collective-permute-start.5 = (bf16[2,128,128]{2,1,0:T(8,128)(2,1)S(1)}, bf16[2,128,128]{2,1,0:T(8,128)(2,1)S(1)}, u32[]{:S(2)}, u32[]{:S(2)}) collective-permute-start(bf16[2,128,128]{2,1,0:T(8,128)(2,1)S(1)} %get-tuple-element.30), channel_id=1, source_target_pairs={{0,24},{4,12},{8,16},{12,4},{16,8},{20,28},{24,0},{28,20},{1,25},{... | collective-permute-start | bytes 196616 | tf_op jit(solution)/shard_map/ppermute | solution.py:266
  13.4 1.3 %collective-permute-start.6 = (bf16[2,128,128]{2,1,0:T(8,128)(2,1)S(1)}, bf16[2,128,128]{2,1,0:T(8,128)(2,1)S(1)}, u32[]{:S(2)}, u32[]{:S(2)}) collective-permute-start(bf16[2,128,128]{2,1,0:T(8,128)(2,1)S(1)} %get-tuple-element.31), channel_id=1, source_target_pairs={{0,8},{4,20},{8,0},{12,28},{16,24},{20,4},{24,16},{28,12},{1,9},{5... | collective-permute-start | bytes 196616 | tf_op jit(solution)/shard_map/ppermute | solution.py:266
  14.7 0.4 %shard_map.100.query_ref = f32[768,128]{1,0:T(8,128)S(1)} custom-call(bf16[128,768]{1,0:T(8,128)(2,1)S(1)} %get-tuple-element.32.refs_0_, bf16[128,768]{1,0:T(8,128)(2,1)S(1)} %get-tuple-element.33.refs_1_, bf16[256,768]{1,0:T(8,128)(2,1)S(1)} %get-tuple-element.34.refs_2_, bf16[2,128,128]{2,1,0:T(8,128)(2,1)S(1)} %get-tuple-element.23.pair_ref.refs_3_, ...), custom_call_target="tpu_custom_call" | custom-call | tf_op jit(solution)/shard_map/pallas_call | solution.py:367
  15.1 0.0 collective-permute-done.2.refs_1_
  15.2 0.4 %shard_map.101 = bf16[768,128]{1,0:T(8,128)(2,1)S(1)} custom-call(bf16[128,768]{1,0:T(8,128)(2,1)S(1)} %get-tuple-element.35.refs_0_, bf16[128,768]{1,0:T(8,128)(2,1)S(1)} %get-tuple-element.36.refs_1_, bf16[256,768]{1,0:T(8,128)(2,1)S(1)} %get-tuple-element.37.refs_2_, bf16[2,128,128]{2,1,0:T(8,128)(2,1)S(1)} %get-tuple-element.23.pair_ref.refs_3_, ...), custom_call_target="tpu_custom_call" | custom-call | tf_op jit(solution)/shard_map/pallas_call | solution.py:357
  15.6 0.1 collective-permute-start.7
  15.7 2.2 %collective-permute-done.5.refs_1_ = bf16[2,128,128]{2,1,0:T(8,128)(2,1)S(1)} collective-permute-done((bf16[2,128,128]{2,1,0:T(8,128)(2,1)S(1)}, bf16[2,128,128]{2,1,0:T(8,128)(2,1)S(1)}, u32[]{:S(2)}, u32[]{:S(2)}) %collective-permute-start.5) | collective-permute-done | bytes 65568 | tf_op jit(solution)/shard_map/ppermute | solution.py:266
  17.9 0.0 collective-permute-done.6.refs_2_
  17.9 0.0 collective-permute-done.7.back_ref
  18.0 0.8 %shard_map.102 = (bf16[768,128]{1,0:T(8,128)(2,1)}, bf16[128,128]{1,0:T(8,128)(2,1)}, bf16[128,128]{1,0:T(8,128)(2,1)}) custom-call(bf16[2,128,128]{2,1,0:T(8,128)(2,1)S(1)} %shard_map.99.sum_ref, f32[768,128]{1,0:T(8,128)S(1)} %shard_map.100.query_ref, bf16[768,128]{1,0:T(8,128)(2,1)S(1)} %collective-permute-done.7.back_ref), custom_call_target="tpu_custom_call" | custom-call | tf_op jit(solution)/shard_map/pallas_call | solution.py:385
  (2 shorter events, 0.0 us)
Async XLA Ops:
  1.9 4.7 %collective-permute-start = (bf16[2352,128]{1,0:T(8,128)(2,1)S(1)}, bf16[2352,128]{1,0:T(8,128)(2,1)S(1)}, u32[]{:S(2)}, u32[]{:S(2)}) collective-permute-start(bf16[2352,128]{1,0:T(8,128)(2,1)S(1)} %get-tuple-element.22.packet_ref), channel_id=1, source_target_pairs={{0,4},{4,0},{1,5},{5,1},{2,6},{6,2},{3,7},{7,3},{8,12},{12,8},{9,1... | collective-permute-start | bytes 1806344 | tf_op jit(solution)/shard_map/ppermute | solution.py:258
  2.4 5.9 %collective-permute-start.1 = (bf16[2,128,128]{2,1,0:T(8,128)(2,1)S(1)}, bf16[2,128,128]{2,1,0:T(8,128)(2,1)S(1)}, u32[]{:S(2)}, u32[]{:S(2)}) collective-permute-start(bf16[2,128,128]{2,1,0:T(8,128)(2,1)S(1)} %get-tuple-element.23.pair_ref.refs_3_), channel_id=1, source_target_pairs={{0,16},{4,28},{8,24},{12,20},{16,0},{20,12},{24,8},{28,4},{1,17},{... | collective-permute-start | bytes 196616 | tf_op jit(solution)/shard_map/ppermute | solution.py:266
  5.0 6.7 %collective-permute-start.3 = (bf16[2,128,128]{2,1,0:T(8,128)(2,1)S(1)}, bf16[2,128,128]{2,1,0:T(8,128)(2,1)S(1)}, u32[]{:S(2)}, u32[]{:S(2)}) collective-permute-start(bf16[2,128,128]{2,1,0:T(8,128)(2,1)S(1)} %get-tuple-element.23.pair_ref.refs_3_), channel_id=1, source_target_pairs={{0,24},{4,12},{8,16},{12,4},{16,8},{20,28},{24,0},{28,20},{1,25},{... | collective-permute-start | bytes 196616 | tf_op jit(solution)/shard_map/ppermute | solution.py:266
  6.4 5.3 %collective-permute-start.4 = (bf16[2,128,128]{2,1,0:T(8,128)(2,1)S(1)}, bf16[2,128,128]{2,1,0:T(8,128)(2,1)S(1)}, u32[]{:S(2)}, u32[]{:S(2)}) collective-permute-start(bf16[2,128,128]{2,1,0:T(8,128)(2,1)S(1)} %get-tuple-element.23.pair_ref.refs_3_), channel_id=1, source_target_pairs={{0,8},{4,20},{8,0},{12,28},{16,24},{20,4},{24,16},{28,12},{1,9},{5... | collective-permute-start | bytes 196616 | tf_op jit(solution)/shard_map/ppermute | solution.py:266
  8.9 6.2 %collective-permute-start.2 = (bf16[2,128,128]{2,1,0:T(8,128)(2,1)S(1)}, bf16[2,128,128]{2,1,0:T(8,128)(2,1)S(1)}, u32[]{:S(2)}, u32[]{:S(2)}) collective-permute-start(bf16[2,128,128]{2,1,0:T(8,128)(2,1)S(1)} %get-tuple-element.27), channel_id=1, source_target_pairs={{0,16},{4,28},{8,24},{12,20},{16,0},{20,12},{24,8},{28,4},{1,17},{... | collective-permute-start | bytes 196616 | tf_op jit(solution)/shard_map/ppermute | solution.py:266
  12.7 5.2 %collective-permute-start.5 = (bf16[2,128,128]{2,1,0:T(8,128)(2,1)S(1)}, bf16[2,128,128]{2,1,0:T(8,128)(2,1)S(1)}, u32[]{:S(2)}, u32[]{:S(2)}) collective-permute-start(bf16[2,128,128]{2,1,0:T(8,128)(2,1)S(1)} %get-tuple-element.30), channel_id=1, source_target_pairs={{0,24},{4,12},{8,16},{12,4},{16,8},{20,28},{24,0},{28,20},{1,25},{... | collective-permute-start | bytes 196616 | tf_op jit(solution)/shard_map/ppermute | solution.py:266
  13.4 4.5 %collective-permute-start.6 = (bf16[2,128,128]{2,1,0:T(8,128)(2,1)S(1)}, bf16[2,128,128]{2,1,0:T(8,128)(2,1)S(1)}, u32[]{:S(2)}, u32[]{:S(2)}) collective-permute-start(bf16[2,128,128]{2,1,0:T(8,128)(2,1)S(1)} %get-tuple-element.31), channel_id=1, source_target_pairs={{0,8},{4,20},{8,0},{12,28},{16,24},{20,4},{24,16},{28,12},{1,9},{5... | collective-permute-start | bytes 196616 | tf_op jit(solution)/shard_map/ppermute | solution.py:266
  15.6 2.4 %collective-permute-start.7 = (bf16[768,128]{1,0:T(8,128)(2,1)S(1)}, bf16[768,128]{1,0:T(8,128)(2,1)S(1)}, u32[]{:S(2)}, u32[]{:S(2)}) collective-permute-start(bf16[768,128]{1,0:T(8,128)(2,1)S(1)} %shard_map.101), channel_id=1, source_target_pairs={{0,4},{4,0},{1,5},{5,1},{2,6},{6,2},{3,7},{7,3},{8,12},{12,8},{9,1... | collective-permute-start | bytes 589832 | tf_op jit(solution)/shard_map/ppermute | solution.py:258

commit v9 on v8

--- a/solution.py
+++ b/solution.py
@@ -27,8 +27,8 @@
 def peer_offset(step, outer, inner_count):
     last = inner_count - 1
     if outer % 2 == 1:
-        return {0: 0, 1: last}.get(step, step - 1)
-    return {0: 0, 1: last - 1, 2: last}.get(step, step - 2) if last > 1 else step
+        return (inner_count - step) % inner_count
+    return {0: 0, 1: 1, 2: last}.get(step, step - 1)
 
 
 def load_kernel(
@@ -40,18 +40,18 @@
         pltpu.make_async_copy(source, target, sems.at[at])
         for at, (source, target) in enumerate(
             [
+                (query_hbm, packet_ref.at[pl.ds(0, half)]),
+                (grad_hbm, packet_ref.at[pl.ds(half, half)]),
+                (out_hbm, packet_ref.at[pl.ds(2 * half, half)]),
                 (norm_hbm, norm_ref.at[pl.ds(0, group_size)]),
                 (key_hbm, pair_ref.at[0]),
                 (value_hbm, pair_ref.at[1]),
-                (query_hbm, packet_ref.at[pl.ds(0, half)]),
-                (grad_hbm, packet_ref.at[pl.ds(half, half)]),
-                (out_hbm, packet_ref.at[pl.ds(2 * half, half)]),
             ]
         )
     ]
     for copy in copies:
         copy.start()
-    copies[0].wait()
+    copies[3].wait()
     held = lax.broadcasted_iota(jnp.int32, (STAT_ROWS, row_count), 0) < group_size
     rest = jnp.where(held, jnp.clip(norm_ref[...], -3.38e38, 3.38e38), 0.0)
     for term in range(SPLIT):
@@ -59,7 +59,7 @@
         start = 3 * half + term * STAT_ROWS
         packet_ref[start : start + STAT_ROWS, :] = piece
         rest = rest - piece.astype(jnp.float32)
-    for copy in copies[1:]:
+    for copy in copies[:3] + copies[4:]:
         copy.wait()
 
 
@@ -142,17 +142,19 @@
     copy = pltpu.make_async_copy(order_hbm, order_ref, sem)
     copy.start()
     has_next = lax.axis_index("outer") < outer_count - 1
-    row_stats(packet_ref, stat_ref.at[0], sizes)
-    row_stats(next_ref, stat_ref.at[1], sizes)
-
-    @pl.when(jnp.logical_not(has_next))
-    def _():
-        stat_ref[1, :8, :] = jnp.full((8, row_count), 1e30, jnp.float32)
-
     key_rows = lax.broadcasted_iota(jnp.int32, (row_count, row_count), 0)
     visible = key_rows <= lax.broadcasted_iota(jnp.int32, (row_count, row_count), 1)
-    parts = ((packet_ref, stat_ref[0], visible, scores_ref), (next_ref, stat_ref[1], None, next_scores_ref))
-    total_ref[0], total_ref[1] = block_terms(pair_ref[0], pair_ref[1], parts, sizes)
+    row_stats(packet_ref, stat_ref.at[0], sizes)
+
+    def add_up(both):
+        parts = [(packet_ref, stat_ref[0], visible, scores_ref)]
+        if both:
+            row_stats(next_ref, stat_ref.at[1], sizes)
+            parts.append((next_ref, stat_ref[1], None, next_scores_ref))
+        total_ref[0], total_ref[1] = block_terms(pair_ref[0], pair_ref[1], parts, sizes)
+
+    pl.when(has_next)(lambda: add_up(True))
+    pl.when(jnp.logical_not(has_next))(lambda: add_up(False))
     copy.wait()
     my_index = lax.axis_index("inner")
     turned = lax.rem(lax.axis_index("outer"), 2) == 1
@@ -161,18 +163,26 @@
         rank_ref[step : step + 1, :] = jnp.full((1, row_count), order_ref[my_index ^ offset], jnp.int32)
 
 
-def far_kernel(sizes, inner_count, steps, packet_ref, next_ref, rank_ref, stat_ref, *refs):
+def far_kernel(sizes, inner_count, outer_count, steps, packet_ref, next_ref, rank_ref, stat_ref, *refs):
     count = len(steps)
     _, row_count, head_size = sizes
     inv_root = 1.0 / math.sqrt(head_size)
     blocks, (scores_ref, next_scores_ref), sums = refs[:count], refs[count : count + 2], refs[count + 2 :]
-    visible = visible_rows(rank_ref, steps, inner_count, row_count)
-    parts = ((packet_ref, stat_ref[0], visible, scores_ref), (next_ref, stat_ref[1], None, next_scores_ref))
-    key_total, value_total = block_terms(stacked(blocks, 0), stacked(blocks, 1), parts, sizes)
-    for at, ref in enumerate(sums):
-        rows = slice(at * row_count, (at + 1) * row_count)
-        ref[0] = (key_total[rows] * inv_root).astype(jnp.bfloat16)
-        ref[1] = value_total[rows].astype(jnp.bfloat16)
+    has_next = lax.axis_index("outer") < outer_count - 1
+
+    def add_up(both):
+        visible = visible_rows(rank_ref, steps, inner_count, row_count)
+        parts = [(packet_ref, stat_ref[0], visible, scores_ref)]
+        if both:
+            parts.append((next_ref, stat_ref[1], None, next_scores_ref))
+        key_total, value_total = block_terms(stacked(blocks, 0), stacked(blocks, 1), parts, sizes)
+        for at, ref in enumerate(sums):
+            rows = slice(at * row_count, (at + 1) * row_count)
+            ref[0] = (key_total[rows] * inv_root).astype(jnp.bfloat16)
+            ref[1] = value_total[rows].astype(jnp.bfloat16)
+
+    pl.when(has_next)(lambda: add_up(True))
+    pl.when(jnp.logical_not(has_next))(lambda: add_up(False))
 
 
 def query_terms(refs, groups, lanes):
@@ -181,8 +191,8 @@
 
 
 def store_queries(result_ref, refs, groups, sizes):
-    group_size, row_count, _ = sizes
-    terms = query_terms(refs, groups, slice(None))
+    group_size, row_count, head_size = sizes
+    terms = query_terms(refs, groups, slice(None)) * (1.0 / math.sqrt(head_size))
     for head in range(group_size):
         rows = slice(head * row_count, (head + 1) * row_count)
         result_ref[rows, :] = terms[:, rows].T.astype(result_ref.dtype)
@@ -220,20 +230,23 @@
 
 
 def final_kernel(
-    sizes, sum_ref, query_ref, back_ref, query_hbm, key_hbm, value_hbm, result_ref, sems
+    parts, sum_ref, query_ref, back_ref, query_hbm, key_hbm, value_hbm, result_ref, sems
 ):
-    inv_root = 1.0 / math.sqrt(sizes[2])
     copies = [
         pltpu.make_async_copy(sum_ref.at[0], key_hbm, sems.at[0]),
         pltpu.make_async_copy(sum_ref.at[1], value_hbm, sems.at[1]),
-        pltpu.make_async_copy(result_ref, query_hbm, sems.at[2]),
     ]
-    copies[0].start()
-    copies[1].start()
+    for copy in copies:
+        copy.start()
     has_prev = lax.axis_index("outer") > 0
-    back = jnp.where(has_prev, back_ref[...].astype(jnp.float32), 0.0)
-    result_ref[...] = ((query_ref[...] + back) * inv_root).astype(jnp.bfloat16)
-    copies[2].start()
+    count = query_ref.shape[0] // parts
+    for part in range(parts):
+        rows = pl.ds(part * count, count)
+        back = jnp.where(has_prev, back_ref[rows, :].astype(jnp.float32), 0.0)
+        result_ref[rows, :] = (query_ref[rows, :] + back).astype(jnp.bfloat16)
+        copy = pltpu.make_async_copy(result_ref.at[rows], query_hbm.at[rows], sems.at[2 + part])
+        copy.start()
+        copies.append(copy)
     for copy in copies:
         copy.wait()
 
@@ -329,7 +342,7 @@
     for steps in (away[:middle], away[middle:]):
         if steps:
             far_scores, far_next_scores, *terms = pl.pallas_call(
-                functools.partial(far_kernel, sizes, inner_count, steps),
+                functools.partial(far_kernel, sizes, inner_count, outer_count, steps),
                 out_shape=(scores_shape(len(steps)),) * 2 + (block_shape,) * len(steps),
                 in_specs=[vmem] * (4 + len(steps)),
                 out_specs=(vmem,) * (2 + len(steps)),
@@ -383,7 +396,7 @@
     )(early_total, *returned[middle:])
 
     query_out, key_out, value_out = pl.pallas_call(
-        functools.partial(final_kernel, sizes),
+        functools.partial(final_kernel, group_size),
         out_shape=(
             shape((half, head_size), jnp.bfloat16),
             shape((row_count, head_size), jnp.bfloat16),
@@ -391,7 +404,7 @@
         ),
         in_specs=[vmem] * 3,
         out_specs=(hbm,) * 3,
-        scratch_shapes=[pltpu.VMEM((half, head_size), jnp.bfloat16), pltpu.SemaphoreType.DMA((3,))],
+        scratch_shapes=[pltpu.VMEM((half, head_size), jnp.bfloat16), pltpu.SemaphoreType.DMA((2 + group_size,))],
         compiler_params=roomy,
     )(late_sum, query_own, query_back)
     grad_queries = jnp.swapaxes(query_out.reshape(group_size, row_count, head_size), 0, 1)

time: 18.9 us -> 18.8 us (level)
  starting transfers between devices: 9.53 us -> 9.78 us
    ppermute x6, starting transfers between devices: 8.94 us -> 9.19 us  [exchange(): return lax.ppermute(block, ('inner', 'outer'), route)]
  transfers between devices with their start and end apart: 8 -> 8, of which waited for: 2 -> 4; matrix products, arithmetic and copies ran while one was open for 0% -> 0% of each run, Pallas kernels for 19% -> 18%
where the time goes in v9:
time: 18.8 us; the launch traced here: 18.7 us
  starting transfers between devices  9.78 us (52%)
  Pallas kernels  5.34 us (28%)
  waiting for transfers between devices  2.83 us (15%)
  between operations  0.73 us (4%)
    ppermute x6, starting transfers between devices, exchange(): return lax.ppermute(block, ('inner', 'outer'), route)  9.19 us
    ppermute x6, waiting for transfers between devices, exchange(): return lax.ppermute(block, ('inner', 'outer'), route)  2.83 us
    pallas_call x2, Pallas kernels, on_device(): pl.pallas_call(functools.partial(far_kernel, sizes, inner_count, outer_co...  1.68 us
    pallas_call x1, Pallas kernels, on_device(): pl.pallas_call(functools.partial(load_kernel, sizes), out_shape=(block_sh...  1.17 us
    pallas_call x1, Pallas kernels, on_device(): pl.pallas_call(functools.partial(near_kernel, sizes, inner_count, outer_c...  0.87 us
    pallas_call x1, Pallas kernels, on_device(): pl.pallas_call(functools.partial(final_kernel, group_size), out_shape=(sh...  0.76 us
    ppermute x2, starting transfers between devices, to_segment(): return lax.ppermute(block, 'outer', route)  0.59 us
    pallas_call x1, Pallas kernels, on_device(): pl.pallas_call(functools.partial(query_kernel, sizes, groups), out_shape=...  0.41 us
  transfers between devices with their start and end apart: 8, of which 4 were waited for; matrix products, arithmetic and copies ran while one was open for 0% of the time, Pallas kernels for 18%

profile of v9, /device:TPU:0, one launch (start us, length us, event | category | flops | bytes accessed | tf_op | source)
XLA Modules:
  0.0 18.7 jit_solution(10272518147112436953)
XLA Ops:
  0.6 1.2 %shard_map.94 = (bf16[2,128,128]{2,1,0:T(8,128)(2,1)S(1)}, bf16[2352,128]{1,0:T(8,128)(2,1)S(1)}) custom-call(bf16[768,128]{1,0:T(8,128)(2,1)} %bitcast.16, bf16[768,128]{1,0:T(8,128)(2,1)} %bitcast.17, bf16[768,128]{1,0:T(8,128)(2,1)} %bitcast.18, f32[6,128]{1,0:T(8,128)} %norm_hbm.1, bf16[128,128]{1,0:T(8,128)(2,1)} %bitcast.19, bf16[128,128]{1,0:T(8,128)(2,1)} %bitcast.20), custom_call_target="tpu_custom_call" | custom-call | bytes 1048576 | tf_op jit(solution)/shard_map/pallas_call | solution.py:296
  1.8 0.5 %collective-permute-start = (bf16[2352,128]{1,0:T(8,128)(2,1)S(1)}, bf16[2352,128]{1,0:T(8,128)(2,1)S(1)}, u32[]{:S(2)}, u32[]{:S(2)}) collective-permute-start(bf16[2352,128]{1,0:T(8,128)(2,1)S(1)} %get-tuple-element.22.packet_ref), channel_id=1, source_target_pairs={{0,4},{4,0},{1,5},{5,1},{2,6},{6,2},{3,7},{7,3},{8,12},{12,8},{9,1... | collective-permute-start | bytes 1806344 | tf_op jit(solution)/shard_map/ppermute | solution.py:271
  2.3 2.6 %collective-permute-start.1 = (bf16[2,128,128]{2,1,0:T(8,128)(2,1)S(1)}, bf16[2,128,128]{2,1,0:T(8,128)(2,1)S(1)}, u32[]{:S(2)}, u32[]{:S(2)}) collective-permute-start(bf16[2,128,128]{2,1,0:T(8,128)(2,1)S(1)} %get-tuple-element.23.pair_ref.refs_3_), channel_id=1, source_target_pairs={{0,8},{4,28},{8,0},{12,20},{16,24},{20,12},{24,16},{28,4},{1,9},{5... | collective-permute-start | bytes 196616 | tf_op jit(solution)/shard_map/ppermute | solution.py:279
  4.9 1.5 %collective-permute-start.3 = (bf16[2,128,128]{2,1,0:T(8,128)(2,1)S(1)}, bf16[2,128,128]{2,1,0:T(8,128)(2,1)S(1)}, u32[]{:S(2)}, u32[]{:S(2)}) collective-permute-start(bf16[2,128,128]{2,1,0:T(8,128)(2,1)S(1)} %get-tuple-element.23.pair_ref.refs_3_), channel_id=1, source_target_pairs={{0,24},{4,20},{8,16},{12,28},{16,8},{20,4},{24,0},{28,12},{1,25},{... | collective-permute-start | bytes 196616 | tf_op jit(solution)/shard_map/ppermute | solution.py:279
  6.4 0.0 collective-permute-start.4
  6.4 0.0 collective-permute-done.next_ref
  6.4 0.9 %shard_map.95 = (bf16[128,768]{1,0:T(8,128)(2,1)S(1)}, bf16[128,768]{1,0:T(8,128)(2,1)S(1)}, f32[2,128,128]{2,1,0:T(8,128)S(1)}, f32[2,16,128]{2,1,0:T(8,128)S(1)}, s32[8,128]{1,0:T(8,128)S(1)}) custom-call(bf16[2352,128]{1,0:T(8,128)(2,1)S(1)} %get-tuple-element.22.packet_ref, bf16[2352,128]{1,0:T(8,128)(2,1)S(1)} %collective-permute-done.next_ref, ...), custom_call_target="tpu_custom_call" | custom-call | flops 251658240 | bytes 1048576 | tf_op jit(solution)/shard_map/pallas_call | solution.py:323
  7.3 0.0 collective-permute-done.1.refs_0_.refs_4_
  7.3 0.7 %shard_map.96 = (bf16[128,768]{1,0:T(8,128)(2,1)S(1)}, bf16[128,768]{1,0:T(8,128)(2,1)S(1)}, bf16[2,128,128]{2,1,0:T(8,128)(2,1)S(1)}) custom-call(bf16[2352,128]{1,0:T(8,128)(2,1)S(1)} %get-tuple-element.22.packet_ref, bf16[2352,128]{1,0:T(8,128)(2,1)S(1)} %collective-permute-done.next_ref, s32[8,128]{1,0:T(8,128)S(1)} %get-tuple-element.25.rank_ref, ...), custom_call_target="tpu_custom_call" | custom-call | flops 251658240 | bytes 1048576 | tf_op jit(solution)/shard_map/pallas_call | solution.py:344
  8.0 2.2 %collective-permute-start.2 = (bf16[2,128,128]{2,1,0:T(8,128)(2,1)S(1)}, bf16[2,128,128]{2,1,0:T(8,128)(2,1)S(1)}, u32[]{:S(2)}, u32[]{:S(2)}) collective-permute-start(bf16[2,128,128]{2,1,0:T(8,128)(2,1)S(1)} %get-tuple-element.27), channel_id=1, source_target_pairs={{0,8},{4,28},{8,0},{12,20},{16,24},{20,12},{24,16},{28,4},{1,9},{5... | collective-permute-start | bytes 196616 | tf_op jit(solution)/shard_map/ppermute | solution.py:279
  10.3 0.2 collective-permute-done.3.refs_0_.refs_5_
  10.4 0.5 %collective-permute-done.4.refs_1_.refs_6_ = bf16[2,128,128]{2,1,0:T(8,128)(2,1)S(1)} collective-permute-done((bf16[2,128,128]{2,1,0:T(8,128)(2,1)S(1)}, bf16[2,128,128]{2,1,0:T(8,128)(2,1)S(1)}, u32[]{:S(2)}, u32[]{:S(2)}) %collective-permute-start.4) | collective-permute-done | bytes 65568 | tf_op jit(solution)/shard_map/ppermute | solution.py:279
  10.9 1.0 %shard_map.98 = (bf16[256,768]{1,0:T(8,128)(2,1)S(1)}, bf16[256,768]{1,0:T(8,128)(2,1)S(1)}, bf16[2,128,128]{2,1,0:T(8,128)(2,1)S(1)}, bf16[2,128,128]{2,1,0:T(8,128)(2,1)S(1)}) custom-call(bf16[2352,128]{1,0:T(8,128)(2,1)S(1)} %get-tuple-element.22.packet_ref, bf16[2352,128]{1,0:T(8,128)(2,1)S(1)} %collective-permute-done.next_ref, ...), custom_call_target="tpu_custom_call" | custom-call | flops 503316480 | bytes 1048576 | tf_op jit(solution)/shard_map/pallas_call | solution.py:344
  11.9 1.7 %collective-permute-start.5 = (bf16[2,128,128]{2,1,0:T(8,128)(2,1)S(1)}, bf16[2,128,128]{2,1,0:T(8,128)(2,1)S(1)}, u32[]{:S(2)}, u32[]{:S(2)}) collective-permute-start(bf16[2,128,128]{2,1,0:T(8,128)(2,1)S(1)} %get-tuple-element.30), channel_id=1, source_target_pairs={{0,24},{4,20},{8,16},{12,28},{16,8},{20,4},{24,0},{28,12},{1,25},{... | collective-permute-start | bytes 196616 | tf_op jit(solution)/shard_map/ppermute | solution.py:279
  13.6 1.1 %collective-permute-start.6 = (bf16[2,128,128]{2,1,0:T(8,128)(2,1)S(1)}, bf16[2,128,128]{2,1,0:T(8,128)(2,1)S(1)}, u32[]{:S(2)}, u32[]{:S(2)}) collective-permute-start(bf16[2,128,128]{2,1,0:T(8,128)(2,1)S(1)} %get-tuple-element.31), channel_id=1, source_target_pairs={{0,16},{4,12},{8,24},{12,4},{16,0},{20,28},{24,8},{28,20},{1,17},{... | collective-permute-start | bytes 196616 | tf_op jit(solution)/shard_map/ppermute | solution.py:279
  14.7 0.4 %shard_map.100.query_ref = f32[768,128]{1,0:T(8,128)S(1)} custom-call(bf16[128,768]{1,0:T(8,128)(2,1)S(1)} %get-tuple-element.32.refs_0_, bf16[128,768]{1,0:T(8,128)(2,1)S(1)} %get-tuple-element.33.refs_1_, bf16[256,768]{1,0:T(8,128)(2,1)S(1)} %get-tuple-element.34.refs_2_, bf16[2,128,128]{2,1,0:T(8,128)(2,1)S(1)} %get-tuple-element.23.pair_ref.refs_3_, ...), custom_call_target="tpu_custom_call" | custom-call | tf_op jit(solution)/shard_map/pallas_call | solution.py:380
  15.2 0.0 collective-permute-done.2.refs_1_
  15.2 0.4 %shard_map.101 = bf16[768,128]{1,0:T(8,128)(2,1)S(1)} custom-call(bf16[128,768]{1,0:T(8,128)(2,1)S(1)} %get-tuple-element.35.refs_0_, bf16[128,768]{1,0:T(8,128)(2,1)S(1)} %get-tuple-element.36.refs_1_, bf16[256,768]{1,0:T(8,128)(2,1)S(1)} %get-tuple-element.37.refs_2_, bf16[2,128,128]{2,1,0:T(8,128)(2,1)S(1)} %get-tuple-element.23.pair_ref.refs_3_, ...), custom_call_target="tpu_custom_call" | custom-call | tf_op jit(solution)/shard_map/pallas_call | solution.py:370
  15.6 0.1 collective-permute-start.7
  15.7 1.5 %collective-permute-done.5.refs_1_ = bf16[2,128,128]{2,1,0:T(8,128)(2,1)S(1)} collective-permute-done((bf16[2,128,128]{2,1,0:T(8,128)(2,1)S(1)}, bf16[2,128,128]{2,1,0:T(8,128)(2,1)S(1)}, u32[]{:S(2)}, u32[]{:S(2)}) %collective-permute-start.5) | collective-permute-done | bytes 65568 | tf_op jit(solution)/shard_map/ppermute | solution.py:279
  17.1 0.7 %collective-permute-done.6.refs_2_ = bf16[2,128,128]{2,1,0:T(8,128)(2,1)S(1)} collective-permute-done((bf16[2,128,128]{2,1,0:T(8,128)(2,1)S(1)}, bf16[2,128,128]{2,1,0:T(8,128)(2,1)S(1)}, u32[]{:S(2)}, u32[]{:S(2)}) %collective-permute-start.6) | collective-permute-done | bytes 65568 | tf_op jit(solution)/shard_map/ppermute | solution.py:279
  17.9 0.0 collective-permute-done.7.back_ref
  17.9 0.8 %shard_map.102 = (bf16[768,128]{1,0:T(8,128)(2,1)}, bf16[128,128]{1,0:T(8,128)(2,1)}, bf16[128,128]{1,0:T(8,128)(2,1)}) custom-call(bf16[2,128,128]{2,1,0:T(8,128)(2,1)S(1)} %shard_map.99.sum_ref, f32[768,128]{1,0:T(8,128)S(1)} %shard_map.100.query_ref, bf16[768,128]{1,0:T(8,128)(2,1)S(1)} %collective-permute-done.7.back_ref), custom_call_target="tpu_custom_call" | custom-call | tf_op jit(solution)/shard_map/pallas_call | solution.py:398
  (2 shorter events, 0.0 us)
Async XLA Ops:
  1.8 4.6 %collective-permute-start = (bf16[2352,128]{1,0:T(8,128)(2,1)S(1)}, bf16[2352,128]{1,0:T(8,128)(2,1)S(1)}, u32[]{:S(2)}, u32[]{:S(2)}) collective-permute-start(bf16[2352,128]{1,0:T(8,128)(2,1)S(1)} %get-tuple-element.22.packet_ref), channel_id=1, source_target_pairs={{0,4},{4,0},{1,5},{5,1},{2,6},{6,2},{3,7},{7,3},{8,12},{12,8},{9,1... | collective-permute-start | bytes 1806344 | tf_op jit(solution)/shard_map/ppermute | solution.py:271
  2.3 5.0 %collective-permute-start.1 = (bf16[2,128,128]{2,1,0:T(8,128)(2,1)S(1)}, bf16[2,128,128]{2,1,0:T(8,128)(2,1)S(1)}, u32[]{:S(2)}, u32[]{:S(2)}) collective-permute-start(bf16[2,128,128]{2,1,0:T(8,128)(2,1)S(1)} %get-tuple-element.23.pair_ref.refs_3_), channel_id=1, source_target_pairs={{0,8},{4,28},{8,0},{12,20},{16,24},{20,12},{24,16},{28,4},{1,9},{5... | collective-permute-start | bytes 196616 | tf_op jit(solution)/shard_map/ppermute | solution.py:279
  4.9 5.5 %collective-permute-start.3 = (bf16[2,128,128]{2,1,0:T(8,128)(2,1)S(1)}, bf16[2,128,128]{2,1,0:T(8,128)(2,1)S(1)}, u32[]{:S(2)}, u32[]{:S(2)}) collective-permute-start(bf16[2,128,128]{2,1,0:T(8,128)(2,1)S(1)} %get-tuple-element.23.pair_ref.refs_3_), channel_id=1, source_target_pairs={{0,24},{4,20},{8,16},{12,28},{16,8},{20,4},{24,0},{28,12},{1,25},{... | collective-permute-start | bytes 196616 | tf_op jit(solution)/shard_map/ppermute | solution.py:279
  6.4 4.5 %collective-permute-start.4 = (bf16[2,128,128]{2,1,0:T(8,128)(2,1)S(1)}, bf16[2,128,128]{2,1,0:T(8,128)(2,1)S(1)}, u32[]{:S(2)}, u32[]{:S(2)}) collective-permute-start(bf16[2,128,128]{2,1,0:T(8,128)(2,1)S(1)} %get-tuple-element.23.pair_ref.refs_3_), channel_id=1, source_target_pairs={{0,16},{4,12},{8,24},{12,4},{16,0},{20,28},{24,8},{28,20},{1,17},{... | collective-permute-start | bytes 196616 | tf_op jit(solution)/shard_map/ppermute | solution.py:279
  8.0 7.2 %collective-permute-start.2 = (bf16[2,128,128]{2,1,0:T(8,128)(2,1)S(1)}, bf16[2,128,128]{2,1,0:T(8,128)(2,1)S(1)}, u32[]{:S(2)}, u32[]{:S(2)}) collective-permute-start(bf16[2,128,128]{2,1,0:T(8,128)(2,1)S(1)} %get-tuple-element.27), channel_id=1, source_target_pairs={{0,8},{4,28},{8,0},{12,20},{16,24},{20,12},{24,16},{28,4},{1,9},{5... | collective-permute-start | bytes 196616 | tf_op jit(solution)/shard_map/ppermute | solution.py:279
  11.9 5.2 %collective-permute-start.5 = (bf16[2,128,128]{2,1,0:T(8,128)(2,1)S(1)}, bf16[2,128,128]{2,1,0:T(8,128)(2,1)S(1)}, u32[]{:S(2)}, u32[]{:S(2)}) collective-permute-start(bf16[2,128,128]{2,1,0:T(8,128)(2,1)S(1)} %get-tuple-element.30), channel_id=1, source_target_pairs={{0,24},{4,20},{8,16},{12,28},{16,8},{20,4},{24,0},{28,12},{1,25},{... | collective-permute-start | bytes 196616 | tf_op jit(solution)/shard_map/ppermute | solution.py:279
  13.6 4.3 %collective-permute-start.6 = (bf16[2,128,128]{2,1,0:T(8,128)(2,1)S(1)}, bf16[2,128,128]{2,1,0:T(8,128)(2,1)S(1)}, u32[]{:S(2)}, u32[]{:S(2)}) collective-permute-start(bf16[2,128,128]{2,1,0:T(8,128)(2,1)S(1)} %get-tuple-element.31), channel_id=1, source_target_pairs={{0,16},{4,12},{8,24},{12,4},{16,0},{20,28},{24,8},{28,20},{1,17},{... | collective-permute-start | bytes 196616 | tf_op jit(solution)/shard_map/ppermute | solution.py:279
  15.6 2.3 %collective-permute-start.7 = (bf16[768,128]{1,0:T(8,128)(2,1)S(1)}, bf16[768,128]{1,0:T(8,128)(2,1)S(1)}, u32[]{:S(2)}, u32[]{:S(2)}) collective-permute-start(bf16[768,128]{1,0:T(8,128)(2,1)S(1)} %shard_map.101), channel_id=1, source_target_pairs={{0,4},{4,0},{1,5},{5,1},{2,6},{6,2},{3,7},{7,3},{8,12},{12,8},{9,1... | collective-permute-start | bytes 589832 | tf_op jit(solution)/shard_map/ppermute | solution.py:271

commit v10 on v9

--- a/solution.py
+++ b/solution.py
@@ -83,28 +83,22 @@
     group_size, row_count, head_size = sizes
     half = group_size * row_count
     scale = LOG2E / math.sqrt(head_size)
-    per_step = 2 if group_size % 2 == 0 else 1
     key_total = 0.0
     value_total = 0.0
     for packet_ref, stats, visible, scores_ref in parts:
         weights_parts = []
         score_parts = []
-        for first in range(0, group_size, per_step):
-            start, stop = first * row_count, (first + per_step) * row_count
-            queries = packet_ref[start:stop, :]
-            grads = packet_ref[half + start : half + stop, :]
-            scores = contract(keys, queries, 1, 1)
-            grad_weights = contract(values, grads, 1, 1)
-            for at in range(per_step):
-                head = first + at
-                lanes = slice(at * row_count, (at + 1) * row_count)
-                weights = jnp.exp2(scores[:, lanes] * scale - stats[head : head + 1, :])
-                if visible is not None:
-                    weights = jnp.where(visible, weights, 0.0)
-                weights_parts.append(weights.astype(jnp.bfloat16))
-                score_parts.append(
-                    (weights * (grad_weights[:, lanes] - stats[8 + head : 9 + head, :])).astype(jnp.bfloat16)
-                )
+        scores = contract(keys, packet_ref[:half, :], 1, 1)
+        grad_weights = contract(values, packet_ref[half : 2 * half, :], 1, 1)
+        for head in range(group_size):
+            lanes = slice(head * row_count, (head + 1) * row_count)
+            weights = jnp.exp2(scores[:, lanes] * scale - stats[head : head + 1, :])
+            if visible is not None:
+                weights = jnp.where(visible, weights, 0.0)
+            weights_parts.append(weights.astype(jnp.bfloat16))
+            score_parts.append(
+                (weights * (grad_weights[:, lanes] - stats[8 + head : 9 + head, :])).astype(jnp.bfloat16)
+            )
         grad_scores = jnp.concatenate(score_parts, axis=1)
         scores_ref[...] = grad_scores
         value_total += contract(jnp.concatenate(weights_parts, axis=1), packet_ref[half : 2 * half, :], 1, 0)

time: 18.8 us -> 18.9 us (level)
  no operation moved by 1% of the time
where the time goes in v10:
time: 18.9 us; the launch traced here: 18.7 us
  starting transfers between devices  9.78 us (52%)
  Pallas kernels  5.37 us (28%)
  waiting for transfers between devices  2.84 us (15%)
  between operations  0.73 us (4%)
    ppermute x6, starting transfers between devices, exchange(): return lax.ppermute(block, ('inner', 'outer'), route)  9.19 us
    ppermute x6, waiting for transfers between devices, exchange(): return lax.ppermute(block, ('inner', 'outer'), route)  2.84 us
    pallas_call x2, Pallas kernels, on_device(): pl.pallas_call(functools.partial(far_kernel, sizes, inner_count, outer_co...  1.72 us
    pallas_call x1, Pallas kernels, on_device(): pl.pallas_call(functools.partial(load_kernel, sizes), out_shape=(block_sh...  1.17 us
    pallas_call x1, Pallas kernels, on_device(): pl.pallas_call(functools.partial(near_kernel, sizes, inner_count, outer_c...  0.87 us
    pallas_call x1, Pallas kernels, on_device(): pl.pallas_call(functools.partial(final_kernel, group_size), out_shape=(sh...  0.76 us
    ppermute x2, starting transfers between devices, to_segment(): return lax.ppermute(block, 'outer', route)  0.59 us
    pallas_call x1, Pallas kernels, on_device(): pl.pallas_call(functools.partial(query_kernel, sizes, groups), out_shape=...  0.41 us
  transfers between devices with their start and end apart: 8, of which 4 were waited for; matrix products, arithmetic and copies ran while one was open for 0% of the time, Pallas kernels for 18%

profile of v10, /device:TPU:0, one launch (start us, length us, event | category | flops | bytes accessed | tf_op | source)
XLA Modules:
  0.0 18.7 jit_solution(2618470233581856744)
XLA Ops:
  0.6 1.2 %shard_map.94 = (bf16[2,128,128]{2,1,0:T(8,128)(2,1)S(1)}, bf16[2352,128]{1,0:T(8,128)(2,1)S(1)}) custom-call(bf16[768,128]{1,0:T(8,128)(2,1)} %bitcast.16, bf16[768,128]{1,0:T(8,128)(2,1)} %bitcast.17, bf16[768,128]{1,0:T(8,128)(2,1)} %bitcast.18, f32[6,128]{1,0:T(8,128)} %norm_hbm.1, bf16[128,128]{1,0:T(8,128)(2,1)} %bitcast.19, bf16[128,128]{1,0:T(8,128)(2,1)} %bitcast.20), custom_call_target="tpu_custom_call" | custom-call | bytes 1048576 | tf_op jit(solution)/shard_map/pallas_call | solution.py:290
  1.8 0.5 %collective-permute-start = (bf16[2352,128]{1,0:T(8,128)(2,1)S(1)}, bf16[2352,128]{1,0:T(8,128)(2,1)S(1)}, u32[]{:S(2)}, u32[]{:S(2)}) collective-permute-start(bf16[2352,128]{1,0:T(8,128)(2,1)S(1)} %get-tuple-element.22.packet_ref), channel_id=1, source_target_pairs={{0,4},{4,0},{1,5},{5,1},{2,6},{6,2},{3,7},{7,3},{8,12},{12,8},{9,1... | collective-permute-start | bytes 1806344 | tf_op jit(solution)/shard_map/ppermute | solution.py:265
  2.3 2.6 %collective-permute-start.1 = (bf16[2,128,128]{2,1,0:T(8,128)(2,1)S(1)}, bf16[2,128,128]{2,1,0:T(8,128)(2,1)S(1)}, u32[]{:S(2)}, u32[]{:S(2)}) collective-permute-start(bf16[2,128,128]{2,1,0:T(8,128)(2,1)S(1)} %get-tuple-element.23.pair_ref.refs_3_), channel_id=1, source_target_pairs={{0,8},{4,28},{8,0},{12,20},{16,24},{20,12},{24,16},{28,4},{1,9},{5... | collective-permute-start | bytes 196616 | tf_op jit(solution)/shard_map/ppermute | solution.py:273
  4.9 1.5 %collective-permute-start.3 = (bf16[2,128,128]{2,1,0:T(8,128)(2,1)S(1)}, bf16[2,128,128]{2,1,0:T(8,128)(2,1)S(1)}, u32[]{:S(2)}, u32[]{:S(2)}) collective-permute-start(bf16[2,128,128]{2,1,0:T(8,128)(2,1)S(1)} %get-tuple-element.23.pair_ref.refs_3_), channel_id=1, source_target_pairs={{0,24},{4,20},{8,16},{12,28},{16,8},{20,4},{24,0},{28,12},{1,25},{... | collective-permute-start | bytes 196616 | tf_op jit(solution)/shard_map/ppermute | solution.py:273
  6.4 0.0 collective-permute-start.4
  6.4 0.0 collective-permute-done.next_ref
  6.4 0.9 %shard_map.95 = (bf16[128,768]{1,0:T(8,128)(2,1)S(1)}, bf16[128,768]{1,0:T(8,128)(2,1)S(1)}, f32[2,128,128]{2,1,0:T(8,128)S(1)}, f32[2,16,128]{2,1,0:T(8,128)S(1)}, s32[8,128]{1,0:T(8,128)S(1)}) custom-call(bf16[2352,128]{1,0:T(8,128)(2,1)S(1)} %get-tuple-element.22.packet_ref, bf16[2352,128]{1,0:T(8,128)(2,1)S(1)} %collective-permute-done.next_ref, ...), custom_call_target="tpu_custom_call" | custom-call | flops 251658240 | bytes 1048576 | tf_op jit(solution)/shard_map/pallas_call | solution.py:317
  7.3 0.0 collective-permute-done.1.refs_0_.refs_4_
  7.3 0.7 %shard_map.96 = (bf16[128,768]{1,0:T(8,128)(2,1)S(1)}, bf16[128,768]{1,0:T(8,128)(2,1)S(1)}, bf16[2,128,128]{2,1,0:T(8,128)(2,1)S(1)}) custom-call(bf16[2352,128]{1,0:T(8,128)(2,1)S(1)} %get-tuple-element.22.packet_ref, bf16[2352,128]{1,0:T(8,128)(2,1)S(1)} %collective-permute-done.next_ref, s32[8,128]{1,0:T(8,128)S(1)} %get-tuple-element.25.rank_ref, ...), custom_call_target="tpu_custom_call" | custom-call | flops 251658240 | bytes 1048576 | tf_op jit(solution)/shard_map/pallas_call | solution.py:338
  8.0 2.2 %collective-permute-start.2 = (bf16[2,128,128]{2,1,0:T(8,128)(2,1)S(1)}, bf16[2,128,128]{2,1,0:T(8,128)(2,1)S(1)}, u32[]{:S(2)}, u32[]{:S(2)}) collective-permute-start(bf16[2,128,128]{2,1,0:T(8,128)(2,1)S(1)} %get-tuple-element.27), channel_id=1, source_target_pairs={{0,8},{4,28},{8,0},{12,20},{16,24},{20,12},{24,16},{28,4},{1,9},{5... | collective-permute-start | bytes 196616 | tf_op jit(solution)/shard_map/ppermute | solution.py:273
  10.2 0.2 collective-permute-done.3.refs_0_.refs_5_
  10.4 0.5 %collective-permute-done.4.refs_1_.refs_6_ = bf16[2,128,128]{2,1,0:T(8,128)(2,1)S(1)} collective-permute-done((bf16[2,128,128]{2,1,0:T(8,128)(2,1)S(1)}, bf16[2,128,128]{2,1,0:T(8,128)(2,1)S(1)}, u32[]{:S(2)}, u32[]{:S(2)}) %collective-permute-start.4) | collective-permute-done | bytes 65568 | tf_op jit(solution)/shard_map/ppermute | solution.py:273
  10.9 1.1 %shard_map.98 = (bf16[256,768]{1,0:T(8,128)(2,1)S(1)}, bf16[256,768]{1,0:T(8,128)(2,1)S(1)}, bf16[2,128,128]{2,1,0:T(8,128)(2,1)S(1)}, bf16[2,128,128]{2,1,0:T(8,128)(2,1)S(1)}) custom-call(bf16[2352,128]{1,0:T(8,128)(2,1)S(1)} %get-tuple-element.22.packet_ref, bf16[2352,128]{1,0:T(8,128)(2,1)S(1)} %collective-permute-done.next_ref, ...), custom_call_target="tpu_custom_call" | custom-call | flops 503316480 | bytes 1048576 | tf_op jit(solution)/shard_map/pallas_call | solution.py:338
  11.9 1.7 %collective-permute-start.5 = (bf16[2,128,128]{2,1,0:T(8,128)(2,1)S(1)}, bf16[2,128,128]{2,1,0:T(8,128)(2,1)S(1)}, u32[]{:S(2)}, u32[]{:S(2)}) collective-permute-start(bf16[2,128,128]{2,1,0:T(8,128)(2,1)S(1)} %get-tuple-element.30), channel_id=1, source_target_pairs={{0,24},{4,20},{8,16},{12,28},{16,8},{20,4},{24,0},{28,12},{1,25},{... | collective-permute-start | bytes 196616 | tf_op jit(solution)/shard_map/ppermute | solution.py:273
  13.6 1.1 %collective-permute-start.6 = (bf16[2,128,128]{2,1,0:T(8,128)(2,1)S(1)}, bf16[2,128,128]{2,1,0:T(8,128)(2,1)S(1)}, u32[]{:S(2)}, u32[]{:S(2)}) collective-permute-start(bf16[2,128,128]{2,1,0:T(8,128)(2,1)S(1)} %get-tuple-element.31), channel_id=1, source_target_pairs={{0,16},{4,12},{8,24},{12,4},{16,0},{20,28},{24,8},{28,20},{1,17},{... | collective-permute-start | bytes 196616 | tf_op jit(solution)/shard_map/ppermute | solution.py:273
  14.8 0.4 %shard_map.100.query_ref = f32[768,128]{1,0:T(8,128)S(1)} custom-call(bf16[128,768]{1,0:T(8,128)(2,1)S(1)} %get-tuple-element.32.refs_0_, bf16[128,768]{1,0:T(8,128)(2,1)S(1)} %get-tuple-element.33.refs_1_, bf16[256,768]{1,0:T(8,128)(2,1)S(1)} %get-tuple-element.34.refs_2_, bf16[2,128,128]{2,1,0:T(8,128)(2,1)S(1)} %get-tuple-element.23.pair_ref.refs_3_, ...), custom_call_target="tpu_custom_call" | custom-call | tf_op jit(solution)/shard_map/pallas_call | solution.py:374
  15.2 0.0 collective-permute-done.2.refs_1_
  15.2 0.4 %shard_map.101 = bf16[768,128]{1,0:T(8,128)(2,1)S(1)} custom-call(bf16[128,768]{1,0:T(8,128)(2,1)S(1)} %get-tuple-element.35.refs_0_, bf16[128,768]{1,0:T(8,128)(2,1)S(1)} %get-tuple-element.36.refs_1_, bf16[256,768]{1,0:T(8,128)(2,1)S(1)} %get-tuple-element.37.refs_2_, bf16[2,128,128]{2,1,0:T(8,128)(2,1)S(1)} %get-tuple-element.23.pair_ref.refs_3_, ...), custom_call_target="tpu_custom_call" | custom-call | tf_op jit(solution)/shard_map/pallas_call | solution.py:364
  15.6 0.1 collective-permute-start.7
  15.7 1.5 %collective-permute-done.5.refs_1_ = bf16[2,128,128]{2,1,0:T(8,128)(2,1)S(1)} collective-permute-done((bf16[2,128,128]{2,1,0:T(8,128)(2,1)S(1)}, bf16[2,128,128]{2,1,0:T(8,128)(2,1)S(1)}, u32[]{:S(2)}, u32[]{:S(2)}) %collective-permute-start.5) | collective-permute-done | bytes 65568 | tf_op jit(solution)/shard_map/ppermute | solution.py:273
  17.2 0.7 %collective-permute-done.6.refs_2_ = bf16[2,128,128]{2,1,0:T(8,128)(2,1)S(1)} collective-permute-done((bf16[2,128,128]{2,1,0:T(8,128)(2,1)S(1)}, bf16[2,128,128]{2,1,0:T(8,128)(2,1)S(1)}, u32[]{:S(2)}, u32[]{:S(2)}) %collective-permute-start.6) | collective-permute-done | bytes 65568 | tf_op jit(solution)/shard_map/ppermute | solution.py:273
  17.9 0.0 collective-permute-done.7.back_ref
  18.0 0.8 %shard_map.102 = (bf16[768,128]{1,0:T(8,128)(2,1)}, bf16[128,128]{1,0:T(8,128)(2,1)}, bf16[128,128]{1,0:T(8,128)(2,1)}) custom-call(bf16[2,128,128]{2,1,0:T(8,128)(2,1)S(1)} %shard_map.99.sum_ref, f32[768,128]{1,0:T(8,128)S(1)} %shard_map.100.query_ref, bf16[768,128]{1,0:T(8,128)(2,1)S(1)} %collective-permute-done.7.back_ref), custom_call_target="tpu_custom_call" | custom-call | tf_op jit(solution)/shard_map/pallas_call | solution.py:392
  (2 shorter events, 0.0 us)
Async XLA Ops:
  1.8 4.6 %collective-permute-start = (bf16[2352,128]{1,0:T(8,128)(2,1)S(1)}, bf16[2352,128]{1,0:T(8,128)(2,1)S(1)}, u32[]{:S(2)}, u32[]{:S(2)}) collective-permute-start(bf16[2352,128]{1,0:T(8,128)(2,1)S(1)} %get-tuple-element.22.packet_ref), channel_id=1, source_target_pairs={{0,4},{4,0},{1,5},{5,1},{2,6},{6,2},{3,7},{7,3},{8,12},{12,8},{9,1... | collective-permute-start | bytes 1806344 | tf_op jit(solution)/shard_map/ppermute | solution.py:265
  2.3 5.0 %collective-permute-start.1 = (bf16[2,128,128]{2,1,0:T(8,128)(2,1)S(1)}, bf16[2,128,128]{2,1,0:T(8,128)(2,1)S(1)}, u32[]{:S(2)}, u32[]{:S(2)}) collective-permute-start(bf16[2,128,128]{2,1,0:T(8,128)(2,1)S(1)} %get-tuple-element.23.pair_ref.refs_3_), channel_id=1, source_target_pairs={{0,8},{4,28},{8,0},{12,20},{16,24},{20,12},{24,16},{28,4},{1,9},{5... | collective-permute-start | bytes 196616 | tf_op jit(solution)/shard_map/ppermute | solution.py:273
  4.9 5.5 %collective-permute-start.3 = (bf16[2,128,128]{2,1,0:T(8,128)(2,1)S(1)}, bf16[2,128,128]{2,1,0:T(8,128)(2,1)S(1)}, u32[]{:S(2)}, u32[]{:S(2)}) collective-permute-start(bf16[2,128,128]{2,1,0:T(8,128)(2,1)S(1)} %get-tuple-element.23.pair_ref.refs_3_), channel_id=1, source_target_pairs={{0,24},{4,20},{8,16},{12,28},{16,8},{20,4},{24,0},{28,12},{1,25},{... | collective-permute-start | bytes 196616 | tf_op jit(solution)/shard_map/ppermute | solution.py:273
  6.4 4.5 %collective-permute-start.4 = (bf16[2,128,128]{2,1,0:T(8,128)(2,1)S(1)}, bf16[2,128,128]{2,1,0:T(8,128)(2,1)S(1)}, u32[]{:S(2)}, u32[]{:S(2)}) collective-permute-start(bf16[2,128,128]{2,1,0:T(8,128)(2,1)S(1)} %get-tuple-element.23.pair_ref.refs_3_), channel_id=1, source_target_pairs={{0,16},{4,12},{8,24},{12,4},{16,0},{20,28},{24,8},{28,20},{1,17},{... | collective-permute-start | bytes 196616 | tf_op jit(solution)/shard_map/ppermute | solution.py:273
  8.0 7.2 %collective-permute-start.2 = (bf16[2,128,128]{2,1,0:T(8,128)(2,1)S(1)}, bf16[2,128,128]{2,1,0:T(8,128)(2,1)S(1)}, u32[]{:S(2)}, u32[]{:S(2)}) collective-permute-start(bf16[2,128,128]{2,1,0:T(8,128)(2,1)S(1)} %get-tuple-element.27), channel_id=1, source_target_pairs={{0,8},{4,28},{8,0},{12,20},{16,24},{20,12},{24,16},{28,4},{1,9},{5... | collective-permute-start | bytes 196616 | tf_op jit(solution)/shard_map/ppermute | solution.py:273
  11.9 5.2 %collective-permute-start.5 = (bf16[2,128,128]{2,1,0:T(8,128)(2,1)S(1)}, bf16[2,128,128]{2,1,0:T(8,128)(2,1)S(1)}, u32[]{:S(2)}, u32[]{:S(2)}) collective-permute-start(bf16[2,128,128]{2,1,0:T(8,128)(2,1)S(1)} %get-tuple-element.30), channel_id=1, source_target_pairs={{0,24},{4,20},{8,16},{12,28},{16,8},{20,4},{24,0},{28,12},{1,25},{... | collective-permute-start | bytes 196616 | tf_op jit(solution)/shard_map/ppermute | solution.py:273
  13.6 4.3 %collective-permute-start.6 = (bf16[2,128,128]{2,1,0:T(8,128)(2,1)S(1)}, bf16[2,128,128]{2,1,0:T(8,128)(2,1)S(1)}, u32[]{:S(2)}, u32[]{:S(2)}) collective-permute-start(bf16[2,128,128]{2,1,0:T(8,128)(2,1)S(1)} %get-tuple-element.31), channel_id=1, source_target_pairs={{0,16},{4,12},{8,24},{12,4},{16,0},{20,28},{24,8},{28,20},{1,17},{... | collective-permute-start | bytes 196616 | tf_op jit(solution)/shard_map/ppermute | solution.py:273
  15.6 2.3 %collective-permute-start.7 = (bf16[768,128]{1,0:T(8,128)(2,1)S(1)}, bf16[768,128]{1,0:T(8,128)(2,1)S(1)}, u32[]{:S(2)}, u32[]{:S(2)}) collective-permute-start(bf16[768,128]{1,0:T(8,128)(2,1)S(1)} %shard_map.101), channel_id=1, source_target_pairs={{0,4},{4,0},{1,5},{5,1},{2,6},{6,2},{3,7},{7,3},{8,12},{12,8},{9,1... | collective-permute-start | bytes 589832 | tf_op jit(solution)/shard_map/ppermute | solution.py:265

commit v11 on v9

--- a/solution.py
+++ b/solution.py
@@ -27,7 +27,7 @@
 def peer_offset(step, outer, inner_count):
     last = inner_count - 1
     if outer % 2 == 1:
-        return (inner_count - step) % inner_count
+        return {0: 0, 1: last - 1, last: last}.get(step, step - 1)
     return {0: 0, 1: 1, 2: last}.get(step, step - 1)
 
 

time: 18.8 us -> 19.9 us (1.059)
  waiting for transfers between devices: 2.83 us -> 4.31 us
  starting transfers between devices: 9.78 us -> 9.37 us
    ppermute x6, waiting for transfers between devices: 2.83 us -> 4.3 us  [exchange(): return lax.ppermute(block, ('inner', 'outer'), route)]
    ppermute x6, starting transfers between devices: 9.19 us -> 8.78 us  [exchange(): return lax.ppermute(block, ('inner', 'outer'), route)]
  transfers between devices with their start and end apart: 8 -> 8, of which waited for: 4 -> 4; matrix products, arithmetic and copies ran while one was open for 0% -> 0% of each run, Pallas kernels for 18% -> 17%
where the time goes in v11:
time: 19.9 us; the launch traced here: 19.7 us
  starting transfers between devices  9.37 us (47%)
  Pallas kernels  5.33 us (27%)
  waiting for transfers between devices  4.31 us (22%)
  between operations  0.73 us (4%)
    ppermute x6, starting transfers between devices, exchange(): return lax.ppermute(block, ('inner', 'outer'), route)  8.78 us
    ppermute x6, waiting for transfers between devices, exchange(): return lax.ppermute(block, ('inner', 'outer'), route)  4.3 us
    pallas_call x2, Pallas kernels, on_device(): pl.pallas_call(functools.partial(far_kernel, sizes, inner_count, outer_co...  1.68 us
    pallas_call x1, Pallas kernels, on_device(): pl.pallas_call(functools.partial(load_kernel, sizes), out_shape=(block_sh...  1.17 us
    pallas_call x1, Pallas kernels, on_device(): pl.pallas_call(functools.partial(near_kernel, sizes, inner_count, outer_c...  0.87 us
    pallas_call x1, Pallas kernels, on_device(): pl.pallas_call(functools.partial(final_kernel, group_size), out_shape=(sh...  0.76 us
    ppermute x2, starting transfers between devices, to_segment(): return lax.ppermute(block, 'outer', route)  0.59 us
    pallas_call x1, Pallas kernels, on_device(): pl.pallas_call(functools.partial(query_kernel, sizes, groups), out_shape=...  0.41 us
  transfers between devices with their start and end apart: 8, of which 4 were waited for; matrix products, arithmetic and copies ran while one was open for 0% of the time, Pallas kernels for 17%

profile of v11, /device:TPU:0, one launch (start us, length us, event | category | flops | bytes accessed | tf_op | source)
XLA Modules:
  0.0 19.7 jit_solution(11520714145272600530)
XLA Ops:
  0.6 1.2 %shard_map.94 = (bf16[2,128,128]{2,1,0:T(8,128)(2,1)S(1)}, bf16[2352,128]{1,0:T(8,128)(2,1)S(1)}) custom-call(bf16[768,128]{1,0:T(8,128)(2,1)} %bitcast.16, bf16[768,128]{1,0:T(8,128)(2,1)} %bitcast.17, bf16[768,128]{1,0:T(8,128)(2,1)} %bitcast.18, f32[6,128]{1,0:T(8,128)} %norm_hbm.1, bf16[128,128]{1,0:T(8,128)(2,1)} %bitcast.19, bf16[128,128]{1,0:T(8,128)(2,1)} %bitcast.20), custom_call_target="tpu_custom_call" | custom-call | bytes 1048576 | tf_op jit(solution)/shard_map/pallas_call | solution.py:296
  1.8 0.5 %collective-permute-start = (bf16[2352,128]{1,0:T(8,128)(2,1)S(1)}, bf16[2352,128]{1,0:T(8,128)(2,1)S(1)}, u32[]{:S(2)}, u32[]{:S(2)}) collective-permute-start(bf16[2352,128]{1,0:T(8,128)(2,1)S(1)} %get-tuple-element.22.packet_ref), channel_id=1, source_target_pairs={{0,4},{4,0},{1,5},{5,1},{2,6},{6,2},{3,7},{7,3},{8,12},{12,8},{9,1... | collective-permute-start | bytes 1806344 | tf_op jit(solution)/shard_map/ppermute | solution.py:271
  2.3 2.6 %collective-permute-start.1 = (bf16[2,128,128]{2,1,0:T(8,128)(2,1)S(1)}, bf16[2,128,128]{2,1,0:T(8,128)(2,1)S(1)}, u32[]{:S(2)}, u32[]{:S(2)}) collective-permute-start(bf16[2,128,128]{2,1,0:T(8,128)(2,1)S(1)} %get-tuple-element.23.pair_ref.refs_3_), channel_id=1, source_target_pairs={{0,8},{4,20},{8,0},{12,28},{16,24},{20,4},{24,16},{28,12},{1,9},{5... | collective-permute-start | bytes 196616 | tf_op jit(solution)/shard_map/ppermute | solution.py:279
  4.9 1.5 %collective-permute-start.3 = (bf16[2,128,128]{2,1,0:T(8,128)(2,1)S(1)}, bf16[2,128,128]{2,1,0:T(8,128)(2,1)S(1)}, u32[]{:S(2)}, u32[]{:S(2)}) collective-permute-start(bf16[2,128,128]{2,1,0:T(8,128)(2,1)S(1)} %get-tuple-element.23.pair_ref.refs_3_), channel_id=1, source_target_pairs={{0,24},{4,12},{8,16},{12,4},{16,8},{20,28},{24,0},{28,20},{1,25},{... | collective-permute-start | bytes 196616 | tf_op jit(solution)/shard_map/ppermute | solution.py:279
  6.4 0.1 collective-permute-start.4
  6.4 0.0 collective-permute-done.next_ref
  6.4 0.9 %shard_map.95 = (bf16[128,768]{1,0:T(8,128)(2,1)S(1)}, bf16[128,768]{1,0:T(8,128)(2,1)S(1)}, f32[2,128,128]{2,1,0:T(8,128)S(1)}, f32[2,16,128]{2,1,0:T(8,128)S(1)}, s32[8,128]{1,0:T(8,128)S(1)}) custom-call(bf16[2352,128]{1,0:T(8,128)(2,1)S(1)} %get-tuple-element.22.packet_ref, bf16[2352,128]{1,0:T(8,128)(2,1)S(1)} %collective-permute-done.next_ref, ...), custom_call_target="tpu_custom_call" | custom-call | flops 251658240 | bytes 1048576 | tf_op jit(solution)/shard_map/pallas_call | solution.py:323
  7.3 0.0 collective-permute-done.1.refs_0_.refs_4_
  7.3 0.7 %shard_map.96 = (bf16[128,768]{1,0:T(8,128)(2,1)S(1)}, bf16[128,768]{1,0:T(8,128)(2,1)S(1)}, bf16[2,128,128]{2,1,0:T(8,128)(2,1)S(1)}) custom-call(bf16[2352,128]{1,0:T(8,128)(2,1)S(1)} %get-tuple-element.22.packet_ref, bf16[2352,128]{1,0:T(8,128)(2,1)S(1)} %collective-permute-done.next_ref, s32[8,128]{1,0:T(8,128)S(1)} %get-tuple-element.25.rank_ref, ...), custom_call_target="tpu_custom_call" | custom-call | flops 251658240 | bytes 1048576 | tf_op jit(solution)/shard_map/pallas_call | solution.py:344
  8.0 2.0 %collective-permute-start.2 = (bf16[2,128,128]{2,1,0:T(8,128)(2,1)S(1)}, bf16[2,128,128]{2,1,0:T(8,128)(2,1)S(1)}, u32[]{:S(2)}, u32[]{:S(2)}) collective-permute-start(bf16[2,128,128]{2,1,0:T(8,128)(2,1)S(1)} %get-tuple-element.27), channel_id=1, source_target_pairs={{0,8},{4,20},{8,0},{12,28},{16,24},{20,4},{24,16},{28,12},{1,9},{5... | collective-permute-start | bytes 196616 | tf_op jit(solution)/shard_map/ppermute | solution.py:279
  10.0 0.4 %collective-permute-done.3.refs_0_.refs_5_ = bf16[2,128,128]{2,1,0:T(8,128)(2,1)S(1)} collective-permute-done((bf16[2,128,128]{2,1,0:T(8,128)(2,1)S(1)}, bf16[2,128,128]{2,1,0:T(8,128)(2,1)S(1)}, u32[]{:S(2)}, u32[]{:S(2)}) %collective-permute-start.3) | collective-permute-done | bytes 65568 | tf_op jit(solution)/shard_map/ppermute | solution.py:279
  10.5 1.7 %collective-permute-done.4.refs_1_.refs_6_ = bf16[2,128,128]{2,1,0:T(8,128)(2,1)S(1)} collective-permute-done((bf16[2,128,128]{2,1,0:T(8,128)(2,1)S(1)}, bf16[2,128,128]{2,1,0:T(8,128)(2,1)S(1)}, u32[]{:S(2)}, u32[]{:S(2)}) %collective-permute-start.4) | collective-permute-done | bytes 65568 | tf_op jit(solution)/shard_map/ppermute | solution.py:279
  12.2 1.0 %shard_map.98 = (bf16[256,768]{1,0:T(8,128)(2,1)S(1)}, bf16[256,768]{1,0:T(8,128)(2,1)S(1)}, bf16[2,128,128]{2,1,0:T(8,128)(2,1)S(1)}, bf16[2,128,128]{2,1,0:T(8,128)(2,1)S(1)}) custom-call(bf16[2352,128]{1,0:T(8,128)(2,1)S(1)} %get-tuple-element.22.packet_ref, bf16[2352,128]{1,0:T(8,128)(2,1)S(1)} %collective-permute-done.next_ref, ...), custom_call_target="tpu_custom_call" | custom-call | flops 503316480 | bytes 1048576 | tf_op jit(solution)/shard_map/pallas_call | solution.py:344
  13.2 0.8 %collective-permute-start.5 = (bf16[2,128,128]{2,1,0:T(8,128)(2,1)S(1)}, bf16[2,128,128]{2,1,0:T(8,128)(2,1)S(1)}, u32[]{:S(2)}, u32[]{:S(2)}) collective-permute-start(bf16[2,128,128]{2,1,0:T(8,128)(2,1)S(1)} %get-tuple-element.30), channel_id=1, source_target_pairs={{0,24},{4,12},{8,16},{12,4},{16,8},{20,28},{24,0},{28,20},{1,25},{... | collective-permute-start | bytes 196616 | tf_op jit(solution)/shard_map/ppermute | solution.py:279
  14.0 1.9 %collective-permute-start.6 = (bf16[2,128,128]{2,1,0:T(8,128)(2,1)S(1)}, bf16[2,128,128]{2,1,0:T(8,128)(2,1)S(1)}, u32[]{:S(2)}, u32[]{:S(2)}) collective-permute-start(bf16[2,128,128]{2,1,0:T(8,128)(2,1)S(1)} %get-tuple-element.31), channel_id=1, source_target_pairs={{0,16},{4,28},{8,24},{12,20},{16,0},{20,12},{24,8},{28,4},{1,17},{... | collective-permute-start | bytes 196616 | tf_op jit(solution)/shard_map/ppermute | solution.py:279
  15.8 0.4 %shard_map.100.query_ref = f32[768,128]{1,0:T(8,128)S(1)} custom-call(bf16[128,768]{1,0:T(8,128)(2,1)S(1)} %get-tuple-element.32.refs_0_, bf16[128,768]{1,0:T(8,128)(2,1)S(1)} %get-tuple-element.33.refs_1_, bf16[256,768]{1,0:T(8,128)(2,1)S(1)} %get-tuple-element.34.refs_2_, bf16[2,128,128]{2,1,0:T(8,128)(2,1)S(1)} %get-tuple-element.23.pair_ref.refs_3_, ...), custom_call_target="tpu_custom_call" | custom-call | tf_op jit(solution)/shard_map/pallas_call | solution.py:380
  16.2 0.0 collective-permute-done.2.refs_1_
  16.3 0.4 %shard_map.101 = bf16[768,128]{1,0:T(8,128)(2,1)S(1)} custom-call(bf16[128,768]{1,0:T(8,128)(2,1)S(1)} %get-tuple-element.35.refs_0_, bf16[128,768]{1,0:T(8,128)(2,1)S(1)} %get-tuple-element.36.refs_1_, bf16[256,768]{1,0:T(8,128)(2,1)S(1)} %get-tuple-element.37.refs_2_, bf16[2,128,128]{2,1,0:T(8,128)(2,1)S(1)} %get-tuple-element.23.pair_ref.refs_3_, ...), custom_call_target="tpu_custom_call" | custom-call | tf_op jit(solution)/shard_map/pallas_call | solution.py:370
  16.7 0.1 collective-permute-start.7
  16.8 1.7 %collective-permute-done.5.refs_1_ = bf16[2,128,128]{2,1,0:T(8,128)(2,1)S(1)} collective-permute-done((bf16[2,128,128]{2,1,0:T(8,128)(2,1)S(1)}, bf16[2,128,128]{2,1,0:T(8,128)(2,1)S(1)}, u32[]{:S(2)}, u32[]{:S(2)}) %collective-permute-start.5) | collective-permute-done | bytes 65568 | tf_op jit(solution)/shard_map/ppermute | solution.py:279
  18.5 0.4 %collective-permute-done.6.refs_2_ = bf16[2,128,128]{2,1,0:T(8,128)(2,1)S(1)} collective-permute-done((bf16[2,128,128]{2,1,0:T(8,128)(2,1)S(1)}, bf16[2,128,128]{2,1,0:T(8,128)(2,1)S(1)}, u32[]{:S(2)}, u32[]{:S(2)}) %collective-permute-start.6) | collective-permute-done | bytes 65568 | tf_op jit(solution)/shard_map/ppermute | solution.py:279
  19.0 0.0 collective-permute-done.7.back_ref
  19.0 0.8 %shard_map.102 = (bf16[768,128]{1,0:T(8,128)(2,1)}, bf16[128,128]{1,0:T(8,128)(2,1)}, bf16[128,128]{1,0:T(8,128)(2,1)}) custom-call(bf16[2,128,128]{2,1,0:T(8,128)(2,1)S(1)} %shard_map.99.sum_ref, f32[768,128]{1,0:T(8,128)S(1)} %shard_map.100.query_ref, bf16[768,128]{1,0:T(8,128)(2,1)S(1)} %collective-permute-done.7.back_ref), custom_call_target="tpu_custom_call" | custom-call | tf_op jit(solution)/shard_map/pallas_call | solution.py:398
  (2 shorter events, 0.0 us)
Async XLA Ops:
  1.8 4.6 %collective-permute-start = (bf16[2352,128]{1,0:T(8,128)(2,1)S(1)}, bf16[2352,128]{1,0:T(8,128)(2,1)S(1)}, u32[]{:S(2)}, u32[]{:S(2)}) collective-permute-start(bf16[2352,128]{1,0:T(8,128)(2,1)S(1)} %get-tuple-element.22.packet_ref), channel_id=1, source_target_pairs={{0,4},{4,0},{1,5},{5,1},{2,6},{6,2},{3,7},{7,3},{8,12},{12,8},{9,1... | collective-permute-start | bytes 1806344 | tf_op jit(solution)/shard_map/ppermute | solution.py:271
  2.3 5.0 %collective-permute-start.1 = (bf16[2,128,128]{2,1,0:T(8,128)(2,1)S(1)}, bf16[2,128,128]{2,1,0:T(8,128)(2,1)S(1)}, u32[]{:S(2)}, u32[]{:S(2)}) collective-permute-start(bf16[2,128,128]{2,1,0:T(8,128)(2,1)S(1)} %get-tuple-element.23.pair_ref.refs_3_), channel_id=1, source_target_pairs={{0,8},{4,20},{8,0},{12,28},{16,24},{20,4},{24,16},{28,12},{1,9},{5... | collective-permute-start | bytes 196616 | tf_op jit(solution)/shard_map/ppermute | solution.py:279
  4.9 5.6 %collective-permute-start.3 = (bf16[2,128,128]{2,1,0:T(8,128)(2,1)S(1)}, bf16[2,128,128]{2,1,0:T(8,128)(2,1)S(1)}, u32[]{:S(2)}, u32[]{:S(2)}) collective-permute-start(bf16[2,128,128]{2,1,0:T(8,128)(2,1)S(1)} %get-tuple-element.23.pair_ref.refs_3_), channel_id=1, source_target_pairs={{0,24},{4,12},{8,16},{12,4},{16,8},{20,28},{24,0},{28,20},{1,25},{... | collective-permute-start | bytes 196616 | tf_op jit(solution)/shard_map/ppermute | solution.py:279
  6.4 5.8 %collective-permute-start.4 = (bf16[2,128,128]{2,1,0:T(8,128)(2,1)S(1)}, bf16[2,128,128]{2,1,0:T(8,128)(2,1)S(1)}, u32[]{:S(2)}, u32[]{:S(2)}) collective-permute-start(bf16[2,128,128]{2,1,0:T(8,128)(2,1)S(1)} %get-tuple-element.23.pair_ref.refs_3_), channel_id=1, source_target_pairs={{0,16},{4,28},{8,24},{12,20},{16,0},{20,12},{24,8},{28,4},{1,17},{... | collective-permute-start | bytes 196616 | tf_op jit(solution)/shard_map/ppermute | solution.py:279
  8.0 8.2 %collective-permute-start.2 = (bf16[2,128,128]{2,1,0:T(8,128)(2,1)S(1)}, bf16[2,128,128]{2,1,0:T(8,128)(2,1)S(1)}, u32[]{:S(2)}, u32[]{:S(2)}) collective-permute-start(bf16[2,128,128]{2,1,0:T(8,128)(2,1)S(1)} %get-tuple-element.27), channel_id=1, source_target_pairs={{0,8},{4,20},{8,0},{12,28},{16,24},{20,4},{24,16},{28,12},{1,9},{5... | collective-permute-start | bytes 196616 | tf_op jit(solution)/shard_map/ppermute | solution.py:279
  13.2 5.3 %collective-permute-start.5 = (bf16[2,128,128]{2,1,0:T(8,128)(2,1)S(1)}, bf16[2,128,128]{2,1,0:T(8,128)(2,1)S(1)}, u32[]{:S(2)}, u32[]{:S(2)}) collective-permute-start(bf16[2,128,128]{2,1,0:T(8,128)(2,1)S(1)} %get-tuple-element.30), channel_id=1, source_target_pairs={{0,24},{4,12},{8,16},{12,4},{16,8},{20,28},{24,0},{28,20},{1,25},{... | collective-permute-start | bytes 196616 | tf_op jit(solution)/shard_map/ppermute | solution.py:279
  14.0 5.0 %collective-permute-start.6 = (bf16[2,128,128]{2,1,0:T(8,128)(2,1)S(1)}, bf16[2,128,128]{2,1,0:T(8,128)(2,1)S(1)}, u32[]{:S(2)}, u32[]{:S(2)}) collective-permute-start(bf16[2,128,128]{2,1,0:T(8,128)(2,1)S(1)} %get-tuple-element.31), channel_id=1, source_target_pairs={{0,16},{4,28},{8,24},{12,20},{16,0},{20,12},{24,8},{28,4},{1,17},{... | collective-permute-start | bytes 196616 | tf_op jit(solution)/shard_map/ppermute | solution.py:279
  16.7 2.3 %collective-permute-start.7 = (bf16[768,128]{1,0:T(8,128)(2,1)S(1)}, bf16[768,128]{1,0:T(8,128)(2,1)S(1)}, u32[]{:S(2)}, u32[]{:S(2)}) collective-permute-start(bf16[768,128]{1,0:T(8,128)(2,1)S(1)} %shard_map.101), channel_id=1, source_target_pairs={{0,4},{4,0},{1,5},{5,1},{2,6},{6,2},{3,7},{7,3},{8,12},{12,8},{9,1... | collective-permute-start | bytes 589832 | tf_op jit(solution)/shard_map/ppermute | solution.py:271

commit v12 on v9

--- a/solution.py
+++ b/solution.py
@@ -339,7 +339,7 @@
     scores, next_scores, sums = [near_scores], [near_next_scores], {}
     middle = inner_count // 2 - 1
     held = [0]
-    for steps in (away[:middle], away[middle:]):
+    for steps in (away[:middle], away[middle : middle + 1], away[middle + 1 :]):
         if steps:
             far_scores, far_next_scores, *terms = pl.pallas_call(
                 functools.partial(far_kernel, sizes, inner_count, outer_count, steps),

time: 18.8 us -> 18.9 us (level)
  Pallas kernels: 5.34 us -> 5.62 us
    pallas_call x2 -> x3, Pallas kernels: 1.68 us -> 1.98 us  [on_device(): pl.pallas_call(functools.partial(far_kernel, sizes, inner_count, outer_co...]
  transfers between devices with their start and end apart: 8 -> 8, of which waited for: 4 -> 3; matrix products, arithmetic and copies ran while one was open for 0% -> 0% of each run, Pallas kernels for 18% -> 20%
where the time goes in v12:
time: 18.9 us; the launch traced here: 18.8 us
  starting transfers between devices  9.66 us (51%)
  Pallas kernels  5.62 us (30%)
  waiting for transfers between devices  2.77 us (15%)
  between operations  0.74 us (4%)
    ppermute x6, starting transfers between devices, exchange(): return lax.ppermute(block, ('inner', 'outer'), route)  9.08 us
    ppermute x6, waiting for transfers between devices, exchange(): return lax.ppermute(block, ('inner', 'outer'), route)  2.77 us
    pallas_call x3, Pallas kernels, on_device(): pl.pallas_call(functools.partial(far_kernel, sizes, inner_count, outer_co...  1.98 us
    pallas_call x1, Pallas kernels, on_device(): pl.pallas_call(functools.partial(load_kernel, sizes), out_shape=(block_sh...  1.17 us
    pallas_call x1, Pallas kernels, on_device(): pl.pallas_call(functools.partial(near_kernel, sizes, inner_count, outer_c...  0.87 us
    pallas_call x1, Pallas kernels, on_device(): pl.pallas_call(functools.partial(final_kernel, group_size), out_shape=(sh...  0.76 us
    ppermute x2, starting transfers between devices, to_segment(): return lax.ppermute(block, 'outer', route)  0.59 us
    pallas_call x1, Pallas kernels, on_device(): pl.pallas_call(functools.partial(query_kernel, sizes, groups), out_shape=...  0.41 us
  transfers between devices with their start and end apart: 8, of which 3 were waited for; matrix products, arithmetic and copies ran while one was open for 0% of the time, Pallas kernels for 20%

profile of v12, /device:TPU:0, one launch (start us, length us, event | category | flops | bytes accessed | tf_op | source)
XLA Modules:
  0.0 18.8 jit_solution(1694070920647590572)
XLA Ops:
  0.6 1.2 %shard_map.94 = (bf16[2,128,128]{2,1,0:T(8,128)(2,1)S(1)}, bf16[2352,128]{1,0:T(8,128)(2,1)S(1)}) custom-call(bf16[768,128]{1,0:T(8,128)(2,1)} %bitcast.16, bf16[768,128]{1,0:T(8,128)(2,1)} %bitcast.17, bf16[768,128]{1,0:T(8,128)(2,1)} %bitcast.18, f32[6,128]{1,0:T(8,128)} %norm_hbm.1, bf16[128,128]{1,0:T(8,128)(2,1)} %bitcast.19, bf16[128,128]{1,0:T(8,128)(2,1)} %bitcast.20), custom_call_target="tpu_custom_call" | custom-call | bytes 1048576 | tf_op jit(solution)/shard_map/pallas_call | solution.py:296
  1.8 0.5 %collective-permute-start = (bf16[2352,128]{1,0:T(8,128)(2,1)S(1)}, bf16[2352,128]{1,0:T(8,128)(2,1)S(1)}, u32[]{:S(2)}, u32[]{:S(2)}) collective-permute-start(bf16[2352,128]{1,0:T(8,128)(2,1)S(1)} %get-tuple-element.24.packet_ref), channel_id=1, source_target_pairs={{0,4},{4,0},{1,5},{5,1},{2,6},{6,2},{3,7},{7,3},{8,12},{12,8},{9,1... | collective-permute-start | bytes 1806344 | tf_op jit(solution)/shard_map/ppermute | solution.py:271
  2.3 2.6 %collective-permute-start.1 = (bf16[2,128,128]{2,1,0:T(8,128)(2,1)S(1)}, bf16[2,128,128]{2,1,0:T(8,128)(2,1)S(1)}, u32[]{:S(2)}, u32[]{:S(2)}) collective-permute-start(bf16[2,128,128]{2,1,0:T(8,128)(2,1)S(1)} %get-tuple-element.25.pair_ref.refs_4_), channel_id=1, source_target_pairs={{0,8},{4,28},{8,0},{12,20},{16,24},{20,12},{24,16},{28,4},{1,9},{5... | collective-permute-start | bytes 196616 | tf_op jit(solution)/shard_map/ppermute | solution.py:279
  4.9 1.5 %collective-permute-start.3 = (bf16[2,128,128]{2,1,0:T(8,128)(2,1)S(1)}, bf16[2,128,128]{2,1,0:T(8,128)(2,1)S(1)}, u32[]{:S(2)}, u32[]{:S(2)}) collective-permute-start(bf16[2,128,128]{2,1,0:T(8,128)(2,1)S(1)} %get-tuple-element.25.pair_ref.refs_4_), channel_id=1, source_target_pairs={{0,24},{4,20},{8,16},{12,28},{16,8},{20,4},{24,0},{28,12},{1,25},{... | collective-permute-start | bytes 196616 | tf_op jit(solution)/shard_map/ppermute | solution.py:279
  6.4 0.0 collective-permute-start.5
  6.4 0.0 collective-permute-done.next_ref
  6.4 0.9 %shard_map.95 = (bf16[128,768]{1,0:T(8,128)(2,1)S(1)}, bf16[128,768]{1,0:T(8,128)(2,1)S(1)}, f32[2,128,128]{2,1,0:T(8,128)S(1)}, f32[2,16,128]{2,1,0:T(8,128)S(1)}, s32[8,128]{1,0:T(8,128)S(1)}) custom-call(bf16[2352,128]{1,0:T(8,128)(2,1)S(1)} %get-tuple-element.24.packet_ref, bf16[2352,128]{1,0:T(8,128)(2,1)S(1)} %collective-permute-done.next_ref, ...), custom_call_target="tpu_custom_call" | custom-call | flops 251658240 | bytes 1048576 | tf_op jit(solution)/shard_map/pallas_call | solution.py:323
  7.3 0.0 collective-permute-done.1.refs_0_.refs_5_
  7.3 0.7 %shard_map.96 = (bf16[128,768]{1,0:T(8,128)(2,1)S(1)}, bf16[128,768]{1,0:T(8,128)(2,1)S(1)}, bf16[2,128,128]{2,1,0:T(8,128)(2,1)S(1)}) custom-call(bf16[2352,128]{1,0:T(8,128)(2,1)S(1)} %get-tuple-element.24.packet_ref, bf16[2352,128]{1,0:T(8,128)(2,1)S(1)} %collective-permute-done.next_ref, s32[8,128]{1,0:T(8,128)S(1)} %get-tuple-element.27.rank_ref, ...), custom_call_target="tpu_custom_call" | custom-call | flops 251658240 | bytes 1048576 | tf_op jit(solution)/shard_map/pallas_call | solution.py:344
  8.0 2.2 %collective-permute-start.2 = (bf16[2,128,128]{2,1,0:T(8,128)(2,1)S(1)}, bf16[2,128,128]{2,1,0:T(8,128)(2,1)S(1)}, u32[]{:S(2)}, u32[]{:S(2)}) collective-permute-start(bf16[2,128,128]{2,1,0:T(8,128)(2,1)S(1)} %get-tuple-element.29), channel_id=1, source_target_pairs={{0,8},{4,28},{8,0},{12,20},{16,24},{20,12},{24,16},{28,4},{1,9},{5... | collective-permute-start | bytes 196616 | tf_op jit(solution)/shard_map/ppermute | solution.py:279
  10.3 0.2 collective-permute-done.3.refs_0_.refs_6_
  10.4 0.7 %shard_map.98 = (bf16[128,768]{1,0:T(8,128)(2,1)S(1)}, bf16[128,768]{1,0:T(8,128)(2,1)S(1)}, bf16[2,128,128]{2,1,0:T(8,128)(2,1)S(1)}) custom-call(bf16[2352,128]{1,0:T(8,128)(2,1)S(1)} %get-tuple-element.24.packet_ref, bf16[2352,128]{1,0:T(8,128)(2,1)S(1)} %collective-permute-done.next_ref, s32[8,128]{1,0:T(8,128)S(1)} %get-tuple-element.27.rank_ref, ...), custom_call_target="tpu_custom_call" | custom-call | flops 251658240 | bytes 1048576 | tf_op jit(solution)/shard_map/pallas_call | solution.py:344
  11.1 1.9 %collective-permute-start.4 = (bf16[2,128,128]{2,1,0:T(8,128)(2,1)S(1)}, bf16[2,128,128]{2,1,0:T(8,128)(2,1)S(1)}, u32[]{:S(2)}, u32[]{:S(2)}) collective-permute-start(bf16[2,128,128]{2,1,0:T(8,128)(2,1)S(1)} %get-tuple-element.32), channel_id=1, source_target_pairs={{0,24},{4,20},{8,16},{12,28},{16,8},{20,4},{24,0},{28,12},{1,25},{... | collective-permute-start | bytes 196616 | tf_op jit(solution)/shard_map/ppermute | solution.py:279
  13.0 0.0 collective-permute-done.5.refs_0_.refs_7_
  13.0 0.7 %shard_map.99 = (bf16[128,768]{1,0:T(8,128)(2,1)S(1)}, bf16[128,768]{1,0:T(8,128)(2,1)S(1)}, bf16[2,128,128]{2,1,0:T(8,128)(2,1)S(1)}) custom-call(bf16[2352,128]{1,0:T(8,128)(2,1)S(1)} %get-tuple-element.24.packet_ref, bf16[2352,128]{1,0:T(8,128)(2,1)S(1)} %collective-permute-done.next_ref, s32[8,128]{1,0:T(8,128)S(1)} %get-tuple-element.27.rank_ref, ...), custom_call_target="tpu_custom_call" | custom-call | flops 251658240 | bytes 1048576 | tf_op jit(solution)/shard_map/pallas_call | solution.py:344
  13.7 0.8 %collective-permute-start.6 = (bf16[2,128,128]{2,1,0:T(8,128)(2,1)S(1)}, bf16[2,128,128]{2,1,0:T(8,128)(2,1)S(1)}, u32[]{:S(2)}, u32[]{:S(2)}) collective-permute-start(bf16[2,128,128]{2,1,0:T(8,128)(2,1)S(1)} %get-tuple-element.33), channel_id=1, source_target_pairs={{0,16},{4,12},{8,24},{12,4},{16,0},{20,28},{24,8},{28,20},{1,17},{... | collective-permute-start | bytes 196616 | tf_op jit(solution)/shard_map/ppermute | solution.py:279
  14.5 0.4 %shard_map.101.query_ref = f32[768,128]{1,0:T(8,128)S(1)} custom-call(bf16[128,768]{1,0:T(8,128)(2,1)S(1)} %get-tuple-element.34.refs_0_, bf16[128,768]{1,0:T(8,128)(2,1)S(1)} %get-tuple-element.35.refs_1_, bf16[128,768]{1,0:T(8,128)(2,1)S(1)} %get-tuple-element.36.refs_2_, bf16[128,768]{1,0:T(8,128)(2,1)S(1)} %get-tuple-element.37.refs_3_, ...), custom_call_target="tpu_custom_call" | custom-call | tf_op jit(solution)/shard_map/pallas_call | solution.py:380
  14.9 0.0 collective-permute-done.2.refs_1_
  14.9 0.4 %shard_map.102 = bf16[768,128]{1,0:T(8,128)(2,1)S(1)} custom-call(bf16[128,768]{1,0:T(8,128)(2,1)S(1)} %get-tuple-element.38.refs_0_, bf16[128,768]{1,0:T(8,128)(2,1)S(1)} %get-tuple-element.39.refs_1_, bf16[128,768]{1,0:T(8,128)(2,1)S(1)} %get-tuple-element.40.refs_2_, bf16[128,768]{1,0:T(8,128)(2,1)S(1)} %get-tuple-element.41.refs_3_, ...), custom_call_target="tpu_custom_call" | custom-call | tf_op jit(solution)/shard_map/pallas_call | solution.py:370
  15.3 0.1 collective-permute-start.7
  15.4 1.6 %collective-permute-done.4.refs_1_ = bf16[2,128,128]{2,1,0:T(8,128)(2,1)S(1)} collective-permute-done((bf16[2,128,128]{2,1,0:T(8,128)(2,1)S(1)}, bf16[2,128,128]{2,1,0:T(8,128)(2,1)S(1)}, u32[]{:S(2)}, u32[]{:S(2)}) %collective-permute-start.4) | collective-permute-done | bytes 65568 | tf_op jit(solution)/shard_map/ppermute | solution.py:279
  17.0 1.0 %collective-permute-done.6.refs_2_ = bf16[2,128,128]{2,1,0:T(8,128)(2,1)S(1)} collective-permute-done((bf16[2,128,128]{2,1,0:T(8,128)(2,1)S(1)}, bf16[2,128,128]{2,1,0:T(8,128)(2,1)S(1)}, u32[]{:S(2)}, u32[]{:S(2)}) %collective-permute-start.6) | collective-permute-done | bytes 65568 | tf_op jit(solution)/shard_map/ppermute | solution.py:279
  18.0 0.0 collective-permute-done.7.back_ref
  18.0 0.8 %shard_map.103 = (bf16[768,128]{1,0:T(8,128)(2,1)}, bf16[128,128]{1,0:T(8,128)(2,1)}, bf16[128,128]{1,0:T(8,128)(2,1)}) custom-call(bf16[2,128,128]{2,1,0:T(8,128)(2,1)S(1)} %shard_map.100.sum_ref, f32[768,128]{1,0:T(8,128)S(1)} %shard_map.101.query_ref, bf16[768,128]{1,0:T(8,128)(2,1)S(1)} %collective-permute-done.7.back_ref), custom_call_target="tpu_custom_call" | custom-call | tf_op jit(solution)/shard_map/pallas_call | solution.py:398
  (2 shorter events, 0.0 us)
Async XLA Ops:
  1.8 4.6 %collective-permute-start = (bf16[2352,128]{1,0:T(8,128)(2,1)S(1)}, bf16[2352,128]{1,0:T(8,128)(2,1)S(1)}, u32[]{:S(2)}, u32[]{:S(2)}) collective-permute-start(bf16[2352,128]{1,0:T(8,128)(2,1)S(1)} %get-tuple-element.24.packet_ref), channel_id=1, source_target_pairs={{0,4},{4,0},{1,5},{5,1},{2,6},{6,2},{3,7},{7,3},{8,12},{12,8},{9,1... | collective-permute-start | bytes 1806344 | tf_op jit(solution)/shard_map/ppermute | solution.py:271
  2.3 5.0 %collective-permute-start.1 = (bf16[2,128,128]{2,1,0:T(8,128)(2,1)S(1)}, bf16[2,128,128]{2,1,0:T(8,128)(2,1)S(1)}, u32[]{:S(2)}, u32[]{:S(2)}) collective-permute-start(bf16[2,128,128]{2,1,0:T(8,128)(2,1)S(1)} %get-tuple-element.25.pair_ref.refs_4_), channel_id=1, source_target_pairs={{0,8},{4,28},{8,0},{12,20},{16,24},{20,12},{24,16},{28,4},{1,9},{5... | collective-permute-start | bytes 196616 | tf_op jit(solution)/shard_map/ppermute | solution.py:279
  4.9 5.5 %collective-permute-start.3 = (bf16[2,128,128]{2,1,0:T(8,128)(2,1)S(1)}, bf16[2,128,128]{2,1,0:T(8,128)(2,1)S(1)}, u32[]{:S(2)}, u32[]{:S(2)}) collective-permute-start(bf16[2,128,128]{2,1,0:T(8,128)(2,1)S(1)} %get-tuple-element.25.pair_ref.refs_4_), channel_id=1, source_target_pairs={{0,24},{4,20},{8,16},{12,28},{16,8},{20,4},{24,0},{28,12},{1,25},{... | collective-permute-start | bytes 196616 | tf_op jit(solution)/shard_map/ppermute | solution.py:279
  6.4 6.6 %collective-permute-start.5 = (bf16[2,128,128]{2,1,0:T(8,128)(2,1)S(1)}, bf16[2,128,128]{2,1,0:T(8,128)(2,1)S(1)}, u32[]{:S(2)}, u32[]{:S(2)}) collective-permute-start(bf16[2,128,128]{2,1,0:T(8,128)(2,1)S(1)} %get-tuple-element.25.pair_ref.refs_4_), channel_id=1, source_target_pairs={{0,16},{4,12},{8,24},{12,4},{16,0},{20,28},{24,8},{28,20},{1,17},{... | collective-permute-start | bytes 196616 | tf_op jit(solution)/shard_map/ppermute | solution.py:279
  8.0 6.9 %collective-permute-start.2 = (bf16[2,128,128]{2,1,0:T(8,128)(2,1)S(1)}, bf16[2,128,128]{2,1,0:T(8,128)(2,1)S(1)}, u32[]{:S(2)}, u32[]{:S(2)}) collective-permute-start(bf16[2,128,128]{2,1,0:T(8,128)(2,1)S(1)} %get-tuple-element.29), channel_id=1, source_target_pairs={{0,8},{4,28},{8,0},{12,20},{16,24},{20,12},{24,16},{28,4},{1,9},{5... | collective-permute-start | bytes 196616 | tf_op jit(solution)/shard_map/ppermute | solution.py:279
  11.1 5.9 %collective-permute-start.4 = (bf16[2,128,128]{2,1,0:T(8,128)(2,1)S(1)}, bf16[2,128,128]{2,1,0:T(8,128)(2,1)S(1)}, u32[]{:S(2)}, u32[]{:S(2)}) collective-permute-start(bf16[2,128,128]{2,1,0:T(8,128)(2,1)S(1)} %get-tuple-element.32), channel_id=1, source_target_pairs={{0,24},{4,20},{8,16},{12,28},{16,8},{20,4},{24,0},{28,12},{1,25},{... | collective-permute-start | bytes 196616 | tf_op jit(solution)/shard_map/ppermute | solution.py:279
  13.7 4.3 %collective-permute-start.6 = (bf16[2,128,128]{2,1,0:T(8,128)(2,1)S(1)}, bf16[2,128,128]{2,1,0:T(8,128)(2,1)S(1)}, u32[]{:S(2)}, u32[]{:S(2)}) collective-permute-start(bf16[2,128,128]{2,1,0:T(8,128)(2,1)S(1)} %get-tuple-element.33), channel_id=1, source_target_pairs={{0,16},{4,12},{8,24},{12,4},{16,0},{20,28},{24,8},{28,20},{1,17},{... | collective-permute-start | bytes 196616 | tf_op jit(solution)/shard_map/ppermute | solution.py:279
  15.3 2.7 %collective-permute-start.7 = (bf16[768,128]{1,0:T(8,128)(2,1)S(1)}, bf16[768,128]{1,0:T(8,128)(2,1)S(1)}, u32[]{:S(2)}, u32[]{:S(2)}) collective-permute-start(bf16[768,128]{1,0:T(8,128)(2,1)S(1)} %shard_map.102), channel_id=1, source_target_pairs={{0,4},{4,0},{1,5},{5,1},{2,6},{6,2},{3,7},{7,3},{8,12},{12,8},{9,1... | collective-permute-start | bytes 589832 | tf_op jit(solution)/shard_map/ppermute | solution.py:271

commit v13 on v11

--- a/solution.py
+++ b/solution.py
@@ -27,8 +27,8 @@
 def peer_offset(step, outer, inner_count):
     last = inner_count - 1
     if outer % 2 == 1:
-        return {0: 0, 1: last - 1, last: last}.get(step, step - 1)
-    return {0: 0, 1: 1, 2: last}.get(step, step - 1)
+        return {0: 0, 1: last}.get(step, step - 1)
+    return {0: 0, 1: last - 1, 2: last}.get(step, step - 2) if last > 1 else step
 
 
 def load_kernel(

time: 19.9 us -> 18.8 us (0.945)
  waiting for transfers between devices: 4.31 us -> 3.11 us
    ppermute x6, waiting for transfers between devices: 4.3 us -> 3.11 us  [exchange(): return lax.ppermute(block, ('inner', 'outer'), route)]
  transfers between devices with their start and end apart: 8 -> 8, of which waited for: 4 -> 2; matrix products, arithmetic and copies ran while one was open for 0% -> 0% of each run, Pallas kernels for 17% -> 18%
where the time goes in v13:
time: 18.8 us; the launch traced here: 18.7 us
  starting transfers between devices  9.52 us (51%)
  Pallas kernels  5.32 us (28%)
  waiting for transfers between devices  3.11 us (17%)
  between operations  0.72 us (4%)
    ppermute x6, starting transfers between devices, exchange(): return lax.ppermute(block, ('inner', 'outer'), route)  8.93 us
    ppermute x6, waiting for transfers between devices, exchange(): return lax.ppermute(block, ('inner', 'outer'), route)  3.11 us
    pallas_call x2, Pallas kernels, on_device(): pl.pallas_call(functools.partial(far_kernel, sizes, inner_count, outer_co...  1.67 us
    pallas_call x1, Pallas kernels, on_device(): pl.pallas_call(functools.partial(load_kernel, sizes), out_shape=(block_sh...  1.17 us
    pallas_call x1, Pallas kernels, on_device(): pl.pallas_call(functools.partial(near_kernel, sizes, inner_count, outer_c...  0.87 us
    pallas_call x1, Pallas kernels, on_device(): pl.pallas_call(functools.partial(final_kernel, group_size), out_shape=(sh...  0.76 us
    ppermute x2, starting transfers between devices, to_segment(): return lax.ppermute(block, 'outer', route)  0.59 us
    pallas_call x1, Pallas kernels, on_device(): pl.pallas_call(functools.partial(query_kernel, sizes, groups), out_shape=...  0.41 us
  transfers between devices with their start and end apart: 8, of which 2 were waited for; matrix products, arithmetic and copies ran while one was open for 0% of the time, Pallas kernels for 18%

profile of v13, /device:TPU:0, one launch (start us, length us, event | category | flops | bytes accessed | tf_op | source)
XLA Modules:
  0.0 18.7 jit_solution(5081756349367899702)
XLA Ops:
  0.6 1.2 %shard_map.94 = (bf16[2,128,128]{2,1,0:T(8,128)(2,1)S(1)}, bf16[2352,128]{1,0:T(8,128)(2,1)S(1)}) custom-call(bf16[768,128]{1,0:T(8,128)(2,1)} %bitcast.16, bf16[768,128]{1,0:T(8,128)(2,1)} %bitcast.17, bf16[768,128]{1,0:T(8,128)(2,1)} %bitcast.18, f32[6,128]{1,0:T(8,128)} %norm_hbm.1, bf16[128,128]{1,0:T(8,128)(2,1)} %bitcast.19, bf16[128,128]{1,0:T(8,128)(2,1)} %bitcast.20), custom_call_target="tpu_custom_call" | custom-call | bytes 1048576 | tf_op jit(solution)/shard_map/pallas_call | solution.py:296
  1.8 0.5 %collective-permute-start = (bf16[2352,128]{1,0:T(8,128)(2,1)S(1)}, bf16[2352,128]{1,0:T(8,128)(2,1)S(1)}, u32[]{:S(2)}, u32[]{:S(2)}) collective-permute-start(bf16[2352,128]{1,0:T(8,128)(2,1)S(1)} %get-tuple-element.22.packet_ref), channel_id=1, source_target_pairs={{0,4},{4,0},{1,5},{5,1},{2,6},{6,2},{3,7},{7,3},{8,12},{12,8},{9,1... | collective-permute-start | bytes 1806344 | tf_op jit(solution)/shard_map/ppermute | solution.py:271
  2.3 2.6 %collective-permute-start.1 = (bf16[2,128,128]{2,1,0:T(8,128)(2,1)S(1)}, bf16[2,128,128]{2,1,0:T(8,128)(2,1)S(1)}, u32[]{:S(2)}, u32[]{:S(2)}) collective-permute-start(bf16[2,128,128]{2,1,0:T(8,128)(2,1)S(1)} %get-tuple-element.23.pair_ref.refs_3_), channel_id=1, source_target_pairs={{0,16},{4,28},{8,24},{12,20},{16,0},{20,12},{24,8},{28,4},{1,17},{... | collective-permute-start | bytes 196616 | tf_op jit(solution)/shard_map/ppermute | solution.py:279
  4.9 1.4 %collective-permute-start.3 = (bf16[2,128,128]{2,1,0:T(8,128)(2,1)S(1)}, bf16[2,128,128]{2,1,0:T(8,128)(2,1)S(1)}, u32[]{:S(2)}, u32[]{:S(2)}) collective-permute-start(bf16[2,128,128]{2,1,0:T(8,128)(2,1)S(1)} %get-tuple-element.23.pair_ref.refs_3_), channel_id=1, source_target_pairs={{0,24},{4,12},{8,16},{12,4},{16,8},{20,28},{24,0},{28,20},{1,25},{... | collective-permute-start | bytes 196616 | tf_op jit(solution)/shard_map/ppermute | solution.py:279
  6.4 0.1 collective-permute-start.4
  6.5 0.0 collective-permute-done.next_ref
  6.5 0.9 %shard_map.95 = (bf16[128,768]{1,0:T(8,128)(2,1)S(1)}, bf16[128,768]{1,0:T(8,128)(2,1)S(1)}, f32[2,128,128]{2,1,0:T(8,128)S(1)}, f32[2,16,128]{2,1,0:T(8,128)S(1)}, s32[8,128]{1,0:T(8,128)S(1)}) custom-call(bf16[2352,128]{1,0:T(8,128)(2,1)S(1)} %get-tuple-element.22.packet_ref, bf16[2352,128]{1,0:T(8,128)(2,1)S(1)} %collective-permute-done.next_ref, ...), custom_call_target="tpu_custom_call" | custom-call | flops 251658240 | bytes 1048576 | tf_op jit(solution)/shard_map/pallas_call | solution.py:323
  7.3 0.8 %collective-permute-done.1.refs_0_.refs_4_ = bf16[2,128,128]{2,1,0:T(8,128)(2,1)S(1)} collective-permute-done((bf16[2,128,128]{2,1,0:T(8,128)(2,1)S(1)}, bf16[2,128,128]{2,1,0:T(8,128)(2,1)S(1)}, u32[]{:S(2)}, u32[]{:S(2)}) %collective-permute-start.1) | collective-permute-done | bytes 65568 | tf_op jit(solution)/shard_map/ppermute | solution.py:279
  8.2 0.7 %shard_map.96 = (bf16[128,768]{1,0:T(8,128)(2,1)S(1)}, bf16[128,768]{1,0:T(8,128)(2,1)S(1)}, bf16[2,128,128]{2,1,0:T(8,128)(2,1)S(1)}) custom-call(bf16[2352,128]{1,0:T(8,128)(2,1)S(1)} %get-tuple-element.22.packet_ref, bf16[2352,128]{1,0:T(8,128)(2,1)S(1)} %collective-permute-done.next_ref, s32[8,128]{1,0:T(8,128)S(1)} %get-tuple-element.25.rank_ref, ...), custom_call_target="tpu_custom_call" | custom-call | flops 251658240 | bytes 1048576 | tf_op jit(solution)/shard_map/pallas_call | solution.py:344
  8.9 2.8 %collective-permute-start.2 = (bf16[2,128,128]{2,1,0:T(8,128)(2,1)S(1)}, bf16[2,128,128]{2,1,0:T(8,128)(2,1)S(1)}, u32[]{:S(2)}, u32[]{:S(2)}) collective-permute-start(bf16[2,128,128]{2,1,0:T(8,128)(2,1)S(1)} %get-tuple-element.27), channel_id=1, source_target_pairs={{0,16},{4,28},{8,24},{12,20},{16,0},{20,12},{24,8},{28,4},{1,17},{... | collective-permute-start | bytes 196616 | tf_op jit(solution)/shard_map/ppermute | solution.py:279
  11.6 0.0 collective-permute-done.3.refs_0_.refs_5_
  11.6 0.0 collective-permute-done.4.refs_1_.refs_6_
  11.6 1.0 %shard_map.98 = (bf16[256,768]{1,0:T(8,128)(2,1)S(1)}, bf16[256,768]{1,0:T(8,128)(2,1)S(1)}, bf16[2,128,128]{2,1,0:T(8,128)(2,1)S(1)}, bf16[2,128,128]{2,1,0:T(8,128)(2,1)S(1)}) custom-call(bf16[2352,128]{1,0:T(8,128)(2,1)S(1)} %get-tuple-element.22.packet_ref, bf16[2352,128]{1,0:T(8,128)(2,1)S(1)} %collective-permute-done.next_ref, ...), custom_call_target="tpu_custom_call" | custom-call | flops 503316480 | bytes 1048576 | tf_op jit(solution)/shard_map/pallas_call | solution.py:344
  12.6 0.7 %collective-permute-start.5 = (bf16[2,128,128]{2,1,0:T(8,128)(2,1)S(1)}, bf16[2,128,128]{2,1,0:T(8,128)(2,1)S(1)}, u32[]{:S(2)}, u32[]{:S(2)}) collective-permute-start(bf16[2,128,128]{2,1,0:T(8,128)(2,1)S(1)} %get-tuple-element.30), channel_id=1, source_target_pairs={{0,24},{4,12},{8,16},{12,4},{16,8},{20,28},{24,0},{28,20},{1,25},{... | collective-permute-start | bytes 196616 | tf_op jit(solution)/shard_map/ppermute | solution.py:279
  13.4 1.3 %collective-permute-start.6 = (bf16[2,128,128]{2,1,0:T(8,128)(2,1)S(1)}, bf16[2,128,128]{2,1,0:T(8,128)(2,1)S(1)}, u32[]{:S(2)}, u32[]{:S(2)}) collective-permute-start(bf16[2,128,128]{2,1,0:T(8,128)(2,1)S(1)} %get-tuple-element.31), channel_id=1, source_target_pairs={{0,8},{4,20},{8,0},{12,28},{16,24},{20,4},{24,16},{28,12},{1,9},{5... | collective-permute-start | bytes 196616 | tf_op jit(solution)/shard_map/ppermute | solution.py:279
  14.7 0.4 %shard_map.100.query_ref = f32[768,128]{1,0:T(8,128)S(1)} custom-call(bf16[128,768]{1,0:T(8,128)(2,1)S(1)} %get-tuple-element.32.refs_0_, bf16[128,768]{1,0:T(8,128)(2,1)S(1)} %get-tuple-element.33.refs_1_, bf16[256,768]{1,0:T(8,128)(2,1)S(1)} %get-tuple-element.34.refs_2_, bf16[2,128,128]{2,1,0:T(8,128)(2,1)S(1)} %get-tuple-element.23.pair_ref.refs_3_, ...), custom_call_target="tpu_custom_call" | custom-call | tf_op jit(solution)/shard_map/pallas_call | solution.py:380
  15.1 0.0 collective-permute-done.2.refs_1_
  15.1 0.4 %shard_map.101 = bf16[768,128]{1,0:T(8,128)(2,1)S(1)} custom-call(bf16[128,768]{1,0:T(8,128)(2,1)S(1)} %get-tuple-element.35.refs_0_, bf16[128,768]{1,0:T(8,128)(2,1)S(1)} %get-tuple-element.36.refs_1_, bf16[256,768]{1,0:T(8,128)(2,1)S(1)} %get-tuple-element.37.refs_2_, bf16[2,128,128]{2,1,0:T(8,128)(2,1)S(1)} %get-tuple-element.23.pair_ref.refs_3_, ...), custom_call_target="tpu_custom_call" | custom-call | tf_op jit(solution)/shard_map/pallas_call | solution.py:370
  15.5 0.1 collective-permute-start.7
  15.6 2.2 %collective-permute-done.5.refs_1_ = bf16[2,128,128]{2,1,0:T(8,128)(2,1)S(1)} collective-permute-done((bf16[2,128,128]{2,1,0:T(8,128)(2,1)S(1)}, bf16[2,128,128]{2,1,0:T(8,128)(2,1)S(1)}, u32[]{:S(2)}, u32[]{:S(2)}) %collective-permute-start.5) | collective-permute-done | bytes 65568 | tf_op jit(solution)/shard_map/ppermute | solution.py:279
  17.9 0.0 collective-permute-done.6.refs_2_
  17.9 0.0 collective-permute-done.7.back_ref
  17.9 0.8 %shard_map.102 = (bf16[768,128]{1,0:T(8,128)(2,1)}, bf16[128,128]{1,0:T(8,128)(2,1)}, bf16[128,128]{1,0:T(8,128)(2,1)}) custom-call(bf16[2,128,128]{2,1,0:T(8,128)(2,1)S(1)} %shard_map.99.sum_ref, f32[768,128]{1,0:T(8,128)S(1)} %shard_map.100.query_ref, bf16[768,128]{1,0:T(8,128)(2,1)S(1)} %collective-permute-done.7.back_ref), custom_call_target="tpu_custom_call" | custom-call | tf_op jit(solution)/shard_map/pallas_call | solution.py:398
  (2 shorter events, 0.0 us)
Async XLA Ops:
  1.8 4.7 %collective-permute-start = (bf16[2352,128]{1,0:T(8,128)(2,1)S(1)}, bf16[2352,128]{1,0:T(8,128)(2,1)S(1)}, u32[]{:S(2)}, u32[]{:S(2)}) collective-permute-start(bf16[2352,128]{1,0:T(8,128)(2,1)S(1)} %get-tuple-element.22.packet_ref), channel_id=1, source_target_pairs={{0,4},{4,0},{1,5},{5,1},{2,6},{6,2},{3,7},{7,3},{8,12},{12,8},{9,1... | collective-permute-start | bytes 1806344 | tf_op jit(solution)/shard_map/ppermute | solution.py:271
  2.3 5.9 %collective-permute-start.1 = (bf16[2,128,128]{2,1,0:T(8,128)(2,1)S(1)}, bf16[2,128,128]{2,1,0:T(8,128)(2,1)S(1)}, u32[]{:S(2)}, u32[]{:S(2)}) collective-permute-start(bf16[2,128,128]{2,1,0:T(8,128)(2,1)S(1)} %get-tuple-element.23.pair_ref.refs_3_), channel_id=1, source_target_pairs={{0,16},{4,28},{8,24},{12,20},{16,0},{20,12},{24,8},{28,4},{1,17},{... | collective-permute-start | bytes 196616 | tf_op jit(solution)/shard_map/ppermute | solution.py:279
  4.9 6.7 %collective-permute-start.3 = (bf16[2,128,128]{2,1,0:T(8,128)(2,1)S(1)}, bf16[2,128,128]{2,1,0:T(8,128)(2,1)S(1)}, u32[]{:S(2)}, u32[]{:S(2)}) collective-permute-start(bf16[2,128,128]{2,1,0:T(8,128)(2,1)S(1)} %get-tuple-element.23.pair_ref.refs_3_), channel_id=1, source_target_pairs={{0,24},{4,12},{8,16},{12,4},{16,8},{20,28},{24,0},{28,20},{1,25},{... | collective-permute-start | bytes 196616 | tf_op jit(solution)/shard_map/ppermute | solution.py:279
  6.4 5.3 %collective-permute-start.4 = (bf16[2,128,128]{2,1,0:T(8,128)(2,1)S(1)}, bf16[2,128,128]{2,1,0:T(8,128)(2,1)S(1)}, u32[]{:S(2)}, u32[]{:S(2)}) collective-permute-start(bf16[2,128,128]{2,1,0:T(8,128)(2,1)S(1)} %get-tuple-element.23.pair_ref.refs_3_), channel_id=1, source_target_pairs={{0,8},{4,20},{8,0},{12,28},{16,24},{20,4},{24,16},{28,12},{1,9},{5... | collective-permute-start | bytes 196616 | tf_op jit(solution)/shard_map/ppermute | solution.py:279
  8.9 6.2 %collective-permute-start.2 = (bf16[2,128,128]{2,1,0:T(8,128)(2,1)S(1)}, bf16[2,128,128]{2,1,0:T(8,128)(2,1)S(1)}, u32[]{:S(2)}, u32[]{:S(2)}) collective-permute-start(bf16[2,128,128]{2,1,0:T(8,128)(2,1)S(1)} %get-tuple-element.27), channel_id=1, source_target_pairs={{0,16},{4,28},{8,24},{12,20},{16,0},{20,12},{24,8},{28,4},{1,17},{... | collective-permute-start | bytes 196616 | tf_op jit(solution)/shard_map/ppermute | solution.py:279
  12.6 5.2 %collective-permute-start.5 = (bf16[2,128,128]{2,1,0:T(8,128)(2,1)S(1)}, bf16[2,128,128]{2,1,0:T(8,128)(2,1)S(1)}, u32[]{:S(2)}, u32[]{:S(2)}) collective-permute-start(bf16[2,128,128]{2,1,0:T(8,128)(2,1)S(1)} %get-tuple-element.30), channel_id=1, source_target_pairs={{0,24},{4,12},{8,16},{12,4},{16,8},{20,28},{24,0},{28,20},{1,25},{... | collective-permute-start | bytes 196616 | tf_op jit(solution)/shard_map/ppermute | solution.py:279
  13.4 4.5 %collective-permute-start.6 = (bf16[2,128,128]{2,1,0:T(8,128)(2,1)S(1)}, bf16[2,128,128]{2,1,0:T(8,128)(2,1)S(1)}, u32[]{:S(2)}, u32[]{:S(2)}) collective-permute-start(bf16[2,128,128]{2,1,0:T(8,128)(2,1)S(1)} %get-tuple-element.31), channel_id=1, source_target_pairs={{0,8},{4,20},{8,0},{12,28},{16,24},{20,4},{24,16},{28,12},{1,9},{5... | collective-permute-start | bytes 196616 | tf_op jit(solution)/shard_map/ppermute | solution.py:279
  15.5 2.4 %collective-permute-start.7 = (bf16[768,128]{1,0:T(8,128)(2,1)S(1)}, bf16[768,128]{1,0:T(8,128)(2,1)S(1)}, u32[]{:S(2)}, u32[]{:S(2)}) collective-permute-start(bf16[768,128]{1,0:T(8,128)(2,1)S(1)} %shard_map.101), channel_id=1, source_target_pairs={{0,4},{4,0},{1,5},{5,1},{2,6},{6,2},{3,7},{7,3},{8,12},{12,8},{9,1... | collective-permute-start | bytes 589832 | tf_op jit(solution)/shard_map/ppermute | solution.py:271
